TPU v7x, 32 devices: a whole 2x2x4 slice. The times are simulated.
32 devices in a mesh: train: 8 (over z, y), test: 4 (over x, core).
Axes of the slice: x: 2, y: 2, z: 4, core: 2. Of those that a mesh axis runs over, the one named last changes fastest.
Arguments:
- query_out: bfloat16 [2048, 3584], P('train', 'test'), may hold values from -16 to 16, as said below
- query_in: bfloat16 [2048, 3584], P('train', 'test'), may hold values from -6 to 6
- passage_out: bfloat16 [2048, 3584], P('train', 'test'), may hold values from -16 to 16, as said below
- passage_in_sum: bfloat16 [2048, 3584], P('train', 'test'), may hold values from -192 to 192
- passage_len: int32 [2048], P('train'), may hold values from 16 to 512
- positive: int32 [2048], P('train'), may hold values from 0 to 2047
- proj_in: bfloat16 [3584, 64], P('test'), may hold values from -0.09375 to 0.09375
- proj_out: bfloat16 [3584, 64], P('test'), may hold values from -0.09375 to 0.09375
- test_grads: bfloat16 [2048, 4096], P(('test', 'train')), may hold values from -6 to 6
Outputs:
- scores: float32 [2048, 2048], P('train', 'test')
Inputs may be any that keep to these rules, and one draw needn't show every extreme that they name: `query_out`: entries stay within the range. `passage_out`: entries stay within the range.
All inputs are finite; a program needn't handle non-finite values.
Results may differ from a plain program's by a relative error of at most 0.0034.
Values may be sent and summed in bfloat16 or wider, within the bound.
No kernel may reach another device: no remote copies, remote signals or barrier semaphores. Data moves between devices by JAX's collectives and lax.ppermute only.
A program may use at most 64 MiB of HBM per device.

v0:
```python
import math

import jax
import jax.numpy as jnp
from jax import lax
from jax.sharding import PartitionSpec as P

D = 3584


def local(
    query_out,
    query_in,
    passage_out,
    passage_in_sum,
    passage_len,
    positive,
    proj_in,
    proj_out,
    test_grads,
):
    rank_size = proj_in.shape[1]
    logit_scale = 1.0 / math.sqrt(D)
    whole_pass = lax.all_gather(passage_out, "train", axis=0, tiled=True)
    pass_block = lax.all_to_all(whole_pass, "test", split_axis=0, concat_axis=1, tiled=True)
    query_full = lax.all_gather(query_out, "test", axis=1, tiled=True)
    proj_full = lax.all_gather(proj_out, "test", axis=0, tiled=True).astype(jnp.float32)
    block_logits = (
        lax.dot_general(
            query_full, pass_block, (((1,), (1,)), ((), ())), preferred_element_type=jnp.float32
        )
        * logit_scale
    )
    block_cols = block_logits.shape[1]
    block_top = lax.pmax(jnp.max(block_logits, axis=1), "test")
    block_exp = jnp.exp(block_logits - block_top[:, None])
    block_sum = lax.psum(jnp.sum(block_exp, axis=1), "test")
    first_col = lax.axis_index("test") * block_cols
    col_index = lax.broadcasted_iota(jnp.int32, block_logits.shape, 1) + first_col
    block_hit = (col_index == positive[:, None]).astype(jnp.float32)
    block_grad = (block_exp / block_sum[:, None] - block_hit).astype(jnp.bfloat16)
    query_partial = (
        jnp.dot(block_grad, pass_block, preferred_element_type=jnp.float32) * logit_scale
    )
    out_query = jnp.dot(query_partial, proj_full, precision=lax.Precision.HIGHEST)
    pass_partial = (
        lax.dot_general(
            block_grad, query_full, (((0,), (0,)), ((), ())), preferred_element_type=jnp.float32
        )
        * logit_scale
    )
    pass_small = jnp.dot(pass_partial, proj_full, precision=lax.Precision.HIGHEST)
    padded = jnp.zeros((whole_pass.shape[0], rank_size), jnp.float32)
    padded = lax.dynamic_update_slice_in_dim(padded, pass_small, first_col, 0)
    out_pass = lax.psum_scatter(padded, "train", scatter_dimension=0, tiled=True)
    act_query = jnp.dot(query_in, proj_in, preferred_element_type=jnp.float32)
    act_pass = jnp.dot(passage_in_sum, proj_in, preferred_element_type=jnp.float32)
    act_query, act_pass, out_query, out_pass = lax.psum(
        (act_query, act_pass, out_query, out_pass), "test"
    )
    act_pass = act_pass / passage_len[:, None].astype(jnp.float32)
    stacked = jnp.stack((act_query, act_pass, out_query, out_pass), axis=1)
    row_count = stacked.shape[0]
    outer = (
        stacked[:, 0, :, None] * stacked[:, 2, None, :]
        + stacked[:, 1, :, None] * stacked[:, 3, None, :]
    )
    train_grads = outer.reshape(row_count, rank_size * rank_size).astype(jnp.bfloat16)
    return lax.dot_general(
        train_grads,
        lax.all_gather(test_grads, "train", axis=0, tiled=True),
        (((1,), (1,)), ((), ())),
        preferred_element_type=jnp.float32,
    )


def solution(mesh):
    return jax.shard_map(
        local,
        mesh=mesh,
        in_specs=(
            P("train", "test"),
            P("train", "test"),
            P("train", "test"),
            P("train", "test"),
            P("train"),
            P("train"),
            P("test", None),
            P("test", None),
            P(("test", "train"), None),
        ),
        out_specs=P("train", "test"),
        check_vma=False,
    )
```

profile of v0, /device:TPU:0, one launch (start us, length us, event | category | flops | bytes accessed | tf_op | source)
XLA Modules:
  0.0 316.1 jit_solution(14895259904726077220)
XLA Ops:
  7.4 0.0 copy-start
  7.4 0.0 all-gather.6.cloned.1.call-start
  7.4 0.7 all-gather.6.cloned.1.call-update
  8.1 71.8 %all-gather.6.cloned.1.call-done = bf16[2048,896]{1,0:T(8,128)(2,1)} async-done(((bf16[256,896]{1,0:T(8,128)(2,1)}), bf16[2048,896]{1,0:T(8,128)(2,1)}) %all-gather.6.cloned.1.call-update) | async-done | bytes 3670032 | tf_op jit(solution)/shard_map/all_gather | solution.py:24
  79.9 0.0 copy-start.5
  79.9 4.9 %all-to-all-start = ((bf16[4,512,896]{2,1,0:T(8,128)(2,1)}), bf16[4,512,896]{2,1,0:T(8,128)(2,1)}, u32[]{:S(2)}, u32[]{:S(2)}) async-start(bf16[4,512,896]{2,1,0:T(8,128)(2,1)} %bitcast.19), calls=%async_computation | async-start | bytes 7340032 | tf_op jit(solution)/shard_map/all_to_all | solution.py:25
  84.8 0.0 all-gather.4.cloned.1.call-start
  84.9 0.5 all-gather.4.cloned.1.call-update
  85.4 0.0 reduce-scatter.2.cloned.1.call-start
  85.5 0.0 copy-done.5
  85.5 55.0 %all_gather.14 = bf16[3584,64]{0,1:T(8,128)(2,1)S(1)} all-gather(bf16[896,64]{0,1:T(8,128)(2,1)S(1)} %copy-done.5), channel_id=1, replica_groups=mesh['train'=8,'test'=4] {'test'}, dimensions={0}, use_global_device_ids=true | all-gather | bytes 573440 | tf_op jit(solution)/shard_map/all_gather | solution.py:27
  140.5 0.0 all-to-all-done
  140.5 6.0 %copy.14 = bf16[512,4,896]{0,2,1:T(8,128)(2,1)} copy(bf16[512,4,896]{2,0,1:T(8,128)(2,1)} %bitcast.1) | data formatting | bytes 7340032 | tf_op jit(solution)/shard_map/all_to_all | solution.py:25
  146.4 0.0 copy-start.6
  146.4 0.0 all-gather.4.cloned.1.call-done
  146.4 0.0 copy-start.2
  146.4 3.9 %fusion.9 = (f32[256]{0:T(256)S(1)}, f32[256,512]{1,0:T(8,128)S(1)}) fusion(bf16[256,3584]{1,0:T(8,128)(2,1)} %all-gather.4.cloned.1.call-done, bf16[512,3584]{0,1:T(8,128)(2,1)} %bitcast.17), kind=kOutput, calls=%fused_computation.14 | convolution fusion | flops 939785984 | bytes 6030336 | tf_op jit(solution)/shard_map/dot_general | solution.py:29
  150.4 6.0 %pmax.7 = f32[256]{0:T(256)S(1)} all-reduce(f32[256]{0:T(256)S(1)} %get-tuple-element.9), channel_id=1, replica_groups=mesh['train'=8,'test'=4] {'test'}, use_global_device_ids=true, to_apply=%region_2.0 | all-reduce | flops 256 | bytes 2048 | tf_op jit(solution)/shard_map/pmax | solution.py:35
  156.4 0.2 fusion.6
  156.6 5.7 %psum.36 = f32[256]{0:T(256)S(1)} all-reduce(f32[256]{0:T(256)S(1)} %fusion.6), channel_id=1, replica_groups=mesh['train'=8,'test'=4] {'test'}, use_global_device_ids=true, to_apply=%region_4.0 | all-reduce | flops 256 | bytes 2048 | tf_op jit(solution)/shard_map/psum | solution.py:37
  162.3 0.0 copy-done.6
  162.3 0.0 copy-done.2
  162.3 1.3 fusion.8
  163.6 0.0 copy-start.3
  163.6 0.0 copy-start.4
  163.6 4.0 %fusion.3 = f32[2048,64]{0,1:T(8,128)S(1)} fusion(f32[2048,64]{0,1:T(8,128)S(1)} %broadcast_in_dim.2, s32[]{:T(128)S(6)} %select_n.3, bf16[3584,64]{0,1:T(8,128)(2,1)S(1)} %all_gather.14, f32[512,3584]{1,0:T(8,128)S(1)} %fusion.8), kind=kOutput, calls=%fused_computation.6 | convolution fusion | flops 1411121152 | bytes 7929860 | tf_op jit(solution)/shard_map/dot_general | solution.py:52
  167.6 0.0 copy-start.1
  167.7 0.8 copy-done.1
  168.4 0.0 reduce-scatter.2.cloned.1.call-update
  168.5 0.0 all-reduce.3.cloned.1.call-start
  168.5 0.0 copy-done
  168.5 0.0 copy-done.3
  168.5 0.9 fusion.10
  169.4 0.0 copy-done.4
  169.5 0.9 fusion.12
  170.4 3.2 %convolution_multiply_fusion = f32[256,3584]{1,0:T(8,128)S(1)} fusion(bf16[512,3584]{0,1:T(8,128)(2,1)} %bitcast.18, f32[256,512]{1,0:T(8,128)S(1)} %get-tuple-element.10, s32[512]{0:T(512)S(1)} %iota_add_fusion, f32[256]{0:T(256)S(1)} %psum.36, f32[256]{0:T(256)S(1)} %pmax.7, s32[256]{0:T(256)S(1)} %copy-done.6), kind=kOutput, calls=%fused_computation.2 | convolution fusion | flops 941228032 | bytes 7869440 | tf_op jit(solution)/shard_map/dot_general | solution.py:43
  173.6 0.0 copy-start.7
  173.6 2.6 fusion.11
  176.2 52.9 %reduce-scatter.2.cloned.1.call-done = f32[256,64]{0,1:T(8,128)} async-done(((f32[2048,64]{0,1:T(8,128)}), f32[256,64]{0,1:T(8,128)}) %reduce-scatter.2.cloned.1.call-update) | async-done | bytes 65552 | tf_op jit(solution)/shard_map/reduce_scatter | solution.py:55
  229.2 0.0 all-reduce.3.cloned.1.call-update
  229.2 0.0 all-gather.8.cloned.1.call-start
  229.2 0.7 all-gather.8.cloned.1.call-update
  229.9 0.0 copy-done.7
  229.9 30.6 %all-reduce.3.cloned.1.call-done = (f32[256,64]{0,1:T(8,128)}, f32[256,64]{0,1:T(8,128)}, f32[256,64]{0,1:T(8,128)}, f32[256,64]{0,1:T(8,128)}) async-done(((f32[256,64]{0,1:T(8,128)}, f32[256,64]{0,1:T(8,128)}, f32[256,64]{0,1:T(8,128)}, f32[256,64]{0,1:T(8,128)}), (f32[256,64]{0,1:T(8,128)}, f32[256,64]{0,1:T(8,128)}, f32[256,64]{0,1:T(8,128)}, f32[256,64]{0,1:T(8,128)})) %all-reduce.3.cloned.1.call-update) | async-done | bytes 262160 | tf_op jit(solution)/shard_map/psum | solution.py:58
  260.6 0.8 broadcast_divide_fusion
  261.4 1.6 add_convert_fusion
  263.0 41.6 %all-gather.8.cloned.1.call-done = bf16[512,4096]{1,0:T(8,128)(2,1)} async-done(((bf16[64,4096]{1,0:T(8,128)(2,1)}), bf16[512,4096]{1,0:T(8,128)(2,1)}) %all-gather.8.cloned.1.call-update) | async-done | bytes 4194320 | tf_op jit(solution)/shard_map/all_gather | solution.py:71
  304.7 4.3 %fusion.13 = f32[256,512]{1,0:T(8,128)} fusion(bf16[256,4096]{0,1:T(8,128)(2,1)S(1)} %bitcast.20, bf16[512,4096]{1,0:T(8,128)(2,1)} %all-gather.8.cloned.1.call-done), kind=kOutput, calls=%fused_computation.18 | convolution fusion | flops 1073741824 | bytes 6815744 | tf_op jit(solution)/shard_map/dot_general | solution.py:69
  (3 shorter events, 0.0 us)
Async XLA Ops:
  7.4 161.1 %copy-start = (bf16[256,896]{1,0:T(8,128)(2,1)S(1)}, bf16[256,896]{1,0:T(8,128)(2,1)}, u32[]{:S(2)}) copy-start(bf16[256,896]{1,0:T(8,128)(2,1)} %param.10) | copy-start | bytes 1376260
  7.4 72.6 %all-gather.6.cloned.1.call-start = ((), (), s32[]{:S(2)}) async-start(), calls=%async_computation.3 | async-start | bytes 4128768 | tf_op jit(solution)/shard_map/all_gather | solution.py:24
  79.9 5.5 %copy-start.5 = (bf16[896,64]{0,1:T(8,128)(2,1)S(1)}, bf16[896,64]{0,1:T(8,128)(2,1)}, u32[]{:S(2)}) copy-start(bf16[896,64]{0,1:T(8,128)(2,1)} %param.16) | copy-start | bytes 344068
  79.9 60.6 %all-to-all-start = ((bf16[4,512,896]{2,1,0:T(8,128)(2,1)}), bf16[4,512,896]{2,1,0:T(8,128)(2,1)}, u32[]{:S(2)}, u32[]{:S(2)}) async-start(bf16[4,512,896]{2,1,0:T(8,128)(2,1)} %bitcast.19), calls=%async_computation | async-start | bytes 7340032 | tf_op jit(solution)/shard_map/all_to_all | solution.py:25
  84.8 61.6 %all-gather.4.cloned.1.call-start = ((), (), s32[]{:S(2)}) async-start(), calls=%async_computation.2 | async-start | bytes 2293760 | tf_op jit(solution)/shard_map/all_gather | solution.py:26
  85.4 143.8 %reduce-scatter.2.cloned.1.call-start = ((), (), s32[]{:S(2)}) async-start(), calls=%async_computation.4 | async-start | bytes 589824 | tf_op jit(solution)/shard_map/reduce_scatter | solution.py:55
  146.4 15.8 %copy-start.6 = (s32[256]{0:T(256)S(1)}, s32[256]{0:T(256)}, u32[]{:S(2)}) copy-start(s32[256]{0:T(256)} %param.14) | copy-start | bytes 3076
  146.4 15.8 %copy-start.2 = (bf16[256,3584]{1,0:T(8,128)(2,1)S(1)}, bf16[256,3584]{1,0:T(8,128)(2,1)}, u32[]{:S(2)}) copy-start(bf16[256,3584]{1,0:T(8,128)(2,1)} %all-gather.4.cloned.1.call-done) | copy-start | bytes 5505028
  163.6 4.9 %copy-start.3 = (bf16[896,64]{0,1:T(8,128)(2,1)S(1)}, bf16[896,64]{0,1:T(8,128)(2,1)}, u32[]{:S(2)}) copy-start(bf16[896,64]{0,1:T(8,128)(2,1)} %param.15) | copy-start | bytes 344068
  163.6 5.8 %copy-start.4 = (bf16[256,896]{1,0:T(8,128)(2,1)S(1)}, bf16[256,896]{1,0:T(8,128)(2,1)}, u32[]{:S(2)}) copy-start(bf16[256,896]{1,0:T(8,128)(2,1)} %param.12) | copy-start | bytes 1376260
  167.6 0.8 copy-start.1
  168.5 92.1 %all-reduce.3.cloned.1.call-start = ((), (), s32[]{:S(2)}) async-start(), calls=%async_computation.6 | async-start | bytes 524288 | tf_op jit(solution)/shard_map/psum | solution.py:58
  173.6 56.3 %copy-start.7 = (s32[256]{0:T(256)S(1)}, s32[256]{0:T(256)}, u32[]{:S(2)}) copy-start(s32[256]{0:T(256)} %param.13) | copy-start | bytes 3076
  229.2 75.5 %all-gather.8.cloned.1.call-start = ((), (), s32[]{:S(2)}) async-start(), calls=%async_computation.5 | async-start | bytes 4718592 | tf_op jit(solution)/shard_map/all_gather | solution.py:71
Sparse Core Ops, SparseCore 0:
  10.4 69.5 all-gather.5
  168.6 60.5 reduce-scatter.1
  232.1 72.4 all-gather.7
Sparse Core Ops, SparseCore 1:
  86.9 29.8 all-gather.3
  229.3 31.2 all-reduce.2
where the time goes:
time: 317 us; the launch traced here: 316 us
  waiting for transfers between devices  199 us (63%)
  blocking collectives  66.7 us (21%)
  matrix products  21.2 us (7%)
  between operations  14.7 us (5%)
  local copies, waits for them, and re-layouts  6.82 us (2%)
  starting transfers between devices  5.06 us (2%)
    all_gather x1, waiting for transfers between devices, local(): whole_pass = lax.all_gather(passage_out, 'train', axis=0, tiled=True)  71.8 us
    all_gather x1, blocking collectives, local(): lax.all_gather(proj_out, 'test', axis=0, tiled=True).astype(jnp.float32)  55 us
    reduce_scatter x1, waiting for transfers between devices, local(): lax.psum_scatter(padded, 'train', scatter_dimension=0, tiled=True)  52.9 us
    all_gather x1, waiting for transfers between devices, local(): lax.all_gather(test_grads, 'train', axis=0, tiled=True)  41.6 us
    psum x1, waiting for transfers between devices, local(): lax.psum((act_query, act_pass, out_query, out_pass), 'test')  30.6 us
  transfers between devices with their start and end apart: 6, of which 4 were waited for; matrix products, arithmetic and copies ran while one was open for 5% of the time, Pallas kernels for 0%

commit v1 on v0

v1 whole, which is shorter than its diff:
```python
import math

import jax
import jax.numpy as jnp
from jax import lax
from jax.sharding import PartitionSpec as P

D = 3584
F32 = jnp.float32
BF16 = jnp.bfloat16


def dot(a, b, ca, cb):
    return lax.dot_general(a, b, (((ca,), (cb,)), ((), ())), preferred_element_type=F32)


def split_two(a):
    high = a.astype(BF16)
    rest = (a - high.astype(F32)).astype(BF16)
    return jnp.concatenate((high, rest), axis=0)


def local(
    n_train,
    n_test,
    query_out,
    query_in,
    passage_out,
    passage_in_sum,
    passage_len,
    positive,
    proj_in,
    proj_out,
    test_grads,
):
    rank = proj_in.shape[1]
    rows = query_out.shape[0]
    tests = test_grads.shape[0]
    scale = 1.0 / math.sqrt(D)
    me_train = lax.axis_index("train")
    me_test = lax.axis_index("test")
    core = lax.rem(me_test, 2)
    seg_at = lax.div(me_test, 2)
    segs = n_test // 2
    seg = rows // segs
    half = rows // 2
    near = 2
    far = [1 << i for i in range(n_train.bit_length() - 1) if (1 << i) != near]

    def over_train(a, bit):
        return lax.ppermute(a, "train", [(i, i ^ bit) for i in range(n_train)])

    def over_test(a, bit):
        return lax.ppermute(a, "test", [(i, i ^ bit) for i in range(n_test)])

    def gather_far(own):
        held = {0: own}
        for bit in reversed(far):
            held.update({mask | bit: over_train(a, bit) for mask, a in list(held.items())})
        return held

    masks = [0]
    for bit in far:
        masks = masks + [mask | bit for mask in masks]
    n_far = len(masks)

    passages = gather_far(passage_out)
    query_near = over_train(query_out, near)

    factors = jnp.concatenate(
        (
            dot(proj_in, query_in, 0, 1),
            dot(proj_in, passage_in_sum, 0, 1),
            dot(proj_out, query_out, 0, 1),
            dot(proj_out, passage_out, 0, 1),
        ),
        axis=0,
    )
    bit = 1
    while bit < n_test:
        factors = factors + over_test(factors, bit)
        bit *= 2

    queries = jnp.stack((query_out, query_near)).reshape(2, segs, seg, -1)
    queries = queries.transpose(1, 0, 2, 3).reshape(2 * rows, -1)

    def summed_logits(blocks):
        mine = jnp.concatenate(
            [lax.dynamic_slice_in_dim(b, core * half, half, 0) for b in blocks], axis=0
        )
        theirs = jnp.concatenate(
            [lax.dynamic_slice_in_dim(b, (1 - core) * half, half, 0) for b in blocks], axis=0
        )
        sent = over_test(dot(theirs, queries, 1, 1), 1)
        total = dot(mine, queries, 1, 1) + sent
        width = 2 * rows
        bit = n_test // 2
        while bit > 1:
            width //= 2
            upper = lax.rem(lax.div(me_test, bit), 2)
            keep = lax.dynamic_slice_in_dim(total, upper * width, width, 1)
            give = lax.dynamic_slice_in_dim(total, (1 - upper) * width, width, 1)
            total = keep + over_test(give, bit)
            bit //= 2
        return total

    logits = (
        jnp.concatenate(
            [
                summed_logits([passages[m] for m in masks[: n_far // 2]]),
                summed_logits([passages[m] for m in masks[n_far // 2 :]]),
            ],
            axis=0,
        )
        * scale
    )

    def swap(a):
        return jnp.concatenate((a[:, seg:], a[:, :seg]), axis=1)

    top = jnp.max(logits, axis=0, keepdims=True)
    total = jnp.sum(jnp.exp(logits - top), axis=0, keepdims=True)

    def merge(top, total, other):
        new_top = jnp.maximum(top, other[:1])
        return new_top, total * jnp.exp(top - new_top) + other[1:] * jnp.exp(other[:1] - new_top)

    top, total = merge(top, total, over_test(jnp.concatenate((top, total), axis=0), 1))
    top, total = merge(
        top, total, over_train(swap(jnp.concatenate((top, total), axis=0)), near)
    )
    positive_own = positive[None, :]
    positive_near = over_train(positive_own, near)
    wanted = jnp.concatenate(
        [lax.dynamic_slice_in_dim(a, seg_at * seg, seg, 1) for a in (positive_own, positive_near)],
        axis=1,
    )
    columns = jnp.concatenate(
        [
            lax.broadcasted_iota(jnp.int32, (half, 1), 0)
            + ((me_train ^ mask) * rows + core * half)
            for mask in masks
        ],
        axis=0,
    )
    prob = jnp.exp(logits - top) / total
    dlogit = (prob - (columns == wanted).astype(F32)).astype(BF16)

    pass_small = gather_far(
        lax.dynamic_slice_in_dim(factors[3 * rank :], core * half, half, 1)
    )
    pass_small = jnp.concatenate([pass_small[m] for m in masks], axis=1)
    factors_near = over_train(factors[: 3 * rank], near)
    query_small = jnp.concatenate(
        [
            lax.dynamic_slice_in_dim(a[2 * rank : 3 * rank], seg_at * seg, seg, 1)
            for a in (factors, factors_near)
        ],
        axis=1,
    )

    out_query = dot(split_two(pass_small), dlogit, 1, 0)
    out_query = (out_query[:rank] + out_query[rank:]) * scale
    out_pass = dot(split_two(query_small), dlogit, 1, 1)
    out_pass = (out_pass[:rank] + out_pass[rank:]) * scale

    for bit in reversed(far):
        width = out_pass.shape[1] // 2
        out_pass = out_pass[:, :width] + over_train(out_pass[:, width:], bit)
    bit = 2
    while bit < n_test:
        out_pass = out_pass + over_test(out_pass, bit)
        bit *= 2
    out_pass = jnp.concatenate((out_pass, over_train(out_pass, near)), axis=0)
    out_pass_other = over_test(out_pass, 1)
    out_pass = jnp.where(
        core == 0,
        jnp.concatenate((out_pass, out_pass_other), axis=1),
        jnp.concatenate((out_pass_other, out_pass), axis=1),
    )

    out_query = out_query + over_test(out_query, 1)
    out_query = out_query + over_train(swap(out_query), near)
    out_query = jnp.concatenate((out_query[:, :seg], out_query[:, seg:]), axis=0)
    bit = 2
    while bit < n_test:
        other = over_test(out_query, bit)
        out_query = jnp.where(
            lax.rem(lax.div(me_test, bit), 2) == 0,
            jnp.concatenate((out_query, other), axis=1),
            jnp.concatenate((other, out_query), axis=1),
        )
        bit *= 2

    held = gather_far(test_grads)
    test_block = jnp.zeros((n_far * tests, test_grads.shape[1]), BF16)
    for mask in masks:
        owner = me_train ^ mask
        at = lax.div(owner, 2 * near) * near + lax.rem(owner, near)
        test_block = lax.dynamic_update_slice_in_dim(test_block, held[mask], at * tests, 0)

    lens = passage_len[None, :].astype(F32)
    act_query = (factors[:rank], factors_near[:rank])
    act_pass = (
        factors[rank : 2 * rank] / lens,
        factors_near[rank : 2 * rank] / over_train(passage_len[None, :], near).astype(F32),
    )

    def scores_of(which):
        oq = out_query[which * rank : (which + 1) * rank]
        op = out_pass[which * rank : (which + 1) * rank]
        outer = (
            act_query[which][:, None, :] * oq[None, :, :]
            + act_pass[which][:, None, :] * op[None, :, :]
        )
        grads = outer.reshape(rank * rank, rows).astype(BF16)
        return dot(grads, test_block, 0, 1)

    given = over_train(scores_of(1), near)
    mine = scores_of(0)
    unit = near * tests
    mine = [mine[:, i : i + unit] for i in range(0, mine.shape[1], unit)]
    given = [given[:, i : i + unit] for i in range(0, given.shape[1], unit)]
    upper = lax.rem(lax.div(me_train, near), 2) == 1
    pieces = []
    for a, b in zip(mine, given):
        pieces += [jnp.where(upper, b, a), jnp.where(upper, a, b)]
    return jnp.concatenate(pieces, axis=1)


def solution(mesh):
    def body(*args):
        return local(mesh.shape["train"], mesh.shape["test"], *args)

    return jax.shard_map(
        body,
        mesh=mesh,
        in_specs=(
            P("train", "test"),
            P("train", "test"),
            P("train", "test"),
            P("train", "test"),
            P("train"),
            P("train"),
            P("test", None),
            P("test", None),
            P(("test", "train"), None),
        ),
        out_specs=P("train", "test"),
        check_vma=False,
    )
```

time: 317 us -> 121 us (0.38)
  waiting for transfers between devices: 199 us -> 70.3 us
  blocking collectives: 66.7 us -> 0 us
  starting transfers between devices: 5.06 us -> 27.8 us
  between operations: 14.7 us -> 0.59 us
  matrix products: 21.2 us -> 9.2 us
  other arithmetic: 2.71 us -> 7.92 us
    all_gather x3 -> x0, waiting for transfers between devices: 113 us -> none  [the longest x1 71.8 us: local(): whole_pass = lax.all_gather(passage_out, 'train', axis=0, tiled=True)]
    ppermute x0 -> x30, waiting for transfers between devices: none -> 70.3 us  [the longest x19 55.1 us: over_train(): return lax.ppermute(a, 'train', [(i, i ^ bit) for i in range(n_train)])]
    all_gather x1 -> x0, blocking collectives: 55 us -> none  [local(): lax.all_gather(proj_out, 'test', axis=0, tiled=True).astype(jnp.float32)]
    reduce_scatter x1 -> x0, waiting for transfers between devices: 52.9 us -> none  [local(): lax.psum_scatter(padded, 'train', scatter_dimension=0, tiled=True)]
    psum x1 -> x0, waiting for transfers between devices: 30.6 us -> none  [local(): lax.psum((act_query, act_pass, out_query, out_pass), 'test')]
    ppermute x0 -> x30, starting transfers between devices: none -> 27.8 us  [the longest x19 20.8 us: over_train(): return lax.ppermute(a, 'train', [(i, i ^ bit) for i in range(n_train)])]
    dot_general x8 -> x12, matrix products: 21.2 us -> 9.2 us  [dot(): lax.dot_general(a, b, (((ca,), (cb,)), ((), ())), preferred_element_type=...]
    pmax x1 -> x0, blocking collectives: 6 us -> none  [local(): block_top = lax.pmax(jnp.max(block_logits, axis=1), 'test')]
  transfers between devices with their start and end apart: 6 -> 30, of which waited for: 4 -> 16; matrix products, arithmetic and copies ran while one was open for 5% -> 16% of each run, Pallas kernels for 0% -> 0%
where the time goes in v1:
time: 121 us
  waiting for transfers between devices  70.3 us (58%)
  starting transfers between devices  27.8 us (23%)
  matrix products  9.2 us (8%)
  other arithmetic  7.92 us (7%)
  local copies, waits for them, and re-layouts  5.05 us (4%)
    ppermute x19, waiting for transfers between devices, over_train(): return lax.ppermute(a, 'train', [(i, i ^ bit) for i in range(n_train)])  55.1 us
    ppermute x19, starting transfers between devices, over_train(): return lax.ppermute(a, 'train', [(i, i ^ bit) for i in range(n_train)])  20.8 us
    ppermute x11, waiting for transfers between devices, over_test(): return lax.ppermute(a, 'test', [(i, i ^ bit) for i in range(n_test)])  15.2 us
    dot_general x12, matrix products, dot(): lax.dot_general(a, b, (((ca,), (cb,)), ((), ())), preferred_element_type=...  9.2 us
    ppermute x11, starting transfers between devices, over_test(): return lax.ppermute(a, 'test', [(i, i ^ bit) for i in range(n_test)])  7 us
  transfers between devices with their start and end apart: 30, of which 16 were waited for; matrix products, arithmetic and copies ran while one was open for 16% of the time, Pallas kernels for 0%

profile of v1, /device:TPU:0, one launch (start us, length us, event | category | flops | bytes accessed | tf_op | source)
XLA Modules:
  0.0 120.9 jit_solution(6049345184028311438)
XLA Ops:
  0.0 3.0 %collective-permute-start.6 = (bf16[256,896]{1,0:T(8,128)(2,1)}, bf16[256,896]{1,0:T(8,128)(2,1)}, u32[]{:S(2)}, u32[]{:S(2)}) collective-permute-start(bf16[256,896]{1,0:T(8,128)(2,1)} %param.11), channel_id=1, source_target_pairs={{0,4},{4,0},{8,12},{12,8},{16,20},{20,16},{24,28},{28,24},{1,5},{5... | collective-permute-start | bytes 1376264 | tf_op jit(solution)/shard_map/ppermute | solution.py:51
  3.0 1.6 %collective-permute-start.7 = (bf16[256,896]{1,0:T(8,128)(2,1)}, bf16[256,896]{1,0:T(8,128)(2,1)}, u32[]{:S(2)}, u32[]{:S(2)}) collective-permute-start(bf16[256,896]{1,0:T(8,128)(2,1)} %param.9), channel_id=1, source_target_pairs={{0,8},{4,12},{8,0},{12,4},{16,24},{20,28},{24,16},{28,20},{1,9},{5... | collective-permute-start | bytes 1376264 | tf_op jit(solution)/shard_map/ppermute | solution.py:51
  4.5 1.4 %fusion.46 = f32[64,256]{1,0:T(8,128)S(1)} fusion(bf16[896,64]{0,1:T(8,128)(2,1)} %param.16, bf16[256,896]{1,0:T(8,128)(2,1)} %param.9), kind=kOutput, calls=%fused_computation.110 | convolution fusion | flops 29360128 | bytes 638976 | tf_op jit(solution)/shard_map/dot_general | solution.py:14
  5.9 1.4 %fusion.47 = f32[64,256]{1,0:T(8,128)S(1)} fusion(bf16[896,64]{0,1:T(8,128)(2,1)} %param.16, bf16[256,896]{1,0:T(8,128)(2,1)} %param.11), kind=kOutput, calls=%fused_computation.111 | convolution fusion | flops 29360128 | bytes 638976 | tf_op jit(solution)/shard_map/dot_general | solution.py:14
  7.3 1.2 fusion.44
  8.5 1.4 %fusion.45 = f32[64,256]{1,0:T(8,128)S(1)} fusion(bf16[896,64]{0,1:T(8,128)(2,1)} %param.15, bf16[256,896]{1,0:T(8,128)(2,1)} %param.12), kind=kOutput, calls=%fused_computation.109 | convolution fusion | flops 29360128 | bytes 638976 | tf_op jit(solution)/shard_map/dot_general | solution.py:14
  9.9 0.7 pad_maximum_fusion.2
  11.1 1.6 %collective-permute-start.20 = (s32[1,256]{1,0:T(1,128)}, s32[1,256]{1,0:T(1,128)}, u32[]{:S(2)}, u32[]{:S(2)}) collective-permute-start(s32[1,256]{1,0:T(1,128)} %bitcast.13), channel_id=1, source_target_pairs={{0,8},{4,12},{8,0},{12,4},{16,24},{20,28},{24,16},{28,20},{1,9},{5... | collective-permute-start | bytes 3080 | tf_op jit(solution)/shard_map/ppermute | solution.py:51
  12.7 0.8 constant_dynamic-slice_fusion.12
  13.5 0.6 iota_add_fusion.2
  14.4 1.1 constant_dynamic-update-slice_fusion.3
  15.5 0.8 dynamic-slice_bitcast_fusion
  16.2 0.7 convert_element_type.54
  16.9 2.6 %collective-permute-start.10 = (bf16[256,896]{1,0:T(8,128)(2,1)S(1)}, bf16[256,896]{1,0:T(8,128)(2,1)S(1)}, u32[]{:S(2)}, u32[]{:S(2)}) collective-permute-start(bf16[256,896]{1,0:T(8,128)(2,1)S(1)} %copy-done.2), channel_id=1, source_target_pairs={{0,16},{4,20},{8,24},{12,28},{16,0},{20,4},{24,8},{28,12},{1,17},{... | collective-permute-start | bytes 1376264 | tf_op jit(solution)/shard_map/ppermute | solution.py:51
  19.5 0.7 convert_element_type.48
  20.7 0.7 constant_dynamic-slice_fusion.2
  21.7 1.0 fusion.37
  22.7 1.5 %collective-permute-start.1 = (f32[256,256]{1,0:T(8,128)S(1)}, f32[256,256]{1,0:T(8,128)S(1)}, u32[]{:S(2)}, u32[]{:S(2)}) collective-permute-start(f32[256,256]{1,0:T(8,128)S(1)} %fusion.37), channel_id=1, source_target_pairs={{0,2},{1,3},{2,0},{3,1},{4,6},{5,7},{6,4},{7,5},{8,10},{9,11},{10,... | collective-permute-start | bytes 786440 | tf_op jit(solution)/shard_map/ppermute | solution.py:54
  24.3 1.1 constant_dynamic-slice_fusion.11
  25.4 1.1 pad_maximum_fusion
  27.0 24.2 %collective-permute-done.10 = bf16[256,896]{1,0:T(8,128)(2,1)S(1)} collective-permute-done((bf16[256,896]{1,0:T(8,128)(2,1)S(1)}, bf16[256,896]{1,0:T(8,128)(2,1)S(1)}, u32[]{:S(2)}, u32[]{:S(2)}) %collective-permute-start.10) | collective-permute-done | bytes 458784 | tf_op jit(solution)/shard_map/ppermute | solution.py:51
  51.9 1.6 %collective-permute-start.3 = (f32[64,128]{1,0:T(8,128)S(1)}, f32[64,128]{1,0:T(8,128)S(1)}, u32[]{:S(2)}, u32[]{:S(2)}) collective-permute-start(f32[64,128]{1,0:T(8,128)S(1)} %constant_dynamic-slice_fusion.13), channel_id=1, source_target_pairs={{0,4},{4,0},{8,12},{12,8},{16,20},{20,16},{24,28},{28,24},{1,5},{5... | collective-permute-start | bytes 98312 | tf_op jit(solution)/shard_map/ppermute | solution.py:51
  53.6 9.5 %collective-permute-done.27 = bf16[64,4096]{1,0:T(8,128)(2,1)S(1)} collective-permute-done((bf16[64,4096]{1,0:T(8,128)(2,1)}, bf16[64,4096]{1,0:T(8,128)(2,1)S(1)}, u32[]{:S(2)}, u32[]{:S(2)}) %collective-permute-start.27) | collective-permute-done | bytes 524320 | tf_op jit(solution)/shard_map/ppermute | solution.py:51
  64.3 1.5 %collective-permute-start.28 = (bf16[64,4096]{1,0:T(8,128)(2,1)S(1)}, bf16[64,4096]{1,0:T(8,128)(2,1)S(1)}, u32[]{:S(2)}, u32[]{:S(2)}) collective-permute-start(bf16[64,4096]{1,0:T(8,128)(2,1)S(1)} %collective-permute-done.27), channel_id=1, source_target_pairs={{0,4},{4,0},{8,12},{12,8},{16,20},{20,16},{24,28},{28,24},{1,5},{5... | collective-permute-start | bytes 1572872 | tf_op jit(solution)/shard_map/ppermute | solution.py:51
  65.8 2.2 %collective-permute-done.5 = f32[64,128]{1,0:T(8,128)S(1)} collective-permute-done((f32[64,128]{1,0:T(8,128)S(1)}, f32[64,128]{1,0:T(8,128)S(1)}, u32[]{:S(2)}, u32[]{:S(2)}) %collective-permute-start.5) | collective-permute-done | bytes 32800 | tf_op jit(solution)/shard_map/ppermute | solution.py:51
  68.7 1.2 %collective-permute-done.2 = f32[192,256]{1,0:T(8,128)S(1)} collective-permute-done((f32[192,256]{1,0:T(8,128)S(1)}, f32[192,256]{1,0:T(8,128)S(1)}, u32[]{:S(2)}, u32[]{:S(2)}) %collective-permute-start.2) | collective-permute-done | bytes 196640 | tf_op jit(solution)/shard_map/ppermute | solution.py:51
  70.5 1.6 %collective-permute-start.9 = (f32[256,256]{1,0:T(8,128)S(1)}, f32[256,256]{1,0:T(8,128)S(1)}, u32[]{:S(2)}, u32[]{:S(2)}) collective-permute-start(f32[256,256]{1,0:T(8,128)S(1)} %constant_dynamic-slice_fusion.8), channel_id=1, source_target_pairs={{0,2},{1,3},{2,0},{3,1},{4,6},{5,7},{6,4},{7,5},{8,10},{9,11},{10,... | collective-permute-start | bytes 786440 | tf_op jit(solution)/shard_map/ppermute | solution.py:54
  72.5 0.6 collective-permute-start.13
  73.2 6.6 %collective-permute-done.9 = f32[256,256]{1,0:T(8,128)S(1)} collective-permute-done((f32[256,256]{1,0:T(8,128)S(1)}, f32[256,256]{1,0:T(8,128)S(1)}, u32[]{:S(2)}, u32[]{:S(2)}) %collective-permute-start.9) | collective-permute-done | bytes 262176 | tf_op jit(solution)/shard_map/ppermute | solution.py:54
  79.8 3.8 %collective-permute-done.13 = f32[256,256]{1,0:T(8,128)S(1)} collective-permute-done((f32[256,256]{1,0:T(8,128)S(1)}, f32[256,256]{1,0:T(8,128)S(1)}, u32[]{:S(2)}, u32[]{:S(2)}) %collective-permute-start.13) | collective-permute-done | bytes 262176 | tf_op jit(solution)/shard_map/ppermute | solution.py:54
  84.0 1.1 collective-permute-done.14
  85.2 1.7 %collective-permute-start.15 = (f32[2,256]{1,0:T(2,128)S(1)}, f32[2,256]{1,0:T(2,128)S(1)}, u32[]{:S(2)}, u32[]{:S(2)}) collective-permute-start(f32[2,256]{1,0:T(2,128)S(1)} %fusion.27), channel_id=1, source_target_pairs={{0,8},{4,12},{8,0},{12,4},{16,24},{20,28},{24,16},{28,20},{1,9},{5... | collective-permute-start | bytes 6152 | tf_op jit(solution)/shard_map/ppermute | solution.py:51
  86.9 1.9 %collective-permute-done.15 = f32[2,256]{1,0:T(2,128)S(1)} collective-permute-done((f32[2,256]{1,0:T(2,128)S(1)}, f32[2,256]{1,0:T(2,128)S(1)}, u32[]{:S(2)}, u32[]{:S(2)}) %collective-permute-start.15) | collective-permute-done | bytes 2080 | tf_op jit(solution)/shard_map/ppermute | solution.py:51
  89.6 3.1 %collective-permute-start.21 = (f32[64,256]{1,0:T(8,128)S(1)}, f32[64,256]{1,0:T(8,128)S(1)}, u32[]{:S(2)}, u32[]{:S(2)}) collective-permute-start(f32[64,256]{1,0:T(8,128)S(1)} %slice.160), channel_id=1, source_target_pairs={{0,16},{4,20},{8,24},{12,28},{16,0},{20,4},{24,8},{28,12},{1,17},{... | collective-permute-start | bytes 196616 | tf_op jit(solution)/shard_map/ppermute | solution.py:51
  92.7 4.1 %collective-permute-done.21 = f32[64,256]{1,0:T(8,128)S(1)} collective-permute-done((f32[64,256]{1,0:T(8,128)S(1)}, f32[64,256]{1,0:T(8,128)S(1)}, u32[]{:S(2)}, u32[]{:S(2)}) %collective-permute-start.21) | collective-permute-done | bytes 65568 | tf_op jit(solution)/shard_map/ppermute | solution.py:51
  97.4 3.4 %collective-permute-done.22 = f32[64,128]{1,0:T(8,128)S(1)} collective-permute-done((f32[64,128]{1,0:T(8,128)S(1)}, f32[64,128]{1,0:T(8,128)S(1)}, u32[]{:S(2)}, u32[]{:S(2)}) %collective-permute-start.22) | collective-permute-done | bytes 32800 | tf_op jit(solution)/shard_map/ppermute | solution.py:51
  100.8 1.5 %collective-permute-start.23 = (f32[64,128]{1,0:T(8,128)S(1)}, f32[64,128]{1,0:T(8,128)S(1)}, u32[]{:S(2)}, u32[]{:S(2)}) collective-permute-start(f32[64,128]{1,0:T(8,128)S(1)} %slice_add_fusion.3), channel_id=1, source_target_pairs={{0,2},{1,3},{2,0},{3,1},{4,6},{5,7},{6,4},{7,5},{8,10},{9,11},{10,... | collective-permute-start | bytes 98312 | tf_op jit(solution)/shard_map/ppermute | solution.py:54
  102.4 2.4 %collective-permute-done.23 = f32[64,128]{1,0:T(8,128)S(1)} collective-permute-done((f32[64,128]{1,0:T(8,128)S(1)}, f32[64,128]{1,0:T(8,128)S(1)}, u32[]{:S(2)}, u32[]{:S(2)}) %collective-permute-start.23) | collective-permute-done | bytes 32800 | tf_op jit(solution)/shard_map/ppermute | solution.py:54
  104.8 1.6 %collective-permute-start.19 = (f32[128,128]{1,0:T(8,128)S(1)}, f32[128,128]{1,0:T(8,128)S(1)}, u32[]{:S(2)}, u32[]{:S(2)}) collective-permute-start(f32[128,128]{1,0:T(8,128)S(1)} %pad_maximum_fusion.5), channel_id=1, source_target_pairs={{0,2},{1,3},{2,0},{3,1},{4,6},{5,7},{6,4},{7,5},{8,10},{9,11},{10,... | collective-permute-start | bytes 196616 | tf_op jit(solution)/shard_map/ppermute | solution.py:54
  106.4 2.3 %collective-permute-done.24 = f32[64,128]{1,0:T(8,128)S(1)} collective-permute-done((f32[64,128]{1,0:T(8,128)S(1)}, f32[64,128]{1,0:T(8,128)S(1)}, u32[]{:S(2)}, u32[]{:S(2)}) %collective-permute-start.24) | collective-permute-done | bytes 32800 | tf_op jit(solution)/shard_map/ppermute | solution.py:51
  109.2 0.8 collective-permute-done.25
  110.0 0.8 add_convert_fusion.1
  110.7 0.8 fusion.48
  111.6 1.2 %collective-permute-start.29 = (f32[256,256]{1,0:T(8,128)S(1)}, f32[256,256]{1,0:T(8,128)S(1)}, u32[]{:S(2)}, u32[]{:S(2)}) collective-permute-start(f32[256,256]{1,0:T(8,128)S(1)} %fusion.48), channel_id=1, source_target_pairs={{0,8},{4,12},{8,0},{12,4},{16,24},{20,28},{24,16},{28,20},{1,9},{5... | collective-permute-start | bytes 786440 | tf_op jit(solution)/shard_map/ppermute | solution.py:51
  112.8 0.8 add_convert_fusion
  113.6 0.8 fusion.49
  114.4 5.6 %collective-permute-done.29 = f32[256,256]{1,0:T(8,128)S(1)} collective-permute-done((f32[256,256]{1,0:T(8,128)S(1)}, f32[256,256]{1,0:T(8,128)S(1)}, u32[]{:S(2)}, u32[]{:S(2)}) %collective-permute-start.29) | collective-permute-done | bytes 262176 | tf_op jit(solution)/shard_map/ppermute | solution.py:51
  120.0 0.8 pad_maximum_fusion.1
  (107 shorter events, 7.8 us)
Async XLA Ops:
  0.0 7.3 %copy-start = (bf16[256,896]{1,0:T(8,128)(2,1)S(1)}, bf16[256,896]{1,0:T(8,128)(2,1)}, u32[]{:S(2)}) copy-start(bf16[256,896]{1,0:T(8,128)(2,1)} %param.10) | copy-start | bytes 1376260
  0.0 12.7 %copy-start.2 = (bf16[256,896]{1,0:T(8,128)(2,1)S(1)}, bf16[256,896]{1,0:T(8,128)(2,1)}, u32[]{:S(2)}) copy-start(bf16[256,896]{1,0:T(8,128)(2,1)} %param.11) | copy-start | bytes 1376260
  0.0 22.7 %collective-permute-start.6 = (bf16[256,896]{1,0:T(8,128)(2,1)}, bf16[256,896]{1,0:T(8,128)(2,1)}, u32[]{:S(2)}, u32[]{:S(2)}) collective-permute-start(bf16[256,896]{1,0:T(8,128)(2,1)} %param.11), channel_id=1, source_target_pairs={{0,4},{4,0},{8,12},{12,8},{16,20},{20,16},{24,28},{28,24},{1,5},{5... | collective-permute-start | bytes 1376264 | tf_op jit(solution)/shard_map/ppermute | solution.py:51
  3.0 22.4 %collective-permute-start.7 = (bf16[256,896]{1,0:T(8,128)(2,1)}, bf16[256,896]{1,0:T(8,128)(2,1)}, u32[]{:S(2)}, u32[]{:S(2)}) collective-permute-start(bf16[256,896]{1,0:T(8,128)(2,1)} %param.9), channel_id=1, source_target_pairs={{0,8},{4,12},{8,0},{12,4},{16,24},{20,28},{24,16},{28,20},{1,9},{5... | collective-permute-start | bytes 1376264 | tf_op jit(solution)/shard_map/ppermute | solution.py:51
  7.3 6.8 %copy-start.4 = (f32[64,256]{1,0:T(8,128)}, f32[64,256]{1,0:T(8,128)S(1)}, u32[]{:S(2)}) copy-start(f32[64,256]{1,0:T(8,128)S(1)} %fusion.47) | copy-start | bytes 196612
  8.5 5.6 %copy-start.5 = (f32[64,256]{1,0:T(8,128)}, f32[64,256]{1,0:T(8,128)S(1)}, u32[]{:S(2)}) copy-start(f32[64,256]{1,0:T(8,128)S(1)} %fusion.44) | copy-start | bytes 196612
  9.9 4.2 %copy-start.6 = (f32[64,256]{1,0:T(8,128)}, f32[64,256]{1,0:T(8,128)S(1)}, u32[]{:S(2)}) copy-start(f32[64,256]{1,0:T(8,128)S(1)} %fusion.45) | copy-start | bytes 196612
  10.7 10.7 %collective-permute-start = (f32[256,256]{1,0:T(8,128)}, f32[256,256]{1,0:T(8,128)}, u32[]{:S(2)}, u32[]{:S(2)}) collective-permute-start(f32[256,256]{1,0:T(8,128)} %pad_maximum_fusion.2), channel_id=1, source_target_pairs={{0,1},{1,0},{2,3},{3,2},{4,5},{5,4},{6,7},{7,6},{8,9},{9,8},{10,11... | collective-permute-start | bytes 786440 | tf_op jit(solution)/shard_map/ppermute | solution.py:54
  10.7 9.5 %collective-permute-start.16 = (s32[1,256]{1,0:T(1,128)}, s32[1,256]{1,0:T(1,128)}, u32[]{:S(2)}, u32[]{:S(2)}) collective-permute-start(s32[1,256]{1,0:T(1,128)} %bitcast.11), channel_id=1, source_target_pairs={{0,8},{4,12},{8,0},{12,4},{16,24},{20,28},{24,16},{28,20},{1,9},{5... | collective-permute-start | bytes 3080 | tf_op jit(solution)/shard_map/ppermute | solution.py:51
  11.1 5.8 %collective-permute-start.20 = (s32[1,256]{1,0:T(1,128)}, s32[1,256]{1,0:T(1,128)}, u32[]{:S(2)}, u32[]{:S(2)}) collective-permute-start(s32[1,256]{1,0:T(1,128)} %bitcast.13), channel_id=1, source_target_pairs={{0,8},{4,12},{8,0},{12,4},{16,24},{20,28},{24,16},{28,20},{1,9},{5... | collective-permute-start | bytes 3080 | tf_op jit(solution)/shard_map/ppermute | solution.py:51
  14.1 1.3 %copy-start.8 = (s32[128,1]{0,1:T(1,128)S(1)}, s32[128,1]{0,1:T(1,128)}, u32[]{:S(2)}) copy-start(s32[128,1]{0,1:T(1,128)} %get-tuple-element.39) | copy-start | bytes 1540
  14.1 11.2 %copy-start.1 = (bf16[256,896]{1,0:T(8,128)(2,1)S(1)}, bf16[256,896]{1,0:T(8,128)(2,1)}, u32[]{:S(2)}) copy-start(bf16[256,896]{1,0:T(8,128)(2,1)} %param.9) | copy-start | bytes 1376260
  16.9 9.6 %copy-start.7 = (bf16[128,896]{1,0:T(8,128)(2,1)S(1)}, bf16[128,896]{1,0:T(8,128)(2,1)}, u32[]{:S(2)}) copy-start(bf16[128,896]{1,0:T(8,128)(2,1)} %get-tuple-element.12) | copy-start | bytes 688132
  16.9 34.3 %collective-permute-start.10 = (bf16[256,896]{1,0:T(8,128)(2,1)S(1)}, bf16[256,896]{1,0:T(8,128)(2,1)S(1)}, u32[]{:S(2)}, u32[]{:S(2)}) collective-permute-start(bf16[256,896]{1,0:T(8,128)(2,1)S(1)} %copy-done.2), channel_id=1, source_target_pairs={{0,16},{4,20},{8,24},{12,28},{16,0},{20,4},{24,8},{28,12},{1,17},{... | collective-permute-start | bytes 1376264 | tf_op jit(solution)/shard_map/ppermute | solution.py:51
  20.2 31.7 %collective-permute-start.26 = (bf16[64,4096]{1,0:T(8,128)(2,1)}, bf16[64,4096]{1,0:T(8,128)(2,1)S(1)}, u32[]{:S(2)}, u32[]{:S(2)}) collective-permute-start(bf16[64,4096]{1,0:T(8,128)(2,1)} %param.17), channel_id=1, source_target_pairs={{0,4},{4,0},{8,12},{12,8},{16,20},{20,16},{24,28},{28,24},{1,5},{5... | collective-permute-start | bytes 1572872 | tf_op jit(solution)/shard_map/ppermute | solution.py:51
  21.4 41.8 %collective-permute-start.27 = (bf16[64,4096]{1,0:T(8,128)(2,1)}, bf16[64,4096]{1,0:T(8,128)(2,1)S(1)}, u32[]{:S(2)}, u32[]{:S(2)}) collective-permute-start(bf16[64,4096]{1,0:T(8,128)(2,1)} %param.17), channel_id=1, source_target_pairs={{0,16},{4,20},{8,24},{12,28},{16,0},{20,4},{24,8},{28,12},{1,17},{... | collective-permute-start | bytes 1572872 | tf_op jit(solution)/shard_map/ppermute | solution.py:51
  22.7 29.0 %collective-permute-start.1 = (f32[256,256]{1,0:T(8,128)S(1)}, f32[256,256]{1,0:T(8,128)S(1)}, u32[]{:S(2)}, u32[]{:S(2)}) collective-permute-start(f32[256,256]{1,0:T(8,128)S(1)} %fusion.37), channel_id=1, source_target_pairs={{0,2},{1,3},{2,0},{3,1},{4,6},{5,7},{6,4},{7,5},{8,10},{9,11},{10,... | collective-permute-start | bytes 786440 | tf_op jit(solution)/shard_map/ppermute | solution.py:54
  27.0 43.0 %collective-permute-start.8 = (f32[256,512]{1,0:T(8,128)S(1)}, f32[256,512]{1,0:T(8,128)S(1)}, u32[]{:S(2)}, u32[]{:S(2)}) collective-permute-start(f32[256,512]{1,0:T(8,128)S(1)} %fusion.3), channel_id=1, source_target_pairs={{0,1},{1,0},{2,3},{3,2},{4,5},{5,4},{6,7},{7,6},{8,9},{9,8},{10,11... | collective-permute-start | bytes 1572872 | tf_op jit(solution)/shard_map/ppermute | solution.py:54
  51.2 16.8 %collective-permute-start.11 = (bf16[256,896]{1,0:T(8,128)(2,1)S(1)}, bf16[256,896]{1,0:T(8,128)(2,1)S(1)}, u32[]{:S(2)}, u32[]{:S(2)}) collective-permute-start(bf16[256,896]{1,0:T(8,128)(2,1)S(1)} %collective-permute-done.10), channel_id=1, source_target_pairs={{0,4},{4,0},{8,12},{12,8},{16,20},{20,16},{24,28},{28,24},{1,5},{5... | collective-permute-start | bytes 1376264 | tf_op jit(solution)/shard_map/ppermute | solution.py:51
  51.9 11.9 %collective-permute-start.4 = (f32[64,128]{1,0:T(8,128)S(1)}, f32[64,128]{1,0:T(8,128)S(1)}, u32[]{:S(2)}, u32[]{:S(2)}) collective-permute-start(f32[64,128]{1,0:T(8,128)S(1)} %constant_dynamic-slice_fusion.13), channel_id=1, source_target_pairs={{0,16},{4,20},{8,24},{12,28},{16,0},{20,4},{24,8},{28,12},{1,17},{... | collective-permute-start | bytes 98312 | tf_op jit(solution)/shard_map/ppermute | solution.py:51
  51.9 12.3 %collective-permute-start.3 = (f32[64,128]{1,0:T(8,128)S(1)}, f32[64,128]{1,0:T(8,128)S(1)}, u32[]{:S(2)}, u32[]{:S(2)}) collective-permute-start(f32[64,128]{1,0:T(8,128)S(1)} %constant_dynamic-slice_fusion.13), channel_id=1, source_target_pairs={{0,4},{4,0},{8,12},{12,8},{16,20},{20,16},{24,28},{28,24},{1,5},{5... | collective-permute-start | bytes 98312 | tf_op jit(solution)/shard_map/ppermute | solution.py:51
  63.2 6.7 %collective-permute-start.2 = (f32[192,256]{1,0:T(8,128)S(1)}, f32[192,256]{1,0:T(8,128)S(1)}, u32[]{:S(2)}, u32[]{:S(2)}) collective-permute-start(f32[192,256]{1,0:T(8,128)S(1)} %slice.138), channel_id=1, source_target_pairs={{0,8},{4,12},{8,0},{12,4},{16,24},{20,28},{24,16},{28,20},{1,9},{5... | collective-permute-start | bytes 589832 | tf_op jit(solution)/shard_map/ppermute | solution.py:51
  63.4 6.6 %copy-start.3 = (bf16[128,896]{1,0:T(8,128)(2,1)S(1)}, bf16[128,896]{1,0:T(8,128)(2,1)}, u32[]{:S(2)}) copy-start(bf16[128,896]{1,0:T(8,128)(2,1)} %get-tuple-element.11) | copy-start | bytes 688132
  63.8 4.2 %collective-permute-start.5 = (f32[64,128]{1,0:T(8,128)S(1)}, f32[64,128]{1,0:T(8,128)S(1)}, u32[]{:S(2)}, u32[]{:S(2)}) collective-permute-start(f32[64,128]{1,0:T(8,128)S(1)} %collective-permute-done.4), channel_id=1, source_target_pairs={{0,4},{4,0},{8,12},{12,8},{16,20},{20,16},{24,28},{28,24},{1,5},{5... | collective-permute-start | bytes 98312 | tf_op jit(solution)/shard_map/ppermute | solution.py:51
  64.3 22.6 %collective-permute-start.28 = (bf16[64,4096]{1,0:T(8,128)(2,1)S(1)}, bf16[64,4096]{1,0:T(8,128)(2,1)S(1)}, u32[]{:S(2)}, u32[]{:S(2)}) collective-permute-start(bf16[64,4096]{1,0:T(8,128)(2,1)S(1)} %collective-permute-done.27), channel_id=1, source_target_pairs={{0,4},{4,0},{8,12},{12,8},{16,20},{20,16},{24,28},{28,24},{1,5},{5... | collective-permute-start | bytes 1572872 | tf_op jit(solution)/shard_map/ppermute | solution.py:51
  68.6 3.4 %collective-permute-start.12 = (f32[256,512]{1,0:T(8,128)S(1)}, f32[256,512]{1,0:T(8,128)S(1)}, u32[]{:S(2)}, u32[]{:S(2)}) collective-permute-start(f32[256,512]{1,0:T(8,128)S(1)} %fusion.10), channel_id=1, source_target_pairs={{0,1},{1,0},{2,3},{3,2},{4,5},{5,4},{6,7},{7,6},{8,9},{9,8},{10,11... | collective-permute-start | bytes 1572872 | tf_op jit(solution)/shard_map/ppermute | solution.py:54
  70.5 9.3 %collective-permute-start.9 = (f32[256,256]{1,0:T(8,128)S(1)}, f32[256,256]{1,0:T(8,128)S(1)}, u32[]{:S(2)}, u32[]{:S(2)}) collective-permute-start(f32[256,256]{1,0:T(8,128)S(1)} %constant_dynamic-slice_fusion.8), channel_id=1, source_target_pairs={{0,2},{1,3},{2,0},{3,1},{4,6},{5,7},{6,4},{7,5},{8,10},{9,11},{10,... | collective-permute-start | bytes 786440 | tf_op jit(solution)/shard_map/ppermute | solution.py:54
  72.5 11.1 %collective-permute-start.13 = (f32[256,256]{1,0:T(8,128)S(1)}, f32[256,256]{1,0:T(8,128)S(1)}, u32[]{:S(2)}, u32[]{:S(2)}) collective-permute-start(f32[256,256]{1,0:T(8,128)S(1)} %constant_dynamic-slice_fusion.3), channel_id=1, source_target_pairs={{0,2},{1,3},{2,0},{3,1},{4,6},{5,7},{6,4},{7,5},{8,10},{9,11},{10,... | collective-permute-start | bytes 786440 | tf_op jit(solution)/shard_map/ppermute | solution.py:54
  83.9 1.2 %collective-permute-start.14 = (f32[2,256]{1,0:T(2,128)S(1)}, f32[2,256]{1,0:T(2,128)S(1)}, u32[]{:S(2)}, u32[]{:S(2)}) collective-permute-start(f32[2,256]{1,0:T(2,128)S(1)} %pad_maximum_fusion.9), channel_id=1, source_target_pairs={{0,1},{1,0},{2,3},{3,2},{4,5},{5,4},{6,7},{7,6},{8,9},{9,8},{10,11... | collective-permute-start | bytes 6152 | tf_op jit(solution)/shard_map/ppermute | solution.py:54
  85.2 3.7 %collective-permute-start.15 = (f32[2,256]{1,0:T(2,128)S(1)}, f32[2,256]{1,0:T(2,128)S(1)}, u32[]{:S(2)}, u32[]{:S(2)}) collective-permute-start(f32[2,256]{1,0:T(2,128)S(1)} %fusion.27), channel_id=1, source_target_pairs={{0,8},{4,12},{8,0},{12,4},{16,24},{20,28},{24,16},{28,20},{1,9},{5... | collective-permute-start | bytes 6152 | tf_op jit(solution)/shard_map/ppermute | solution.py:51
  89.3 3.4 %collective-permute-start.17 = (f32[64,256]{1,0:T(8,128)S(1)}, f32[64,256]{1,0:T(8,128)S(1)}, u32[]{:S(2)}, u32[]{:S(2)}) collective-permute-start(f32[64,256]{1,0:T(8,128)S(1)} %fusion.21), channel_id=1, source_target_pairs={{0,1},{1,0},{2,3},{3,2},{4,5},{5,4},{6,7},{7,6},{8,9},{9,8},{10,11... | collective-permute-start | bytes 196616 | tf_op jit(solution)/shard_map/ppermute | solution.py:54
  89.6 7.2 %collective-permute-start.21 = (f32[64,256]{1,0:T(8,128)S(1)}, f32[64,256]{1,0:T(8,128)S(1)}, u32[]{:S(2)}, u32[]{:S(2)}) collective-permute-start(f32[64,256]{1,0:T(8,128)S(1)} %slice.160), channel_id=1, source_target_pairs={{0,16},{4,20},{8,24},{12,28},{16,0},{20,4},{24,8},{28,12},{1,17},{... | collective-permute-start | bytes 196616 | tf_op jit(solution)/shard_map/ppermute | solution.py:51
  96.9 4.0 %collective-permute-start.22 = (f32[64,128]{1,0:T(8,128)S(1)}, f32[64,128]{1,0:T(8,128)S(1)}, u32[]{:S(2)}, u32[]{:S(2)}) collective-permute-start(f32[64,128]{1,0:T(8,128)S(1)} %slice.162), channel_id=1, source_target_pairs={{0,4},{4,0},{8,12},{12,8},{16,20},{20,16},{24,28},{28,24},{1,5},{5... | collective-permute-start | bytes 98312 | tf_op jit(solution)/shard_map/ppermute | solution.py:51
  97.4 4.9 %collective-permute-start.18 = (f32[64,256]{1,0:T(8,128)S(1)}, f32[64,256]{1,0:T(8,128)S(1)}, u32[]{:S(2)}, u32[]{:S(2)}) collective-permute-start(f32[64,256]{1,0:T(8,128)S(1)} %pad_maximum_fusion.4), channel_id=1, source_target_pairs={{0,8},{4,12},{8,0},{12,4},{16,24},{20,28},{24,16},{28,20},{1,9},{5... | collective-permute-start | bytes 196616 | tf_op jit(solution)/shard_map/ppermute | solution.py:51
  100.8 3.9 %collective-permute-start.23 = (f32[64,128]{1,0:T(8,128)S(1)}, f32[64,128]{1,0:T(8,128)S(1)}, u32[]{:S(2)}, u32[]{:S(2)}) collective-permute-start(f32[64,128]{1,0:T(8,128)S(1)} %slice_add_fusion.3), channel_id=1, source_target_pairs={{0,2},{1,3},{2,0},{3,1},{4,6},{5,7},{6,4},{7,5},{8,10},{9,11},{10,... | collective-permute-start | bytes 98312 | tf_op jit(solution)/shard_map/ppermute | solution.py:54
  104.8 3.9 %collective-permute-start.24 = (f32[64,128]{1,0:T(8,128)S(1)}, f32[64,128]{1,0:T(8,128)S(1)}, u32[]{:S(2)}, u32[]{:S(2)}) collective-permute-start(f32[64,128]{1,0:T(8,128)S(1)} %add.205), channel_id=1, source_target_pairs={{0,8},{4,12},{8,0},{12,4},{16,24},{20,28},{24,16},{28,20},{1,9},{5... | collective-permute-start | bytes 98312 | tf_op jit(solution)/shard_map/ppermute | solution.py:51
  104.8 4.3 %collective-permute-start.19 = (f32[128,128]{1,0:T(8,128)S(1)}, f32[128,128]{1,0:T(8,128)S(1)}, u32[]{:S(2)}, u32[]{:S(2)}) collective-permute-start(f32[128,128]{1,0:T(8,128)S(1)} %pad_maximum_fusion.5), channel_id=1, source_target_pairs={{0,2},{1,3},{2,0},{3,1},{4,6},{5,7},{6,4},{7,5},{8,10},{9,11},{10,... | collective-permute-start | bytes 196616 | tf_op jit(solution)/shard_map/ppermute | solution.py:54
  108.7 1.3 %collective-permute-start.25 = (f32[128,128]{1,0:T(8,128)S(1)}, f32[128,128]{1,0:T(8,128)S(1)}, u32[]{:S(2)}, u32[]{:S(2)}) collective-permute-start(f32[128,128]{1,0:T(8,128)S(1)} %pad_maximum_fusion.7), channel_id=1, source_target_pairs={{0,1},{1,0},{2,3},{3,2},{4,5},{5,4},{6,7},{7,6},{8,9},{9,8},{10,11... | collective-permute-start | bytes 196616 | tf_op jit(solution)/shard_map/ppermute | solution.py:54
  111.6 8.4 %collective-permute-start.29 = (f32[256,256]{1,0:T(8,128)S(1)}, f32[256,256]{1,0:T(8,128)S(1)}, u32[]{:S(2)}, u32[]{:S(2)}) collective-permute-start(f32[256,256]{1,0:T(8,128)S(1)} %fusion.48), channel_id=1, source_target_pairs={{0,8},{4,12},{8,0},{12,4},{16,24},{20,28},{24,16},{28,20},{1,9},{5... | collective-permute-start | bytes 786440 | tf_op jit(solution)/shard_map/ppermute | solution.py:51

commit v2 on v1

v2 whole, which is shorter than its diff:
```python
import math

import jax
import jax.numpy as jnp
from jax import lax
from jax.sharding import PartitionSpec as P

D = 3584
F32 = jnp.float32
BF16 = jnp.bfloat16


def dot(a, b, ca, cb):
    return lax.dot_general(a, b, (((ca,), (cb,)), ((), ())), preferred_element_type=F32)


def split_two(a):
    high = lax.reduce_precision(a, exponent_bits=8, mantissa_bits=7)
    return jnp.concatenate((high.astype(BF16), (a - high).astype(BF16)), axis=0)


def after(a, *others):
    return lax.optimization_barrier((a, *others))[0]


def local(
    n_train,
    n_test,
    query_out,
    query_in,
    passage_out,
    passage_in_sum,
    passage_len,
    positive,
    proj_in,
    proj_out,
    test_grads,
):
    rank = proj_in.shape[1]
    rows, feats = query_out.shape
    tests = test_grads.shape[0]
    scale = 1.0 / math.sqrt(D)
    me_train = lax.axis_index("train")
    me_test = lax.axis_index("test")
    core = lax.rem(me_test, 2)
    seg_at = lax.div(me_test, 2)
    segs = n_test // 2
    seg = rows // segs
    half = rows // 2
    near = 2
    high_bits = [1 << i for i in range(2, n_train.bit_length() - 1)]
    far = high_bits + [1]

    def over_train(a, bit):
        return lax.ppermute(a, "train", [(i, i ^ bit) for i in range(n_train)])

    def over_test(a, bit):
        return lax.ppermute(a, "test", [(i, i ^ bit) for i in range(n_test)])

    def gather(held, bits):
        held = dict(held)
        for bit in reversed(bits):
            held.update({mask | bit: over_train(a, bit) for mask, a in list(held.items())})
        return held

    masks = [0]
    for bit in far:
        masks = masks + [mask | bit for mask in masks]
    n_far = len(masks)

    halves = passage_out.reshape(2, half, feats)
    lens = passage_len[None, :].astype(F32)
    passages = gather({0: passage_out}, high_bits)
    passages[1] = over_train(after(passage_out, lens), 1)
    query_near = over_train(after(query_out, lens), near)
    passage_y = passages[1].reshape(2, half, feats)

    def half_of(blocks, which):
        return jnp.concatenate(
            [lax.dynamic_index_in_dim(b, which, 0, keepdims=False) for b in blocks], axis=0
        )

    factors = jnp.concatenate(
        (
            dot(proj_in, after(query_in, lens), 0, 1),
            dot(proj_in, after(passage_in_sum, lens), 0, 1),
            dot(proj_out, after(query_out, lens), 0, 1),
            dot(proj_out, after(passage_out, lens), 0, 1),
        ),
        axis=0,
    )
    bit = 1
    while bit < n_test:
        factors = factors + over_test(factors, bit)
        bit *= 2

    def over_cores(blocks, queries):
        sent = over_test(dot(half_of(blocks, 1 - core), queries, 1, 1), 1)
        return dot(half_of(blocks, core), queries, 1, 1) + sent

    def over_chips(total):
        width = total.shape[1]
        bit = n_test // 2
        while bit > 1:
            width //= 2
            upper = lax.rem(lax.div(me_test, bit), 2)
            keep = lax.dynamic_slice_in_dim(total, upper * width, width, 1)
            give = lax.dynamic_slice_in_dim(total, (1 - upper) * width, width, 1)
            total = keep + over_test(give, bit)
            bit //= 2
        return total

    first = [halves, passage_y]
    own_part = over_cores(first, query_out)
    tests_y = over_train(after(test_grads, passages[1]), 1)
    small = lax.dynamic_slice_in_dim(after(factors, own_part)[3 * rank :], core * half, half, 1)
    small_y = over_train(small, 1)
    for mask in masks:
        if mask & 1 and mask & ~1:
            passages[mask] = over_train(after(passages[mask & ~1], tests_y), 1)

    own_part = over_chips(own_part)
    query_near = after(query_near, small_y, own_part)
    queries = jnp.stack((query_out, query_near)).reshape(2, segs, seg, feats)
    queries = queries.transpose(1, 0, 2, 3).reshape(2 * rows, feats)
    near_part = over_chips(over_cores(first, query_near))
    top_part = jnp.concatenate((own_part, near_part), axis=1)
    logits = {0: top_part[:half], 1: top_part[half:]}
    for mask in masks:
        if mask & ~1:
            last_part = over_cores([passages[mask].reshape(2, half, feats)], queries)
            if not mask & 1:
                mid_part = last_part
            logits[mask] = over_chips(last_part)
    logits = jnp.concatenate([logits[mask] for mask in masks], axis=0) * scale

    pass_small = jnp.concatenate((small, small_y), axis=1)
    pass_small = gather({0: after(pass_small, mid_part)}, high_bits)
    pass_small = jnp.concatenate(
        [pass_small[m & ~1][:, (m & 1) * half : (m & 1) * half + half] for m in masks], axis=1
    )
    shared = jnp.concatenate(
        (
            factors[:rank],
            factors[rank : 2 * rank] / lens,
            factors[2 * rank : 3 * rank],
            jnp.broadcast_to(positive[None, :].astype(F32), (8, rows)),
        ),
        axis=0,
    )
    shared_near = over_train(after(shared, mid_part), near)
    mine_of = jnp.concatenate(
        [
            lax.dynamic_slice_in_dim(a[2 * rank :], seg_at * seg, seg, 1)
            for a in (shared, shared_near)
        ],
        axis=1,
    )
    query_small, wanted = mine_of[:rank], mine_of[rank : rank + 1]

    def swap(a):
        return jnp.concatenate((a[:, seg:], a[:, :seg]), axis=1)

    logits = after(logits, pass_small, shared_near)
    top = jnp.max(logits, axis=0, keepdims=True)
    total = jnp.sum(jnp.exp(logits - top), axis=0, keepdims=True)

    def merge(top, total, other):
        new_top = jnp.maximum(top, other[:1])
        return new_top, total * jnp.exp(top - new_top) + other[1:] * jnp.exp(other[:1] - new_top)

    top, total = merge(top, total, over_test(jnp.concatenate((top, total), axis=0), 1))
    top, total = merge(
        top, total, over_train(swap(jnp.concatenate((top, total), axis=0)), near)
    )
    columns = jnp.concatenate(
        [
            lax.broadcasted_iota(jnp.int32, (half, 1), 0)
            + ((me_train ^ mask) * rows + core * half)
            for mask in masks
        ],
        axis=0,
    )
    prob = jnp.exp(logits - top) / total
    dlogit = (prob - (columns == wanted.astype(jnp.int32)).astype(F32)).astype(BF16)

    out_query = dot(split_two(pass_small), dlogit, 1, 0)
    out_query = (out_query[:rank] + out_query[rank:]) * scale
    out_pass = dot(split_two(query_small), dlogit, 1, 1)
    out_pass = (out_pass[:rank] + out_pass[rank:]) * scale

    for bit in reversed(far):
        width = out_pass.shape[1] // 2
        out_pass = out_pass[:, :width] + over_train(out_pass[:, width:], bit)
        if bit == 1:
            out_pass_y = out_pass
    bit = 2
    while bit < n_test:
        out_pass = out_pass + over_test(out_pass, bit)
        bit *= 2
    out_pass = jnp.concatenate((out_pass, over_train(out_pass, near)), axis=0)
    out_pass_other = over_test(out_pass, 1)
    out_pass = jnp.where(
        core == 0,
        jnp.concatenate((out_pass, out_pass_other), axis=1),
        jnp.concatenate((out_pass_other, out_pass), axis=1),
    )

    out_query = out_query + over_test(out_query, 1)
    out_query = out_query + over_train(swap(out_query), near)
    out_query = jnp.concatenate((out_query[:, :seg], out_query[:, seg:]), axis=0)
    bit = 2
    while bit < n_test:
        other = over_test(out_query, bit)
        out_query = jnp.where(
            lax.rem(lax.div(me_test, bit), 2) == 0,
            jnp.concatenate((out_query, other), axis=1),
            jnp.concatenate((other, out_query), axis=1),
        )
        bit *= 2

    held = gather({0: after(test_grads, mid_part)}, high_bits)
    held = {m: after(a, out_pass_y) if m else a for m, a in held.items()}
    held.update({m | 1: over_train(a, 1) if m else tests_y for m, a in held.items()})
    test_block = jnp.zeros((n_far * tests, test_grads.shape[1]), BF16)
    for mask in masks:
        owner = me_train ^ mask
        at = lax.div(owner, 2 * near) * near + lax.rem(owner, near)
        test_block = lax.dynamic_update_slice_in_dim(test_block, held[mask], at * tests, 0)

    def scores_of(acts, which):
        oq = out_query[which * rank : (which + 1) * rank]
        op = out_pass[which * rank : (which + 1) * rank]
        outer = (
            acts[:rank][:, None, :] * oq[None, :, :]
            + acts[rank : 2 * rank][:, None, :] * op[None, :, :]
        )
        grads = outer.reshape(rank * rank, rows).astype(BF16)
        return dot(grads, test_block, 0, 1)

    given = over_train(scores_of(shared_near, 1).astype(BF16), near).astype(F32)
    mine = scores_of(shared, 0)
    unit = near * tests
    mine = [mine[:, i : i + unit] for i in range(0, mine.shape[1], unit)]
    given = [given[:, i : i + unit] for i in range(0, given.shape[1], unit)]
    upper = lax.rem(lax.div(me_train, near), 2) == 1
    pieces = []
    for a, b in zip(mine, given):
        pieces += [jnp.where(upper, b, a), jnp.where(upper, a, b)]
    return jnp.concatenate(pieces, axis=1)


def solution(mesh):
    def body(*args):
        return local(mesh.shape["train"], mesh.shape["test"], *args)

    return jax.shard_map(
        body,
        mesh=mesh,
        in_specs=(
            P("train", "test"),
            P("train", "test"),
            P("train", "test"),
            P("train", "test"),
            P("train"),
            P("train"),
            P("test", None),
            P("test", None),
            P(("test", "train"), None),
        ),
        out_specs=P("train", "test"),
        check_vma=False,
    )
```

time: 121 us -> 88.9 us (0.73)
  waiting for transfers between devices: 70.3 us -> 34.3 us
  starting transfers between devices: 27.8 us -> 34.8 us
  local copies, waits for them, and re-layouts: 5.05 us -> 2.79 us
  other arithmetic: 7.92 us -> 5.88 us
    ppermute x19 -> x16, waiting for transfers between devices: 55.1 us -> 15.4 us  [over_train(): return lax.ppermute(a, 'train', [(i, i ^ bit) for i in range(n_train)])]
    ppermute x11 -> x15, waiting for transfers between devices: 15.2 us -> 18.9 us  [over_test(): return lax.ppermute(a, 'test', [(i, i ^ bit) for i in range(n_test)])]
    ppermute x19 -> x16, starting transfers between devices: 20.8 us -> 24.4 us  [over_train(): return lax.ppermute(a, 'train', [(i, i ^ bit) for i in range(n_train)])]
    ppermute x11 -> x15, starting transfers between devices: 7 us -> 10.4 us  [over_test(): return lax.ppermute(a, 'test', [(i, i ^ bit) for i in range(n_test)])]
    dynamic_slice x11 -> x6, local copies, waits for them, and re-layouts: 3.52 us -> 0.1 us  [the longest x4 0.07 us: over_chips(): give = lax.dynamic_slice_in_dim(total, (1 - upper) * width, width, 1)]
    dot_general x12 -> x16, matrix products: 9.2 us -> 10.1 us  [dot(): lax.dot_general(a, b, (((ca,), (cb,)), ((), ())), preferred_element_type=...]
  transfers between devices with their start and end apart: 30 -> 31, of which waited for: 16 -> 15; matrix products, arithmetic and copies ran while one was open for 16% -> 19% of each run, Pallas kernels for 0% -> 0%
where the time goes in v2:
time: 88.9 us; the launch traced here: 88.6 us
  starting transfers between devices  34.8 us (39%)
  waiting for transfers between devices  34.3 us (39%)
  matrix products  10.1 us (11%)
  other arithmetic  5.88 us (7%)
  local copies, waits for them, and re-layouts  2.79 us (3%)
    ppermute x16, starting transfers between devices, over_train(): return lax.ppermute(a, 'train', [(i, i ^ bit) for i in range(n_train)])  24.4 us
    ppermute x15, waiting for transfers between devices, over_test(): return lax.ppermute(a, 'test', [(i, i ^ bit) for i in range(n_test)])  18.9 us
    ppermute x16, waiting for transfers between devices, over_train(): return lax.ppermute(a, 'train', [(i, i ^ bit) for i in range(n_train)])  15.4 us
    ppermute x15, starting transfers between devices, over_test(): return lax.ppermute(a, 'test', [(i, i ^ bit) for i in range(n_test)])  10.4 us
    dot_general x16, matrix products, dot(): lax.dot_general(a, b, (((ca,), (cb,)), ((), ())), preferred_element_type=...  10.1 us
    dynamic_update_slice x4, local copies, waits for them, and re-layouts, local(): lax.dynamic_update_slice_in_dim(test_block, held[mask], at * tests, 0)  2.28 us
  transfers between devices with their start and end apart: 31, of which 15 were waited for; matrix products, arithmetic and copies ran while one was open for 19% of the time, Pallas kernels for 0%

profile of v2, /device:TPU:0, one launch (start us, length us, event | category | flops | bytes accessed | tf_op | source)
XLA Modules:
  0.0 88.6 jit_solution(228748384073127304)
XLA Ops:
  0.0 4.1 %collective-permute-start.2 = (bf16[256,896]{1,0:T(8,128)(2,1)}, bf16[256,896]{1,0:T(8,128)(2,1)S(1)}, u32[]{:S(2)}, u32[]{:S(2)}) collective-permute-start(bf16[256,896]{1,0:T(8,128)(2,1)} %param.11), channel_id=1, source_target_pairs={{0,16},{4,20},{8,24},{12,28},{16,0},{20,4},{24,8},{28,12},{1,17},{... | collective-permute-start | bytes 1376264 | tf_op jit(solution)/shard_map/ppermute | solution.py:55
  4.1 0.7 convert_element_type.49
  4.8 1.5 %collective-permute-start.4 = (bf16[256,896]{1,0:T(8,128)(2,1)}, bf16[256,896]{1,0:T(8,128)(2,1)S(1)}, u32[]{:S(2)}, u32[]{:S(2)}) collective-permute-start(bf16[256,896]{1,0:T(8,128)(2,1)} %param.11), channel_id=1, source_target_pairs={{0,4},{4,0},{8,12},{12,8},{16,20},{20,16},{24,28},{28,24},{1,5},{5... | collective-permute-start | bytes 1376264 | tf_op jit(solution)/shard_map/ppermute | solution.py:55
  6.3 1.6 %collective-permute-start.3 = (bf16[256,896]{1,0:T(8,128)(2,1)}, bf16[256,896]{1,0:T(8,128)(2,1)S(1)}, u32[]{:S(2)}, u32[]{:S(2)}) collective-permute-start(bf16[256,896]{1,0:T(8,128)(2,1)} %param.9), channel_id=1, source_target_pairs={{0,8},{4,12},{8,0},{12,4},{16,24},{20,28},{24,16},{28,20},{1,9},{5... | collective-permute-start | bytes 1376264 | tf_op jit(solution)/shard_map/ppermute | solution.py:55
  7.9 1.3 %convolution_bitcast_fusion = f32[64,256]{1,0:T(8,128)S(1)} fusion(bf16[256,896]{1,0:T(8,128)(2,1)} %param.11, bf16[896,64]{0,1:T(8,128)(2,1)} %param.16), kind=kOutput, calls=%fused_computation.7 | convolution fusion | flops 29360128 | bytes 638976 | tf_op jit(solution)/shard_map/dot_general | solution.py:14
  9.2 1.3 %convolution_bitcast_fusion.1 = f32[64,256]{1,0:T(8,128)S(1)} fusion(bf16[256,896]{1,0:T(8,128)(2,1)} %param.9, bf16[896,64]{0,1:T(8,128)(2,1)} %param.16), kind=kOutput, calls=%fused_computation.8 | convolution fusion | flops 29360128 | bytes 638976 | tf_op jit(solution)/shard_map/dot_general | solution.py:14
  10.5 1.2 %convolution_bitcast_fusion.2 = f32[64,256]{1,0:T(8,128)S(1)} fusion(bf16[256,896]{1,0:T(8,128)(2,1)S(1)} %copy-done, bf16[896,64]{0,1:T(8,128)(2,1)} %param.15), kind=kOutput, calls=%fused_computation.9 | convolution fusion | flops 29360128 | bytes 638976 | tf_op jit(solution)/shard_map/dot_general | solution.py:14
  11.7 1.4 %convolution_bitcast_fusion.3 = f32[64,256]{1,0:T(8,128)S(1)} fusion(bf16[256,896]{1,0:T(8,128)(2,1)} %param.10, bf16[896,64]{0,1:T(8,128)(2,1)} %param.15), kind=kOutput, calls=%fused_computation.10 | convolution fusion | flops 29360128 | bytes 638976 | tf_op jit(solution)/shard_map/dot_general | solution.py:14
  14.3 0.7 pad_add_fusion
  15.1 1.6 %collective-permute-start.1 = (f32[256,256]{1,0:T(8,128)S(1)}, f32[256,256]{1,0:T(8,128)S(1)}, u32[]{:S(2)}, u32[]{:S(2)}) collective-permute-start(f32[256,256]{1,0:T(8,128)S(1)} %fusion.44), channel_id=1, source_target_pairs={{0,2},{1,3},{2,0},{3,1},{4,6},{5,7},{6,4},{7,5},{8,10},{9,11},{10,... | collective-permute-start | bytes 786440 | tf_op jit(solution)/shard_map/ppermute | solution.py:58
  17.5 1.6 %collective-permute-start.14 = (bf16[64,4096]{1,0:T(8,128)(2,1)}, bf16[64,4096]{1,0:T(8,128)(2,1)S(1)}, u32[]{:S(2)}, u32[]{:S(2)}) collective-permute-start(bf16[64,4096]{1,0:T(8,128)(2,1)} %param.17), channel_id=1, source_target_pairs={{0,4},{4,0},{8,12},{12,8},{16,20},{20,16},{24,28},{28,24},{1,5},{5... | collective-permute-start | bytes 1572872 | tf_op jit(solution)/shard_map/ppermute | solution.py:55
  19.0 4.8 %collective-permute-done.1 = f32[256,256]{1,0:T(8,128)S(1)} collective-permute-done((f32[256,256]{1,0:T(8,128)S(1)}, f32[256,256]{1,0:T(8,128)S(1)}, u32[]{:S(2)}, u32[]{:S(2)}) %collective-permute-start.1) | collective-permute-done | bytes 262176 | tf_op jit(solution)/shard_map/ppermute | solution.py:58
  24.3 1.6 %collective-permute-start.7 = (f32[256,128]{0,1:T(8,128)S(1)}, f32[256,128]{0,1:T(8,128)S(1)}, u32[]{:S(2)}, u32[]{:S(2)}) collective-permute-start(f32[256,128]{0,1:T(8,128)S(1)} %constant_dynamic-slice_fusion.4), channel_id=1, source_target_pairs={{0,2},{1,3},{2,0},{3,1},{4,6},{5,7},{6,4},{7,5},{8,10},{9,11},{10,... | collective-permute-start | bytes 393224 | tf_op jit(solution)/shard_map/ppermute | solution.py:58
  25.9 0.6 collective-permute-start.6
  26.5 3.0 %collective-permute-done.7 = f32[256,128]{0,1:T(8,128)S(1)} collective-permute-done((f32[256,128]{0,1:T(8,128)S(1)}, f32[256,128]{0,1:T(8,128)S(1)}, u32[]{:S(2)}, u32[]{:S(2)}) %collective-permute-start.7) | collective-permute-done | bytes 131104 | tf_op jit(solution)/shard_map/ppermute | solution.py:58
  29.5 3.2 %collective-permute-done.6 = f32[64,128]{1,0:T(8,128)S(1)} collective-permute-done((f32[64,128]{1,0:T(8,128)S(1)}, f32[64,128]{1,0:T(8,128)S(1)}, u32[]{:S(2)}, u32[]{:S(2)}) %collective-permute-start.6) | collective-permute-done | bytes 32800 | tf_op jit(solution)/shard_map/ppermute | solution.py:55
  34.2 1.5 %collective-permute-start.15 = (bf16[256,896]{1,0:T(8,128)(2,1)S(1)}, bf16[256,896]{1,0:T(8,128)(2,1)S(1)}, u32[]{:S(2)}, u32[]{:S(2)}) collective-permute-start(bf16[256,896]{1,0:T(8,128)(2,1)S(1)} %collective-permute-done.2), channel_id=1, source_target_pairs={{0,4},{4,0},{8,12},{12,8},{16,20},{20,16},{24,28},{28,24},{1,5},{5... | collective-permute-start | bytes 1376264 | tf_op jit(solution)/shard_map/ppermute | solution.py:55
  36.6 1.6 %collective-permute-start.9 = (f32[200,256]{1,0:T(8,128)S(1)}, f32[200,256]{1,0:T(8,128)S(1)}, u32[]{:S(2)}, u32[]{:S(2)}) collective-permute-start(f32[200,256]{1,0:T(8,128)S(1)} %pad_maximum_fusion.9), channel_id=1, source_target_pairs={{0,8},{4,12},{8,0},{12,4},{16,24},{20,28},{24,16},{28,20},{1,9},{5... | collective-permute-start | bytes 614408 | tf_op jit(solution)/shard_map/ppermute | solution.py:55
  38.6 1.6 %collective-permute-start.12 = (f32[256,128]{0,1:T(8,128)S(1)}, f32[256,128]{0,1:T(8,128)S(1)}, u32[]{:S(2)}, u32[]{:S(2)}) collective-permute-start(f32[256,128]{0,1:T(8,128)S(1)} %constant_dynamic-slice_fusion.3), channel_id=1, source_target_pairs={{0,2},{1,3},{2,0},{3,1},{4,6},{5,7},{6,4},{7,5},{8,10},{9,11},{10,... | collective-permute-start | bytes 393224 | tf_op jit(solution)/shard_map/ppermute | solution.py:58
  40.2 2.5 %collective-permute-start.28 = (bf16[64,4096]{1,0:T(8,128)(2,1)}, bf16[64,4096]{1,0:T(8,128)(2,1)}, u32[]{:S(2)}, u32[]{:S(2)}) collective-permute-start(bf16[64,4096]{1,0:T(8,128)(2,1)} %param.17), channel_id=1, source_target_pairs={{0,16},{4,20},{8,24},{12,28},{16,0},{20,4},{24,8},{28,12},{1,17},{... | collective-permute-start | bytes 1572872 | tf_op jit(solution)/shard_map/ppermute | solution.py:55
  42.9 1.1 %constant_dynamic-update-slice_fusion.3 = bf16[256,4096]{1,0:T(8,128)(2,1)S(1)} fusion(bf16[256,4096]{1,0:T(8,128)(2,1)S(1)} %broadcast_in_dim.11, bf16[64,4096]{1,0:T(8,128)(2,1)} %param.17, s32[]{:T(128)S(6)} %select_n.99), kind=kLoop, calls=%fused_computation.88 | loop fusion | bytes 1048580 | tf_op jit(solution)/shard_map/dynamic_update_slice | solution.py:229
  44.0 0.6 collective-permute-start.13
  44.7 2.1 %collective-permute-done.15 = bf16[256,896]{1,0:T(8,128)(2,1)S(1)} collective-permute-done((bf16[256,896]{1,0:T(8,128)(2,1)S(1)}, bf16[256,896]{1,0:T(8,128)(2,1)S(1)}, u32[]{:S(2)}, u32[]{:S(2)}) %collective-permute-start.15) | collective-permute-done | bytes 458784 | tf_op jit(solution)/shard_map/ppermute | solution.py:55
  47.3 1.8 %collective-permute-done.13 = f32[128,256]{0,1:T(8,128)S(1)} collective-permute-done((f32[128,256]{0,1:T(8,128)S(1)}, f32[128,256]{0,1:T(8,128)S(1)}, u32[]{:S(2)}, u32[]{:S(2)}) %collective-permute-start.13) | collective-permute-done | bytes 131104 | tf_op jit(solution)/shard_map/ppermute | solution.py:58
  49.5 1.2 %collective-permute-start.17 = (f32[128,256]{0,1:T(8,128)S(1)}, f32[128,256]{0,1:T(8,128)S(1)}, u32[]{:S(2)}, u32[]{:S(2)}) collective-permute-start(f32[128,256]{0,1:T(8,128)S(1)} %constant_dynamic-slice_fusion.1), channel_id=1, source_target_pairs={{0,2},{1,3},{2,0},{3,1},{4,6},{5,7},{6,4},{7,5},{8,10},{9,11},{10,... | collective-permute-start | bytes 393224 | tf_op jit(solution)/shard_map/ppermute | solution.py:58
  50.8 4.0 %collective-permute-done.17 = f32[128,256]{0,1:T(8,128)S(1)} collective-permute-done((f32[128,256]{0,1:T(8,128)S(1)}, f32[128,256]{0,1:T(8,128)S(1)}, u32[]{:S(2)}, u32[]{:S(2)}) %collective-permute-start.17) | collective-permute-done | bytes 131104 | tf_op jit(solution)/shard_map/ppermute | solution.py:58
  55.3 1.1 %collective-permute-done.18 = f32[2,256]{1,0:T(2,128)S(1)} collective-permute-done((f32[2,256]{1,0:T(2,128)S(1)}, f32[2,256]{1,0:T(2,128)S(1)}, u32[]{:S(2)}, u32[]{:S(2)}) %collective-permute-start.18) | collective-permute-done | bytes 2080 | tf_op jit(solution)/shard_map/ppermute | solution.py:58
  56.5 1.6 %collective-permute-start.19 = (f32[2,256]{1,0:T(2,128)S(1)}, f32[2,256]{1,0:T(2,128)S(1)}, u32[]{:S(2)}, u32[]{:S(2)}) collective-permute-start(f32[2,256]{1,0:T(2,128)S(1)} %fusion.34), channel_id=1, source_target_pairs={{0,8},{4,12},{8,0},{12,4},{16,24},{20,28},{24,16},{28,20},{1,9},{5... | collective-permute-start | bytes 6152 | tf_op jit(solution)/shard_map/ppermute | solution.py:55
  58.2 2.1 %collective-permute-done.19 = f32[2,256]{1,0:T(2,128)S(1)} collective-permute-done((f32[2,256]{1,0:T(2,128)S(1)}, f32[2,256]{1,0:T(2,128)S(1)}, u32[]{:S(2)}, u32[]{:S(2)}) %collective-permute-start.19) | collective-permute-done | bytes 2080 | tf_op jit(solution)/shard_map/ppermute | solution.py:55
  61.1 1.6 %collective-permute-start.23 = (f32[64,256]{1,0:T(8,128)S(1)}, f32[64,256]{1,0:T(8,128)S(1)}, u32[]{:S(2)}, u32[]{:S(2)}) collective-permute-start(f32[64,256]{1,0:T(8,128)S(1)} %slice.194), channel_id=1, source_target_pairs={{0,4},{4,0},{8,12},{12,8},{16,20},{20,16},{24,28},{28,24},{1,5},{5... | collective-permute-start | bytes 196616 | tf_op jit(solution)/shard_map/ppermute | solution.py:55
  62.7 1.5 %collective-permute-start.21 = (f32[64,256]{1,0:T(8,128)S(1)}, f32[64,256]{1,0:T(8,128)S(1)}, u32[]{:S(2)}, u32[]{:S(2)}) collective-permute-start(f32[64,256]{1,0:T(8,128)S(1)} %pad_maximum_fusion.13), channel_id=1, source_target_pairs={{0,8},{4,12},{8,0},{12,4},{16,24},{20,28},{24,16},{28,20},{1,9},{5... | collective-permute-start | bytes 196616 | tf_op jit(solution)/shard_map/ppermute | solution.py:55
  64.2 1.4 %collective-permute-done.23 = f32[64,256]{1,0:T(8,128)S(1)} collective-permute-done((f32[64,256]{1,0:T(8,128)S(1)}, f32[64,256]{1,0:T(8,128)S(1)}, u32[]{:S(2)}, u32[]{:S(2)}) %collective-permute-start.23) | collective-permute-done | bytes 65568 | tf_op jit(solution)/shard_map/ppermute | solution.py:55
  66.1 1.5 %collective-permute-start.29 = (bf16[64,4096]{1,0:T(8,128)(2,1)}, bf16[64,4096]{1,0:T(8,128)(2,1)S(1)}, u32[]{:S(2)}, u32[]{:S(2)}) collective-permute-start(bf16[64,4096]{1,0:T(8,128)(2,1)} %collective-permute-done.28), channel_id=1, source_target_pairs={{0,4},{4,0},{8,12},{12,8},{16,20},{20,16},{24,28},{28,24},{1,5},{5... | collective-permute-start | bytes 1572872 | tf_op jit(solution)/shard_map/ppermute | solution.py:55
  67.6 1.1 %constant_dynamic-update-slice_fusion.2 = bf16[256,4096]{1,0:T(8,128)(2,1)S(1)} fusion(bf16[256,4096]{1,0:T(8,128)(2,1)S(1)} %constant_dynamic-update-slice_fusion.3, bf16[64,4096]{1,0:T(8,128)(2,1)} %collective-permute-done.28, s32[]{:T(128)S(6)} %select_n.100), kind=kLoop, calls=%fused_computation.87 | loop fusion | bytes 1048580 | tf_op jit(solution)/shard_map/dynamic_update_slice | solution.py:229
  68.7 1.8 %collective-permute-done.24 = f32[64,128]{1,0:T(8,128)S(1)} collective-permute-done((f32[64,128]{1,0:T(8,128)S(1)}, f32[64,128]{1,0:T(8,128)S(1)}, u32[]{:S(2)}, u32[]{:S(2)}) %collective-permute-start.24) | collective-permute-done | bytes 32800 | tf_op jit(solution)/shard_map/ppermute | solution.py:55
  70.6 1.5 %collective-permute-start.25 = (f32[64,128]{1,0:T(8,128)S(1)}, f32[64,128]{1,0:T(8,128)S(1)}, u32[]{:S(2)}, u32[]{:S(2)}) collective-permute-start(f32[64,128]{1,0:T(8,128)S(1)} %slice_add_fusion.3), channel_id=1, source_target_pairs={{0,2},{1,3},{2,0},{3,1},{4,6},{5,7},{6,4},{7,5},{8,10},{9,11},{10,... | collective-permute-start | bytes 98312 | tf_op jit(solution)/shard_map/ppermute | solution.py:58
  72.1 2.4 %collective-permute-done.25 = f32[64,128]{1,0:T(8,128)S(1)} collective-permute-done((f32[64,128]{1,0:T(8,128)S(1)}, f32[64,128]{1,0:T(8,128)S(1)}, u32[]{:S(2)}, u32[]{:S(2)}) %collective-permute-start.25) | collective-permute-done | bytes 32800 | tf_op jit(solution)/shard_map/ppermute | solution.py:58
  74.5 1.4 %collective-permute-start.26 = (f32[64,128]{1,0:T(8,128)S(1)}, f32[64,128]{1,0:T(8,128)S(1)}, u32[]{:S(2)}, u32[]{:S(2)}) collective-permute-start(f32[64,128]{1,0:T(8,128)S(1)} %add.238), channel_id=1, source_target_pairs={{0,8},{4,12},{8,0},{12,4},{16,24},{20,28},{24,16},{28,20},{1,9},{5... | collective-permute-start | bytes 98312 | tf_op jit(solution)/shard_map/ppermute | solution.py:55
  75.9 1.5 %collective-permute-start.22 = (f32[128,128]{1,0:T(8,128)S(1)}, f32[128,128]{1,0:T(8,128)S(1)}, u32[]{:S(2)}, u32[]{:S(2)}) collective-permute-start(f32[128,128]{1,0:T(8,128)S(1)} %pad_maximum_fusion.14), channel_id=1, source_target_pairs={{0,2},{1,3},{2,0},{3,1},{4,6},{5,7},{6,4},{7,5},{8,10},{9,11},{10,... | collective-permute-start | bytes 196616 | tf_op jit(solution)/shard_map/ppermute | solution.py:58
  77.4 1.0 %collective-permute-done.26 = f32[64,128]{1,0:T(8,128)S(1)} collective-permute-done((f32[64,128]{1,0:T(8,128)S(1)}, f32[64,128]{1,0:T(8,128)S(1)}, u32[]{:S(2)}, u32[]{:S(2)}) %collective-permute-start.26) | collective-permute-done | bytes 32800 | tf_op jit(solution)/shard_map/ppermute | solution.py:55
  78.4 1.8 %collective-permute-done.22 = f32[128,128]{1,0:T(8,128)S(1)} collective-permute-done((f32[128,128]{1,0:T(8,128)S(1)}, f32[128,128]{1,0:T(8,128)S(1)}, u32[]{:S(2)}, u32[]{:S(2)}) %collective-permute-start.22) | collective-permute-done | bytes 65568 | tf_op jit(solution)/shard_map/ppermute | solution.py:58
  80.3 0.7 add_convert_fusion
  81.0 0.8 add_convert_fusion.1
  81.8 0.8 convolution_convert_fusion
  82.6 0.9 %collective-permute-start.30 = (bf16[256,256]{1,0:T(8,128)(2,1)S(1)}, bf16[256,256]{1,0:T(8,128)(2,1)S(1)}, u32[]{:S(2)}, u32[]{:S(2)}) collective-permute-start(bf16[256,256]{1,0:T(8,128)(2,1)S(1)} %convolution_convert_fusion), channel_id=1, source_target_pairs={{0,8},{4,12},{8,0},{12,4},{16,24},{20,28},{24,16},{28,20},{1,9},{5... | collective-permute-start | bytes 393224 | tf_op jit(solution)/shard_map/ppermute | solution.py:55
  83.6 0.8 fusion.53
  84.4 3.3 %collective-permute-done.30 = bf16[256,256]{1,0:T(8,128)(2,1)S(1)} collective-permute-done((bf16[256,256]{1,0:T(8,128)(2,1)S(1)}, bf16[256,256]{1,0:T(8,128)(2,1)S(1)}, u32[]{:S(2)}, u32[]{:S(2)}) %collective-permute-start.30) | collective-permute-done | bytes 131104 | tf_op jit(solution)/shard_map/ppermute | solution.py:55
  87.8 0.8 pad_maximum_fusion.1
  (114 shorter events, 8.5 us)
Async XLA Ops:
  0.0 10.5 %copy-start = (bf16[256,896]{1,0:T(8,128)(2,1)S(1)}, bf16[256,896]{1,0:T(8,128)(2,1)}, u32[]{:S(2)}) copy-start(bf16[256,896]{1,0:T(8,128)(2,1)} %param.12) | copy-start | bytes 1376260
  0.0 15.0 %copy-start.2 = (bf16[256,896]{1,0:T(8,128)(2,1)S(1)}, bf16[256,896]{1,0:T(8,128)(2,1)}, u32[]{:S(2)}) copy-start(bf16[256,896]{1,0:T(8,128)(2,1)} %param.11) | copy-start | bytes 1376260
  0.0 14.3 %copy-start.5 = (s32[256]{0:T(256)S(1)}, s32[256]{0:T(256)}, u32[]{:S(2)}) copy-start(s32[256]{0:T(256)} %param.14) | copy-start | bytes 3076
  0.0 32.8 %collective-permute-start.2 = (bf16[256,896]{1,0:T(8,128)(2,1)}, bf16[256,896]{1,0:T(8,128)(2,1)S(1)}, u32[]{:S(2)}, u32[]{:S(2)}) collective-permute-start(bf16[256,896]{1,0:T(8,128)(2,1)} %param.11), channel_id=1, source_target_pairs={{0,16},{4,20},{8,24},{12,28},{16,0},{20,4},{24,8},{28,12},{1,17},{... | collective-permute-start | bytes 1376264 | tf_op jit(solution)/shard_map/ppermute | solution.py:55
  4.8 12.2 %collective-permute-start.4 = (bf16[256,896]{1,0:T(8,128)(2,1)}, bf16[256,896]{1,0:T(8,128)(2,1)S(1)}, u32[]{:S(2)}, u32[]{:S(2)}) collective-permute-start(bf16[256,896]{1,0:T(8,128)(2,1)} %param.11), channel_id=1, source_target_pairs={{0,4},{4,0},{8,12},{12,8},{16,20},{20,16},{24,28},{28,24},{1,5},{5... | collective-permute-start | bytes 1376264 | tf_op jit(solution)/shard_map/ppermute | solution.py:55
  6.3 23.2 %collective-permute-start.3 = (bf16[256,896]{1,0:T(8,128)(2,1)}, bf16[256,896]{1,0:T(8,128)(2,1)S(1)}, u32[]{:S(2)}, u32[]{:S(2)}) collective-permute-start(bf16[256,896]{1,0:T(8,128)(2,1)} %param.9), channel_id=1, source_target_pairs={{0,8},{4,12},{8,0},{12,4},{16,24},{20,28},{24,16},{28,20},{1,9},{5... | collective-permute-start | bytes 1376264 | tf_op jit(solution)/shard_map/ppermute | solution.py:55
  11.7 5.3 %copy-start.1 = (bf16[256,896]{1,0:T(8,128)(2,1)S(1)}, bf16[256,896]{1,0:T(8,128)(2,1)}, u32[]{:S(2)}) copy-start(bf16[256,896]{1,0:T(8,128)(2,1)} %param.9) | copy-start | bytes 1376260
  13.1 1.9 %collective-permute-start = (f32[256,256]{1,0:T(8,128)S(1)}, f32[256,256]{1,0:T(8,128)S(1)}, u32[]{:S(2)}, u32[]{:S(2)}) collective-permute-start(f32[256,256]{1,0:T(8,128)S(1)} %pad_maximum_fusion.8), channel_id=1, source_target_pairs={{0,1},{1,0},{2,3},{3,2},{4,5},{5,4},{6,7},{7,6},{8,9},{9,8},{10,11... | collective-permute-start | bytes 786440 | tf_op jit(solution)/shard_map/ppermute | solution.py:58
  15.1 8.7 %collective-permute-start.1 = (f32[256,256]{1,0:T(8,128)S(1)}, f32[256,256]{1,0:T(8,128)S(1)}, u32[]{:S(2)}, u32[]{:S(2)}) collective-permute-start(f32[256,256]{1,0:T(8,128)S(1)} %fusion.44), channel_id=1, source_target_pairs={{0,2},{1,3},{2,0},{3,1},{4,6},{5,7},{6,4},{7,5},{8,10},{9,11},{10,... | collective-permute-start | bytes 786440 | tf_op jit(solution)/shard_map/ppermute | solution.py:58
  17.4 6.5 %collective-permute-start.5 = (f32[256,256]{0,1:T(8,128)S(1)}, f32[256,256]{0,1:T(8,128)S(1)}, u32[]{:S(2)}, u32[]{:S(2)}) collective-permute-start(f32[256,256]{0,1:T(8,128)S(1)} %fusion.5), channel_id=1, source_target_pairs={{0,1},{1,0},{2,3},{3,2},{4,5},{5,4},{6,7},{7,6},{8,9},{9,8},{10,11... | collective-permute-start | bytes 786440 | tf_op jit(solution)/shard_map/ppermute | solution.py:58
  17.5 16.8 %collective-permute-start.14 = (bf16[64,4096]{1,0:T(8,128)(2,1)}, bf16[64,4096]{1,0:T(8,128)(2,1)S(1)}, u32[]{:S(2)}, u32[]{:S(2)}) collective-permute-start(bf16[64,4096]{1,0:T(8,128)(2,1)} %param.17), channel_id=1, source_target_pairs={{0,4},{4,0},{8,12},{12,8},{16,20},{20,16},{24,28},{28,24},{1,5},{5... | collective-permute-start | bytes 1572872 | tf_op jit(solution)/shard_map/ppermute | solution.py:55
  24.3 5.2 %collective-permute-start.7 = (f32[256,128]{0,1:T(8,128)S(1)}, f32[256,128]{0,1:T(8,128)S(1)}, u32[]{:S(2)}, u32[]{:S(2)}) collective-permute-start(f32[256,128]{0,1:T(8,128)S(1)} %constant_dynamic-slice_fusion.4), channel_id=1, source_target_pairs={{0,2},{1,3},{2,0},{3,1},{4,6},{5,7},{6,4},{7,5},{8,10},{9,11},{10,... | collective-permute-start | bytes 393224 | tf_op jit(solution)/shard_map/ppermute | solution.py:58
  25.9 6.8 %collective-permute-start.6 = (f32[64,128]{1,0:T(8,128)S(1)}, f32[64,128]{1,0:T(8,128)S(1)}, u32[]{:S(2)}, u32[]{:S(2)}) collective-permute-start(f32[64,128]{1,0:T(8,128)S(1)} %constant_dynamic-slice_fusion.5), channel_id=1, source_target_pairs={{0,4},{4,0},{8,12},{12,8},{16,20},{20,16},{24,28},{28,24},{1,5},{5... | collective-permute-start | bytes 98312 | tf_op jit(solution)/shard_map/ppermute | solution.py:55
  33.2 2.5 %collective-permute-start.8 = (f32[128,512]{0,1:T(8,128)S(1)}, f32[128,512]{0,1:T(8,128)S(1)}, u32[]{:S(2)}, u32[]{:S(2)}) collective-permute-start(f32[128,512]{0,1:T(8,128)S(1)} %fusion.9), channel_id=1, source_target_pairs={{0,1},{1,0},{2,3},{3,2},{4,5},{5,4},{6,7},{7,6},{8,9},{9,8},{10,11... | collective-permute-start | bytes 786440 | tf_op jit(solution)/shard_map/ppermute | solution.py:58
  33.7 4.6 %collective-permute-start.11 = (f32[256,256]{0,1:T(8,128)S(1)}, f32[256,256]{0,1:T(8,128)S(1)}, u32[]{:S(2)}, u32[]{:S(2)}) collective-permute-start(f32[256,256]{0,1:T(8,128)S(1)} %fusion.4), channel_id=1, source_target_pairs={{0,1},{1,0},{2,3},{3,2},{4,5},{5,4},{6,7},{7,6},{8,9},{9,8},{10,11... | collective-permute-start | bytes 786440 | tf_op jit(solution)/shard_map/ppermute | solution.py:58
  34.2 5.9 %copy-start.3 = (bf16[64,4096]{1,0:T(8,128)(2,1)}, bf16[64,4096]{1,0:T(8,128)(2,1)S(1)}, u32[]{:S(2)}) copy-start(bf16[64,4096]{1,0:T(8,128)(2,1)S(1)} %collective-permute-done.14) | copy-start | bytes 1572868
  34.2 12.5 %collective-permute-start.15 = (bf16[256,896]{1,0:T(8,128)(2,1)S(1)}, bf16[256,896]{1,0:T(8,128)(2,1)S(1)}, u32[]{:S(2)}, u32[]{:S(2)}) collective-permute-start(bf16[256,896]{1,0:T(8,128)(2,1)S(1)} %collective-permute-done.2), channel_id=1, source_target_pairs={{0,4},{4,0},{8,12},{12,8},{16,20},{20,16},{24,28},{28,24},{1,5},{5... | collective-permute-start | bytes 1376264 | tf_op jit(solution)/shard_map/ppermute | solution.py:55
  36.2 7.9 %collective-permute-start.10 = (f32[64,256]{1,0:T(8,128)S(1)}, f32[64,256]{1,0:T(8,128)S(1)}, u32[]{:S(2)}, u32[]{:S(2)}) collective-permute-start(f32[64,256]{1,0:T(8,128)S(1)} %pad_maximum_fusion.12), channel_id=1, source_target_pairs={{0,16},{4,20},{8,24},{12,28},{16,0},{20,4},{24,8},{28,12},{1,17},{... | collective-permute-start | bytes 196616 | tf_op jit(solution)/shard_map/ppermute | solution.py:55
  36.6 14.1 %collective-permute-start.9 = (f32[200,256]{1,0:T(8,128)S(1)}, f32[200,256]{1,0:T(8,128)S(1)}, u32[]{:S(2)}, u32[]{:S(2)}) collective-permute-start(f32[200,256]{1,0:T(8,128)S(1)} %pad_maximum_fusion.9), channel_id=1, source_target_pairs={{0,8},{4,12},{8,0},{12,4},{16,24},{20,28},{24,16},{28,20},{1,9},{5... | collective-permute-start | bytes 614408 | tf_op jit(solution)/shard_map/ppermute | solution.py:55
  38.6 6.1 %collective-permute-start.12 = (f32[256,128]{0,1:T(8,128)S(1)}, f32[256,128]{0,1:T(8,128)S(1)}, u32[]{:S(2)}, u32[]{:S(2)}) collective-permute-start(f32[256,128]{0,1:T(8,128)S(1)} %constant_dynamic-slice_fusion.3), channel_id=1, source_target_pairs={{0,2},{1,3},{2,0},{3,1},{4,6},{5,7},{6,4},{7,5},{8,10},{9,11},{10,... | collective-permute-start | bytes 393224 | tf_op jit(solution)/shard_map/ppermute | solution.py:58
  40.2 25.9 %collective-permute-start.28 = (bf16[64,4096]{1,0:T(8,128)(2,1)}, bf16[64,4096]{1,0:T(8,128)(2,1)}, u32[]{:S(2)}, u32[]{:S(2)}) collective-permute-start(bf16[64,4096]{1,0:T(8,128)(2,1)} %param.17), channel_id=1, source_target_pairs={{0,16},{4,20},{8,24},{12,28},{16,0},{20,4},{24,8},{28,12},{1,17},{... | collective-permute-start | bytes 1572872 | tf_op jit(solution)/shard_map/ppermute | solution.py:55
  44.0 5.0 %collective-permute-start.13 = (f32[128,256]{0,1:T(8,128)S(1)}, f32[128,256]{0,1:T(8,128)S(1)}, u32[]{:S(2)}, u32[]{:S(2)}) collective-permute-start(f32[128,256]{0,1:T(8,128)S(1)} %constant_dynamic-slice_fusion.2), channel_id=1, source_target_pairs={{0,2},{1,3},{2,0},{3,1},{4,6},{5,7},{6,4},{7,5},{8,10},{9,11},{10,... | collective-permute-start | bytes 393224 | tf_op jit(solution)/shard_map/ppermute | solution.py:58
  47.2 1.9 %collective-permute-start.16 = (f32[128,512]{0,1:T(8,128)S(1)}, f32[128,512]{0,1:T(8,128)S(1)}, u32[]{:S(2)}, u32[]{:S(2)}) collective-permute-start(f32[128,512]{0,1:T(8,128)S(1)} %fusion.6), channel_id=1, source_target_pairs={{0,1},{1,0},{2,3},{3,2},{4,5},{5,4},{6,7},{7,6},{8,9},{9,8},{10,11... | collective-permute-start | bytes 786440 | tf_op jit(solution)/shard_map/ppermute | solution.py:58
  49.5 5.3 %collective-permute-start.17 = (f32[128,256]{0,1:T(8,128)S(1)}, f32[128,256]{0,1:T(8,128)S(1)}, u32[]{:S(2)}, u32[]{:S(2)}) collective-permute-start(f32[128,256]{0,1:T(8,128)S(1)} %constant_dynamic-slice_fusion.1), channel_id=1, source_target_pairs={{0,2},{1,3},{2,0},{3,1},{4,6},{5,7},{6,4},{7,5},{8,10},{9,11},{10,... | collective-permute-start | bytes 393224 | tf_op jit(solution)/shard_map/ppermute | solution.py:58
  55.2 1.2 %collective-permute-start.18 = (f32[2,256]{1,0:T(2,128)S(1)}, f32[2,256]{1,0:T(2,128)S(1)}, u32[]{:S(2)}, u32[]{:S(2)}) collective-permute-start(f32[2,256]{1,0:T(2,128)S(1)} %pad_maximum_fusion.17), channel_id=1, source_target_pairs={{0,1},{1,0},{2,3},{3,2},{4,5},{5,4},{6,7},{7,6},{8,9},{9,8},{10,11... | collective-permute-start | bytes 6152 | tf_op jit(solution)/shard_map/ppermute | solution.py:58
  56.5 3.8 %collective-permute-start.19 = (f32[2,256]{1,0:T(2,128)S(1)}, f32[2,256]{1,0:T(2,128)S(1)}, u32[]{:S(2)}, u32[]{:S(2)}) collective-permute-start(f32[2,256]{1,0:T(2,128)S(1)} %fusion.34), channel_id=1, source_target_pairs={{0,8},{4,12},{8,0},{12,4},{16,24},{20,28},{24,16},{28,20},{1,9},{5... | collective-permute-start | bytes 6152 | tf_op jit(solution)/shard_map/ppermute | solution.py:55
  60.3 8.3 %copy-start.4 = (bf16[64,4096]{1,0:T(8,128)(2,1)S(1)}, bf16[64,4096]{1,0:T(8,128)(2,1)}, u32[]{:S(2)}) copy-start(bf16[64,4096]{1,0:T(8,128)(2,1)} %copy-done.3) | copy-start | bytes 1572868
  60.8 1.9 %collective-permute-start.20 = (f32[64,256]{1,0:T(8,128)S(1)}, f32[64,256]{1,0:T(8,128)S(1)}, u32[]{:S(2)}, u32[]{:S(2)}) collective-permute-start(f32[64,256]{1,0:T(8,128)S(1)} %fusion.24), channel_id=1, source_target_pairs={{0,1},{1,0},{2,3},{3,2},{4,5},{5,4},{6,7},{7,6},{8,9},{9,8},{10,11... | collective-permute-start | bytes 196616 | tf_op jit(solution)/shard_map/ppermute | solution.py:58
  61.1 4.6 %collective-permute-start.23 = (f32[64,256]{1,0:T(8,128)S(1)}, f32[64,256]{1,0:T(8,128)S(1)}, u32[]{:S(2)}, u32[]{:S(2)}) collective-permute-start(f32[64,256]{1,0:T(8,128)S(1)} %slice.194), channel_id=1, source_target_pairs={{0,4},{4,0},{8,12},{12,8},{16,20},{20,16},{24,28},{28,24},{1,5},{5... | collective-permute-start | bytes 196616 | tf_op jit(solution)/shard_map/ppermute | solution.py:55
  62.7 9.3 %collective-permute-start.21 = (f32[64,256]{1,0:T(8,128)S(1)}, f32[64,256]{1,0:T(8,128)S(1)}, u32[]{:S(2)}, u32[]{:S(2)}) collective-permute-start(f32[64,256]{1,0:T(8,128)S(1)} %pad_maximum_fusion.13), channel_id=1, source_target_pairs={{0,8},{4,12},{8,0},{12,4},{16,24},{20,28},{24,16},{28,20},{1,9},{5... | collective-permute-start | bytes 196616 | tf_op jit(solution)/shard_map/ppermute | solution.py:55
  65.7 4.9 %collective-permute-start.24 = (f32[64,128]{1,0:T(8,128)S(1)}, f32[64,128]{1,0:T(8,128)S(1)}, u32[]{:S(2)}, u32[]{:S(2)}) collective-permute-start(f32[64,128]{1,0:T(8,128)S(1)} %slice.196), channel_id=1, source_target_pairs={{0,16},{4,20},{8,24},{12,28},{16,0},{20,4},{24,8},{28,12},{1,17},{... | collective-permute-start | bytes 98312 | tf_op jit(solution)/shard_map/ppermute | solution.py:55
  66.1 15.7 %collective-permute-start.29 = (bf16[64,4096]{1,0:T(8,128)(2,1)}, bf16[64,4096]{1,0:T(8,128)(2,1)S(1)}, u32[]{:S(2)}, u32[]{:S(2)}) collective-permute-start(bf16[64,4096]{1,0:T(8,128)(2,1)} %collective-permute-done.28), channel_id=1, source_target_pairs={{0,4},{4,0},{8,12},{12,8},{16,20},{20,16},{24,28},{28,24},{1,5},{5... | collective-permute-start | bytes 1572872 | tf_op jit(solution)/shard_map/ppermute | solution.py:55
  70.6 3.9 %collective-permute-start.25 = (f32[64,128]{1,0:T(8,128)S(1)}, f32[64,128]{1,0:T(8,128)S(1)}, u32[]{:S(2)}, u32[]{:S(2)}) collective-permute-start(f32[64,128]{1,0:T(8,128)S(1)} %slice_add_fusion.3), channel_id=1, source_target_pairs={{0,2},{1,3},{2,0},{3,1},{4,6},{5,7},{6,4},{7,5},{8,10},{9,11},{10,... | collective-permute-start | bytes 98312 | tf_op jit(solution)/shard_map/ppermute | solution.py:58
  74.5 3.9 %collective-permute-start.26 = (f32[64,128]{1,0:T(8,128)S(1)}, f32[64,128]{1,0:T(8,128)S(1)}, u32[]{:S(2)}, u32[]{:S(2)}) collective-permute-start(f32[64,128]{1,0:T(8,128)S(1)} %add.238), channel_id=1, source_target_pairs={{0,8},{4,12},{8,0},{12,4},{16,24},{20,28},{24,16},{28,20},{1,9},{5... | collective-permute-start | bytes 98312 | tf_op jit(solution)/shard_map/ppermute | solution.py:55
  75.9 4.3 %collective-permute-start.22 = (f32[128,128]{1,0:T(8,128)S(1)}, f32[128,128]{1,0:T(8,128)S(1)}, u32[]{:S(2)}, u32[]{:S(2)}) collective-permute-start(f32[128,128]{1,0:T(8,128)S(1)} %pad_maximum_fusion.14), channel_id=1, source_target_pairs={{0,2},{1,3},{2,0},{3,1},{4,6},{5,7},{6,4},{7,5},{8,10},{9,11},{10,... | collective-permute-start | bytes 196616 | tf_op jit(solution)/shard_map/ppermute | solution.py:58
  78.4 1.8 %collective-permute-start.27 = (f32[128,128]{1,0:T(8,128)S(1)}, f32[128,128]{1,0:T(8,128)S(1)}, u32[]{:S(2)}, u32[]{:S(2)}) collective-permute-start(f32[128,128]{1,0:T(8,128)S(1)} %pad_maximum_fusion.15), channel_id=1, source_target_pairs={{0,1},{1,0},{2,3},{3,2},{4,5},{5,4},{6,7},{7,6},{8,9},{9,8},{10,11... | collective-permute-start | bytes 196616 | tf_op jit(solution)/shard_map/ppermute | solution.py:58
  82.6 5.0 %collective-permute-start.30 = (bf16[256,256]{1,0:T(8,128)(2,1)S(1)}, bf16[256,256]{1,0:T(8,128)(2,1)S(1)}, u32[]{:S(2)}, u32[]{:S(2)}) collective-permute-start(bf16[256,256]{1,0:T(8,128)(2,1)S(1)} %convolution_convert_fusion), channel_id=1, source_target_pairs={{0,8},{4,12},{8,0},{12,4},{16,24},{20,28},{24,16},{28,20},{1,9},{5... | collective-permute-start | bytes 393224 | tf_op jit(solution)/shard_map/ppermute | solution.py:55

commit v3 on v2

--- a/solution.py
+++ b/solution.py
@@ -112,15 +112,15 @@
 
     first = [halves, passage_y]
     own_part = over_cores(first, query_out)
-    tests_y = over_train(after(test_grads, passages[1]), 1)
+    tests_y = over_train(after(test_grads[:32], passages[1]), 1)
     small = lax.dynamic_slice_in_dim(after(factors, own_part)[3 * rank :], core * half, half, 1)
     small_y = over_train(small, 1)
     for mask in masks:
         if mask & 1 and mask & ~1:
-            passages[mask] = over_train(after(passages[mask & ~1], tests_y), 1)
+            passages[mask] = over_train(after(passages[mask & ~1], own_part, tests_y), 1)
 
     own_part = over_chips(own_part)
-    query_near = after(query_near, small_y, own_part)
+    query_near = after(query_near, small_y)
     queries = jnp.stack((query_out, query_near)).reshape(2, segs, seg, feats)
     queries = queries.transpose(1, 0, 2, 3).reshape(2 * rows, feats)
     near_part = over_chips(over_cores(first, query_near))
@@ -161,6 +161,8 @@
     def swap(a):
         return jnp.concatenate((a[:, seg:], a[:, :seg]), axis=1)
 
+    tests_y2 = over_train(after(test_grads[32:], *(passages[m] for m in masks if m & 1 and m > 1)), 1)
+    tests_y = jnp.concatenate((tests_y, tests_y2), axis=0)
     logits = after(logits, pass_small, shared_near)
     top = jnp.max(logits, axis=0, keepdims=True)
     total = jnp.sum(jnp.exp(logits - top), axis=0, keepdims=True)
@@ -171,7 +173,7 @@
 
     top, total = merge(top, total, over_test(jnp.concatenate((top, total), axis=0), 1))
     top, total = merge(
-        top, total, over_train(swap(jnp.concatenate((top, total), axis=0)), near)
+        top, total, over_train(after(swap(jnp.concatenate((top, total), axis=0)), tests_y2), near)
     )
     columns = jnp.concatenate(
         [

time: 88.9 us -> 85.2 us (0.958)
  waiting for transfers between devices: 34.3 us -> 28.9 us
  local copies, waits for them, and re-layouts: 2.79 us -> 4.62 us
  starting transfers between devices: 34.8 us -> 33.6 us
  other arithmetic: 5.88 us -> 6.95 us
    ppermute x16 -> x17, waiting for transfers between devices: 15.4 us -> 10 us  [over_train(): return lax.ppermute(a, 'train', [(i, i ^ bit) for i in range(n_train)])]
    slice x0 -> x1, local copies, waits for them, and re-layouts: none -> 1.89 us  [local(): test_grads[32:]]
    ppermute x16 -> x17, starting transfers between devices: 24.4 us -> 22.8 us  [over_train(): return lax.ppermute(a, 'train', [(i, i ^ bit) for i in range(n_train)])]
    dynamic_update_slice x0 -> x1, other arithmetic: none -> 0.99 us  [local(): lax.dynamic_update_slice_in_dim(test_block, held[mask], at * tests, 0)]
    dynamic_update_slice x4 -> x3, local copies, waits for them, and re-layouts: 2.28 us -> 2.23 us  [local(): lax.dynamic_update_slice_in_dim(test_block, held[mask], at * tests, 0)]
  transfers between devices with their start and end apart: 31 -> 32, of which waited for: 15 -> 14; matrix products, arithmetic and copies ran while one was open for 19% -> 23% of each run, Pallas kernels for 0% -> 0%
where the time goes in v3:
time: 85.2 us; the launch traced here: 84.8 us
  starting transfers between devices  33.6 us (39%)
  waiting for transfers between devices  28.9 us (34%)
  matrix products  10.1 us (12%)
  other arithmetic  6.95 us (8%)
  local copies, waits for them, and re-layouts  4.62 us (5%)
    ppermute x17, starting transfers between devices, over_train(): return lax.ppermute(a, 'train', [(i, i ^ bit) for i in range(n_train)])  22.8 us
    ppermute x15, waiting for transfers between devices, over_test(): return lax.ppermute(a, 'test', [(i, i ^ bit) for i in range(n_test)])  18.8 us
    ppermute x15, starting transfers between devices, over_test(): return lax.ppermute(a, 'test', [(i, i ^ bit) for i in range(n_test)])  10.8 us
    dot_general x16, matrix products, dot(): lax.dot_general(a, b, (((ca,), (cb,)), ((), ())), preferred_element_type=...  10.1 us
    ppermute x17, waiting for transfers between devices, over_train(): return lax.ppermute(a, 'train', [(i, i ^ bit) for i in range(n_train)])  10 us
    dynamic_update_slice x3, local copies, waits for them, and re-layouts, local(): lax.dynamic_update_slice_in_dim(test_block, held[mask], at * tests, 0)  2.23 us
    slice x1, local copies, waits for them, and re-layouts, local(): test_grads[32:]  1.89 us
  transfers between devices with their start and end apart: 32, of which 14 were waited for; matrix products, arithmetic and copies ran while one was open for 23% of the time, Pallas kernels for 0%

profile of v3, /device:TPU:0, one launch (start us, length us, event | category | flops | bytes accessed | tf_op | source)
XLA Modules:
  0.0 84.8 jit_solution(5831499985440869863)
XLA Ops:
  0.0 4.0 %collective-permute-start.2 = (bf16[256,896]{1,0:T(8,128)(2,1)}, bf16[256,896]{1,0:T(8,128)(2,1)S(1)}, u32[]{:S(2)}, u32[]{:S(2)}) collective-permute-start(bf16[256,896]{1,0:T(8,128)(2,1)} %param.11), channel_id=1, source_target_pairs={{0,16},{4,20},{8,24},{12,28},{16,0},{20,4},{24,8},{28,12},{1,17},{... | collective-permute-start | bytes 1376264 | tf_op jit(solution)/shard_map/ppermute | solution.py:55
  4.0 0.7 convert_element_type.49
  4.7 1.5 %collective-permute-start.4 = (bf16[256,896]{1,0:T(8,128)(2,1)}, bf16[256,896]{1,0:T(8,128)(2,1)S(1)}, u32[]{:S(2)}, u32[]{:S(2)}) collective-permute-start(bf16[256,896]{1,0:T(8,128)(2,1)} %param.11), channel_id=1, source_target_pairs={{0,4},{4,0},{8,12},{12,8},{16,20},{20,16},{24,28},{28,24},{1,5},{5... | collective-permute-start | bytes 1376264 | tf_op jit(solution)/shard_map/ppermute | solution.py:55
  6.2 1.6 %collective-permute-start.3 = (bf16[256,896]{1,0:T(8,128)(2,1)}, bf16[256,896]{1,0:T(8,128)(2,1)S(1)}, u32[]{:S(2)}, u32[]{:S(2)}) collective-permute-start(bf16[256,896]{1,0:T(8,128)(2,1)} %param.9), channel_id=1, source_target_pairs={{0,8},{4,12},{8,0},{12,4},{16,24},{20,28},{24,16},{28,20},{1,9},{5... | collective-permute-start | bytes 1376264 | tf_op jit(solution)/shard_map/ppermute | solution.py:55
  7.8 1.3 %convolution_bitcast_fusion = f32[64,256]{1,0:T(8,128)S(1)} fusion(bf16[256,896]{1,0:T(8,128)(2,1)} %param.11, bf16[896,64]{0,1:T(8,128)(2,1)} %param.16), kind=kOutput, calls=%fused_computation.7 | convolution fusion | flops 29360128 | bytes 638976 | tf_op jit(solution)/shard_map/dot_general | solution.py:14
  9.1 1.3 %convolution_bitcast_fusion.1 = f32[64,256]{1,0:T(8,128)S(1)} fusion(bf16[256,896]{1,0:T(8,128)(2,1)} %param.9, bf16[896,64]{0,1:T(8,128)(2,1)} %param.16), kind=kOutput, calls=%fused_computation.8 | convolution fusion | flops 29360128 | bytes 638976 | tf_op jit(solution)/shard_map/dot_general | solution.py:14
  10.5 1.2 %convolution_bitcast_fusion.2 = f32[64,256]{1,0:T(8,128)S(1)} fusion(bf16[256,896]{1,0:T(8,128)(2,1)S(1)} %copy-done, bf16[896,64]{0,1:T(8,128)(2,1)} %param.15), kind=kOutput, calls=%fused_computation.9 | convolution fusion | flops 29360128 | bytes 638976 | tf_op jit(solution)/shard_map/dot_general | solution.py:14
  11.7 1.3 %convolution_bitcast_fusion.3 = f32[64,256]{1,0:T(8,128)S(1)} fusion(bf16[256,896]{1,0:T(8,128)(2,1)} %param.10, bf16[896,64]{0,1:T(8,128)(2,1)} %param.15), kind=kOutput, calls=%fused_computation.10 | convolution fusion | flops 29360128 | bytes 638976 | tf_op jit(solution)/shard_map/dot_general | solution.py:14
  13.1 1.9 %fusion.45 = (bf16[32,4096]{1,0:T(8,128)(2,1)}, bf16[32,4096]{1,0:T(8,128)(2,1)}) fusion(bf16[64,4096]{1,0:T(8,128)(2,1)} %param.17), kind=kLoop, calls=%fused_computation.124 | loop fusion | bytes 1048576 | tf_op jit(solution)/shard_map/slice | solution.py:164
  15.5 0.6 iota_add_fusion.2
  16.1 0.7 pad_add_fusion
  16.9 1.6 %collective-permute-start.1 = (f32[256,256]{1,0:T(8,128)S(1)}, f32[256,256]{1,0:T(8,128)S(1)}, u32[]{:S(2)}, u32[]{:S(2)}) collective-permute-start(f32[256,256]{1,0:T(8,128)S(1)} %fusion.44), channel_id=1, source_target_pairs={{0,2},{1,3},{2,0},{3,1},{4,6},{5,7},{6,4},{7,5},{8,10},{9,11},{10,... | collective-permute-start | bytes 786440 | tf_op jit(solution)/shard_map/ppermute | solution.py:58
  19.1 0.5 collective-permute-start.14
  19.6 6.0 %collective-permute-done.1 = f32[256,256]{1,0:T(8,128)S(1)} collective-permute-done((f32[256,256]{1,0:T(8,128)S(1)}, f32[256,256]{1,0:T(8,128)S(1)}, u32[]{:S(2)}, u32[]{:S(2)}) %collective-permute-start.1) | collective-permute-done | bytes 262176 | tf_op jit(solution)/shard_map/ppermute | solution.py:58
  26.1 0.6 collective-permute-start.6
  26.7 1.6 %collective-permute-start.10 = (f32[256,128]{0,1:T(8,128)S(1)}, f32[256,128]{0,1:T(8,128)S(1)}, u32[]{:S(2)}, u32[]{:S(2)}) collective-permute-start(f32[256,128]{0,1:T(8,128)S(1)} %constant_dynamic-slice_fusion.4), channel_id=1, source_target_pairs={{0,2},{1,3},{2,0},{3,1},{4,6},{5,7},{6,4},{7,5},{8,10},{9,11},{10,... | collective-permute-start | bytes 393224 | tf_op jit(solution)/shard_map/ppermute | solution.py:58
  28.3 1.6 %collective-permute-start.15 = (bf16[256,896]{1,0:T(8,128)(2,1)S(1)}, bf16[256,896]{1,0:T(8,128)(2,1)S(1)}, u32[]{:S(2)}, u32[]{:S(2)}) collective-permute-start(bf16[256,896]{1,0:T(8,128)(2,1)S(1)} %collective-permute-done.2), channel_id=1, source_target_pairs={{0,4},{4,0},{8,12},{12,8},{16,20},{20,16},{24,28},{28,24},{1,5},{5... | collective-permute-start | bytes 1376264 | tf_op jit(solution)/shard_map/ppermute | solution.py:55
  31.8 0.9 %collective-permute-done.7 = f32[128,512]{0,1:T(8,128)S(1)} collective-permute-done((f32[128,512]{0,1:T(8,128)S(1)}, f32[128,512]{0,1:T(8,128)S(1)}, u32[]{:S(2)}, u32[]{:S(2)}) %collective-permute-start.7) | collective-permute-done | bytes 262176 | tf_op jit(solution)/shard_map/ppermute | solution.py:58
  34.2 1.6 %collective-permute-start.12 = (f32[256,128]{0,1:T(8,128)S(1)}, f32[256,128]{0,1:T(8,128)S(1)}, u32[]{:S(2)}, u32[]{:S(2)}) collective-permute-start(f32[256,128]{0,1:T(8,128)S(1)} %constant_dynamic-slice_fusion.3), channel_id=1, source_target_pairs={{0,2},{1,3},{2,0},{3,1},{4,6},{5,7},{6,4},{7,5},{8,10},{9,11},{10,... | collective-permute-start | bytes 393224 | tf_op jit(solution)/shard_map/ppermute | solution.py:58
  35.9 2.8 %collective-permute-start.29 = (bf16[64,4096]{1,0:T(8,128)(2,1)}, bf16[64,4096]{1,0:T(8,128)(2,1)}, u32[]{:S(2)}, u32[]{:S(2)}) collective-permute-start(bf16[64,4096]{1,0:T(8,128)(2,1)} %param.17), channel_id=1, source_target_pairs={{0,16},{4,20},{8,24},{12,28},{16,0},{20,4},{24,8},{28,12},{1,17},{... | collective-permute-start | bytes 1572872 | tf_op jit(solution)/shard_map/ppermute | solution.py:55
  38.9 1.1 %constant_dynamic-update-slice_fusion.2 = bf16[256,4096]{1,0:T(8,128)(2,1)S(1)} fusion(bf16[256,4096]{1,0:T(8,128)(2,1)S(1)} %broadcast_in_dim.11, bf16[64,4096]{1,0:T(8,128)(2,1)} %param.17, s32[]{:T(128)S(6)} %select_n.99), kind=kLoop, calls=%fused_computation.88 | loop fusion | bytes 1048580 | tf_op jit(solution)/shard_map/dynamic_update_slice | solution.py:231
  40.1 1.3 %collective-permute-start.13 = (f32[128,256]{0,1:T(8,128)S(1)}, f32[128,256]{0,1:T(8,128)S(1)}, u32[]{:S(2)}, u32[]{:S(2)}) collective-permute-start(f32[128,256]{0,1:T(8,128)S(1)} %constant_dynamic-slice_fusion.2), channel_id=1, source_target_pairs={{0,2},{1,3},{2,0},{3,1},{4,6},{5,7},{6,4},{7,5},{8,10},{9,11},{10,... | collective-permute-start | bytes 393224 | tf_op jit(solution)/shard_map/ppermute | solution.py:58
  42.0 3.1 %collective-permute-done.13 = f32[128,256]{0,1:T(8,128)S(1)} collective-permute-done((f32[128,256]{0,1:T(8,128)S(1)}, f32[128,256]{0,1:T(8,128)S(1)}, u32[]{:S(2)}, u32[]{:S(2)}) %collective-permute-start.13) | collective-permute-done | bytes 131104 | tf_op jit(solution)/shard_map/ppermute | solution.py:58
  46.0 1.3 %collective-permute-start.17 = (f32[128,256]{0,1:T(8,128)S(1)}, f32[128,256]{0,1:T(8,128)S(1)}, u32[]{:S(2)}, u32[]{:S(2)}) collective-permute-start(f32[128,256]{0,1:T(8,128)S(1)} %constant_dynamic-slice_fusion.1), channel_id=1, source_target_pairs={{0,2},{1,3},{2,0},{3,1},{4,6},{5,7},{6,4},{7,5},{8,10},{9,11},{10,... | collective-permute-start | bytes 393224 | tf_op jit(solution)/shard_map/ppermute | solution.py:58
  47.4 3.6 %collective-permute-done.17 = f32[128,256]{0,1:T(8,128)S(1)} collective-permute-done((f32[128,256]{0,1:T(8,128)S(1)}, f32[128,256]{0,1:T(8,128)S(1)}, u32[]{:S(2)}, u32[]{:S(2)}) %collective-permute-start.17) | collective-permute-done | bytes 131104 | tf_op jit(solution)/shard_map/ppermute | solution.py:58
  51.6 1.1 %collective-permute-done.18 = f32[2,256]{1,0:T(2,128)S(1)} collective-permute-done((f32[2,256]{1,0:T(2,128)S(1)}, f32[2,256]{1,0:T(2,128)S(1)}, u32[]{:S(2)}, u32[]{:S(2)}) %collective-permute-start.18) | collective-permute-done | bytes 2080 | tf_op jit(solution)/shard_map/ppermute | solution.py:58
  52.8 1.6 %collective-permute-start.20 = (f32[2,256]{1,0:T(2,128)S(1)}, f32[2,256]{1,0:T(2,128)S(1)}, u32[]{:S(2)}, u32[]{:S(2)}) collective-permute-start(f32[2,256]{1,0:T(2,128)S(1)} %fusion.34), channel_id=1, source_target_pairs={{0,8},{4,12},{8,0},{12,4},{16,24},{20,28},{24,16},{28,20},{1,9},{5... | collective-permute-start | bytes 6152 | tf_op jit(solution)/shard_map/ppermute | solution.py:55
  54.4 2.2 %collective-permute-done.20 = f32[2,256]{1,0:T(2,128)S(1)} collective-permute-done((f32[2,256]{1,0:T(2,128)S(1)}, f32[2,256]{1,0:T(2,128)S(1)}, u32[]{:S(2)}, u32[]{:S(2)}) %collective-permute-start.20) | collective-permute-done | bytes 2080 | tf_op jit(solution)/shard_map/ppermute | solution.py:55
  57.3 1.7 %collective-permute-start.24 = (f32[64,256]{1,0:T(8,128)S(1)}, f32[64,256]{1,0:T(8,128)S(1)}, u32[]{:S(2)}, u32[]{:S(2)}) collective-permute-start(f32[64,256]{1,0:T(8,128)S(1)} %slice.202), channel_id=1, source_target_pairs={{0,4},{4,0},{8,12},{12,8},{16,20},{20,16},{24,28},{28,24},{1,5},{5... | collective-permute-start | bytes 196616 | tf_op jit(solution)/shard_map/ppermute | solution.py:55
  59.1 1.4 %collective-permute-start.22 = (f32[64,256]{1,0:T(8,128)S(1)}, f32[64,256]{1,0:T(8,128)S(1)}, u32[]{:S(2)}, u32[]{:S(2)}) collective-permute-start(f32[64,256]{1,0:T(8,128)S(1)} %pad_maximum_fusion.13), channel_id=1, source_target_pairs={{0,8},{4,12},{8,0},{12,4},{16,24},{20,28},{24,16},{28,20},{1,9},{5... | collective-permute-start | bytes 196616 | tf_op jit(solution)/shard_map/ppermute | solution.py:55
  60.6 1.4 %collective-permute-done.24 = f32[64,256]{1,0:T(8,128)S(1)} collective-permute-done((f32[64,256]{1,0:T(8,128)S(1)}, f32[64,256]{1,0:T(8,128)S(1)}, u32[]{:S(2)}, u32[]{:S(2)}) %collective-permute-start.24) | collective-permute-done | bytes 65568 | tf_op jit(solution)/shard_map/ppermute | solution.py:55
  62.2 1.5 %collective-permute-start.30 = (bf16[64,4096]{1,0:T(8,128)(2,1)}, bf16[64,4096]{1,0:T(8,128)(2,1)S(1)}, u32[]{:S(2)}, u32[]{:S(2)}) collective-permute-start(bf16[64,4096]{1,0:T(8,128)(2,1)} %collective-permute-done.29), channel_id=1, source_target_pairs={{0,4},{4,0},{8,12},{12,8},{16,20},{20,16},{24,28},{28,24},{1,5},{5... | collective-permute-start | bytes 1572872 | tf_op jit(solution)/shard_map/ppermute | solution.py:55
  63.7 1.1 %constant_dynamic-update-slice_fusion.1 = bf16[256,4096]{1,0:T(8,128)(2,1)S(1)} fusion(bf16[256,4096]{1,0:T(8,128)(2,1)S(1)} %constant_dynamic-update-slice_fusion.2, bf16[64,4096]{1,0:T(8,128)(2,1)} %collective-permute-done.29, s32[]{:T(128)S(6)} %select_n.100), kind=kLoop, calls=%fused_computation.87 | loop fusion | bytes 1048580 | tf_op jit(solution)/shard_map/dynamic_update_slice | solution.py:231
  64.9 1.0 %maximum_dynamic-update-slice_fusion = bf16[256,4096]{1,0:T(8,128)(2,1)S(1)} fusion(bf16[256,4096]{1,0:T(8,128)(2,1)S(1)} %constant_dynamic-update-slice_fusion.1, s32[]{:T(128)S(6)} %select_n.101, bf16[32,4096]{1,0:T(8,128)(2,1)} %collective-permute-done.19, bf16[32,4096]{1,0:T(8,128)(2,1)S(1)} %copy-done.5), kind=kLoop, calls=%fused_computation.18 | loop fusion | flops 1048576 | bytes 1048580 | tf_op jit(solution)/shard_map/dynamic_update_slice | solution.py:231
  65.8 1.0 %collective-permute-done.25 = f32[64,128]{1,0:T(8,128)S(1)} collective-permute-done((f32[64,128]{1,0:T(8,128)S(1)}, f32[64,128]{1,0:T(8,128)S(1)}, u32[]{:S(2)}, u32[]{:S(2)}) %collective-permute-start.25) | collective-permute-done | bytes 32800 | tf_op jit(solution)/shard_map/ppermute | solution.py:55
  66.8 1.7 %collective-permute-start.26 = (f32[64,128]{1,0:T(8,128)S(1)}, f32[64,128]{1,0:T(8,128)S(1)}, u32[]{:S(2)}, u32[]{:S(2)}) collective-permute-start(f32[64,128]{1,0:T(8,128)S(1)} %slice_add_fusion.3), channel_id=1, source_target_pairs={{0,2},{1,3},{2,0},{3,1},{4,6},{5,7},{6,4},{7,5},{8,10},{9,11},{10,... | collective-permute-start | bytes 98312 | tf_op jit(solution)/shard_map/ppermute | solution.py:58
  68.6 2.1 %collective-permute-done.26 = f32[64,128]{1,0:T(8,128)S(1)} collective-permute-done((f32[64,128]{1,0:T(8,128)S(1)}, f32[64,128]{1,0:T(8,128)S(1)}, u32[]{:S(2)}, u32[]{:S(2)}) %collective-permute-start.26) | collective-permute-done | bytes 32800 | tf_op jit(solution)/shard_map/ppermute | solution.py:58
  70.7 1.4 %collective-permute-start.27 = (f32[64,128]{1,0:T(8,128)S(1)}, f32[64,128]{1,0:T(8,128)S(1)}, u32[]{:S(2)}, u32[]{:S(2)}) collective-permute-start(f32[64,128]{1,0:T(8,128)S(1)} %add.238), channel_id=1, source_target_pairs={{0,8},{4,12},{8,0},{12,4},{16,24},{20,28},{24,16},{28,20},{1,9},{5... | collective-permute-start | bytes 98312 | tf_op jit(solution)/shard_map/ppermute | solution.py:55
  72.2 0.6 collective-permute-start.23
  72.7 1.9 %collective-permute-done.27 = f32[64,128]{1,0:T(8,128)S(1)} collective-permute-done((f32[64,128]{1,0:T(8,128)S(1)}, f32[64,128]{1,0:T(8,128)S(1)}, u32[]{:S(2)}, u32[]{:S(2)}) %collective-permute-start.27) | collective-permute-done | bytes 32800 | tf_op jit(solution)/shard_map/ppermute | solution.py:55
  74.7 1.8 %collective-permute-done.23 = f32[128,128]{1,0:T(8,128)S(1)} collective-permute-done((f32[128,128]{1,0:T(8,128)S(1)}, f32[128,128]{1,0:T(8,128)S(1)}, u32[]{:S(2)}, u32[]{:S(2)}) %collective-permute-start.23) | collective-permute-done | bytes 65568 | tf_op jit(solution)/shard_map/ppermute | solution.py:58
  76.5 0.7 add_convert_fusion
  77.2 0.8 add_convert_fusion.1
  78.1 0.8 convolution_convert_fusion
  78.9 0.9 %collective-permute-start.31 = (bf16[256,256]{1,0:T(8,128)(2,1)S(1)}, bf16[256,256]{1,0:T(8,128)(2,1)S(1)}, u32[]{:S(2)}, u32[]{:S(2)}) collective-permute-start(bf16[256,256]{1,0:T(8,128)(2,1)S(1)} %convolution_convert_fusion), channel_id=1, source_target_pairs={{0,8},{4,12},{8,0},{12,4},{16,24},{20,28},{24,16},{28,20},{1,9},{5... | collective-permute-start | bytes 393224 | tf_op jit(solution)/shard_map/ppermute | solution.py:55
  79.8 0.8 fusion.54
  80.6 3.3 %collective-permute-done.31 = bf16[256,256]{1,0:T(8,128)(2,1)S(1)} collective-permute-done((bf16[256,256]{1,0:T(8,128)(2,1)S(1)}, bf16[256,256]{1,0:T(8,128)(2,1)S(1)}, u32[]{:S(2)}, u32[]{:S(2)}) %collective-permute-start.31) | collective-permute-done | bytes 131104 | tf_op jit(solution)/shard_map/ppermute | solution.py:55
  84.0 0.8 pad_maximum_fusion.1
  (119 shorter events, 8.6 us)
Async XLA Ops:
  0.0 10.5 %copy-start = (bf16[256,896]{1,0:T(8,128)(2,1)S(1)}, bf16[256,896]{1,0:T(8,128)(2,1)}, u32[]{:S(2)}) copy-start(bf16[256,896]{1,0:T(8,128)(2,1)} %param.12) | copy-start | bytes 1376260
  0.0 28.3 %collective-permute-start.2 = (bf16[256,896]{1,0:T(8,128)(2,1)}, bf16[256,896]{1,0:T(8,128)(2,1)S(1)}, u32[]{:S(2)}, u32[]{:S(2)}) collective-permute-start(bf16[256,896]{1,0:T(8,128)(2,1)} %param.11), channel_id=1, source_target_pairs={{0,16},{4,20},{8,24},{12,28},{16,0},{20,4},{24,8},{28,12},{1,17},{... | collective-permute-start | bytes 1376264 | tf_op jit(solution)/shard_map/ppermute | solution.py:55
  4.7 11.3 %copy-start.6 = (s32[256]{0:T(256)S(1)}, s32[256]{0:T(256)}, u32[]{:S(2)}) copy-start(s32[256]{0:T(256)} %param.14) | copy-start | bytes 3076
  4.7 12.1 %copy-start.2 = (bf16[256,896]{1,0:T(8,128)(2,1)S(1)}, bf16[256,896]{1,0:T(8,128)(2,1)}, u32[]{:S(2)}) copy-start(bf16[256,896]{1,0:T(8,128)(2,1)} %param.11) | copy-start | bytes 1376260
  4.7 13.7 %collective-permute-start.4 = (bf16[256,896]{1,0:T(8,128)(2,1)}, bf16[256,896]{1,0:T(8,128)(2,1)S(1)}, u32[]{:S(2)}, u32[]{:S(2)}) collective-permute-start(bf16[256,896]{1,0:T(8,128)(2,1)} %param.11), channel_id=1, source_target_pairs={{0,4},{4,0},{8,12},{12,8},{16,20},{20,16},{24,28},{28,24},{1,5},{5... | collective-permute-start | bytes 1376264 | tf_op jit(solution)/shard_map/ppermute | solution.py:55
  6.2 23.6 %collective-permute-start.3 = (bf16[256,896]{1,0:T(8,128)(2,1)}, bf16[256,896]{1,0:T(8,128)(2,1)S(1)}, u32[]{:S(2)}, u32[]{:S(2)}) collective-permute-start(bf16[256,896]{1,0:T(8,128)(2,1)} %param.9), channel_id=1, source_target_pairs={{0,8},{4,12},{8,0},{12,4},{16,24},{20,28},{24,16},{28,20},{1,9},{5... | collective-permute-start | bytes 1376264 | tf_op jit(solution)/shard_map/ppermute | solution.py:55
  13.0 5.5 %copy-start.1 = (bf16[256,896]{1,0:T(8,128)(2,1)S(1)}, bf16[256,896]{1,0:T(8,128)(2,1)}, u32[]{:S(2)}) copy-start(bf16[256,896]{1,0:T(8,128)(2,1)} %param.9) | copy-start | bytes 1376260
  13.0 3.8 %collective-permute-start = (f32[256,256]{1,0:T(8,128)S(1)}, f32[256,256]{1,0:T(8,128)S(1)}, u32[]{:S(2)}, u32[]{:S(2)}) collective-permute-start(f32[256,256]{1,0:T(8,128)S(1)} %pad_maximum_fusion.8), channel_id=1, source_target_pairs={{0,1},{1,0},{2,3},{3,2},{4,5},{5,4},{6,7},{7,6},{8,9},{9,8},{10,11... | collective-permute-start | bytes 786440 | tf_op jit(solution)/shard_map/ppermute | solution.py:58
  16.1 3.0 %copy-start.3 = (bf16[32,4096]{1,0:T(8,128)(2,1)S(1)}, bf16[32,4096]{1,0:T(8,128)(2,1)}, u32[]{:S(2)}) copy-start(bf16[32,4096]{1,0:T(8,128)(2,1)} %get-tuple-element.28) | copy-start | bytes 786436
  16.9 8.7 %collective-permute-start.1 = (f32[256,256]{1,0:T(8,128)S(1)}, f32[256,256]{1,0:T(8,128)S(1)}, u32[]{:S(2)}, u32[]{:S(2)}) collective-permute-start(f32[256,256]{1,0:T(8,128)S(1)} %fusion.44), channel_id=1, source_target_pairs={{0,2},{1,3},{2,0},{3,1},{4,6},{5,7},{6,4},{7,5},{8,10},{9,11},{10,... | collective-permute-start | bytes 786440 | tf_op jit(solution)/shard_map/ppermute | solution.py:58
  18.8 6.9 %collective-permute-start.5 = (f32[256,256]{0,1:T(8,128)S(1)}, f32[256,256]{0,1:T(8,128)S(1)}, u32[]{:S(2)}, u32[]{:S(2)}) collective-permute-start(f32[256,256]{0,1:T(8,128)S(1)} %fusion.5), channel_id=1, source_target_pairs={{0,1},{1,0},{2,3},{3,2},{4,5},{5,4},{6,7},{7,6},{8,9},{9,8},{10,11... | collective-permute-start | bytes 786440 | tf_op jit(solution)/shard_map/ppermute | solution.py:58
  19.1 9.2 %collective-permute-start.14 = (bf16[32,4096]{1,0:T(8,128)(2,1)S(1)}, bf16[32,4096]{1,0:T(8,128)(2,1)S(1)}, u32[]{:S(2)}, u32[]{:S(2)}) collective-permute-start(bf16[32,4096]{1,0:T(8,128)(2,1)S(1)} %copy-done.3), channel_id=1, source_target_pairs={{0,4},{4,0},{8,12},{12,8},{16,20},{20,16},{24,28},{28,24},{1,5},{5... | collective-permute-start | bytes 786440 | tf_op jit(solution)/shard_map/ppermute | solution.py:55
  26.1 4.1 %collective-permute-start.6 = (f32[64,128]{1,0:T(8,128)S(1)}, f32[64,128]{1,0:T(8,128)S(1)}, u32[]{:S(2)}, u32[]{:S(2)}) collective-permute-start(f32[64,128]{1,0:T(8,128)S(1)} %constant_dynamic-slice_fusion.5), channel_id=1, source_target_pairs={{0,4},{4,0},{8,12},{12,8},{16,20},{20,16},{24,28},{28,24},{1,5},{5... | collective-permute-start | bytes 98312 | tf_op jit(solution)/shard_map/ppermute | solution.py:55
  26.7 5.0 %collective-permute-start.10 = (f32[256,128]{0,1:T(8,128)S(1)}, f32[256,128]{0,1:T(8,128)S(1)}, u32[]{:S(2)}, u32[]{:S(2)}) collective-permute-start(f32[256,128]{0,1:T(8,128)S(1)} %constant_dynamic-slice_fusion.4), channel_id=1, source_target_pairs={{0,2},{1,3},{2,0},{3,1},{4,6},{5,7},{6,4},{7,5},{8,10},{9,11},{10,... | collective-permute-start | bytes 393224 | tf_op jit(solution)/shard_map/ppermute | solution.py:58
  28.3 2.8 %copy-start.4 = (bf16[32,4096]{1,0:T(8,128)(2,1)}, bf16[32,4096]{1,0:T(8,128)(2,1)S(1)}, u32[]{:S(2)}) copy-start(bf16[32,4096]{1,0:T(8,128)(2,1)S(1)} %collective-permute-done.14) | copy-start | bytes 786436
  28.3 13.2 %collective-permute-start.15 = (bf16[256,896]{1,0:T(8,128)(2,1)S(1)}, bf16[256,896]{1,0:T(8,128)(2,1)S(1)}, u32[]{:S(2)}, u32[]{:S(2)}) collective-permute-start(bf16[256,896]{1,0:T(8,128)(2,1)S(1)} %collective-permute-done.2), channel_id=1, source_target_pairs={{0,4},{4,0},{8,12},{12,8},{16,20},{20,16},{24,28},{28,24},{1,5},{5... | collective-permute-start | bytes 1376264 | tf_op jit(solution)/shard_map/ppermute | solution.py:55
  31.0 1.6 %collective-permute-start.7 = (f32[128,512]{0,1:T(8,128)S(1)}, f32[128,512]{0,1:T(8,128)S(1)}, u32[]{:S(2)}, u32[]{:S(2)}) collective-permute-start(f32[128,512]{0,1:T(8,128)S(1)} %fusion.9), channel_id=1, source_target_pairs={{0,1},{1,0},{2,3},{3,2},{4,5},{5,4},{6,7},{7,6},{8,9},{9,8},{10,11... | collective-permute-start | bytes 786440 | tf_op jit(solution)/shard_map/ppermute | solution.py:58
  31.1 2.7 %collective-permute-start.11 = (f32[256,256]{0,1:T(8,128)S(1)}, f32[256,256]{0,1:T(8,128)S(1)}, u32[]{:S(2)}, u32[]{:S(2)}) collective-permute-start(f32[256,256]{0,1:T(8,128)S(1)} %fusion.4), channel_id=1, source_target_pairs={{0,1},{1,0},{2,3},{3,2},{4,5},{5,4},{6,7},{7,6},{8,9},{9,8},{10,11... | collective-permute-start | bytes 786440 | tf_op jit(solution)/shard_map/ppermute | solution.py:58
  33.0 7.0 %collective-permute-start.9 = (f32[64,256]{1,0:T(8,128)S(1)}, f32[64,256]{1,0:T(8,128)S(1)}, u32[]{:S(2)}, u32[]{:S(2)}) collective-permute-start(f32[64,256]{1,0:T(8,128)S(1)} %pad_maximum_fusion.12), channel_id=1, source_target_pairs={{0,16},{4,20},{8,24},{12,28},{16,0},{20,4},{24,8},{28,12},{1,17},{... | collective-permute-start | bytes 196616 | tf_op jit(solution)/shard_map/ppermute | solution.py:55
  33.4 13.9 %collective-permute-start.8 = (f32[200,256]{1,0:T(8,128)S(1)}, f32[200,256]{1,0:T(8,128)S(1)}, u32[]{:S(2)}, u32[]{:S(2)}) collective-permute-start(f32[200,256]{1,0:T(8,128)S(1)} %pad_maximum_fusion.9), channel_id=1, source_target_pairs={{0,8},{4,12},{8,0},{12,4},{16,24},{20,28},{24,16},{28,20},{1,9},{5... | collective-permute-start | bytes 614408 | tf_op jit(solution)/shard_map/ppermute | solution.py:55
  34.2 7.2 %collective-permute-start.12 = (f32[256,128]{0,1:T(8,128)S(1)}, f32[256,128]{0,1:T(8,128)S(1)}, u32[]{:S(2)}, u32[]{:S(2)}) collective-permute-start(f32[256,128]{0,1:T(8,128)S(1)} %constant_dynamic-slice_fusion.3), channel_id=1, source_target_pairs={{0,2},{1,3},{2,0},{3,1},{4,6},{5,7},{6,4},{7,5},{8,10},{9,11},{10,... | collective-permute-start | bytes 393224 | tf_op jit(solution)/shard_map/ppermute | solution.py:58
  35.9 26.3 %collective-permute-start.29 = (bf16[64,4096]{1,0:T(8,128)(2,1)}, bf16[64,4096]{1,0:T(8,128)(2,1)}, u32[]{:S(2)}, u32[]{:S(2)}) collective-permute-start(bf16[64,4096]{1,0:T(8,128)(2,1)} %param.17), channel_id=1, source_target_pairs={{0,16},{4,20},{8,24},{12,28},{16,0},{20,4},{24,8},{28,12},{1,17},{... | collective-permute-start | bytes 1572872 | tf_op jit(solution)/shard_map/ppermute | solution.py:55
  40.1 5.0 %collective-permute-start.13 = (f32[128,256]{0,1:T(8,128)S(1)}, f32[128,256]{0,1:T(8,128)S(1)}, u32[]{:S(2)}, u32[]{:S(2)}) collective-permute-start(f32[128,256]{0,1:T(8,128)S(1)} %constant_dynamic-slice_fusion.2), channel_id=1, source_target_pairs={{0,2},{1,3},{2,0},{3,1},{4,6},{5,7},{6,4},{7,5},{8,10},{9,11},{10,... | collective-permute-start | bytes 393224 | tf_op jit(solution)/shard_map/ppermute | solution.py:58
  41.9 3.7 %collective-permute-start.16 = (f32[128,512]{0,1:T(8,128)S(1)}, f32[128,512]{0,1:T(8,128)S(1)}, u32[]{:S(2)}, u32[]{:S(2)}) collective-permute-start(f32[128,512]{0,1:T(8,128)S(1)} %fusion.6), channel_id=1, source_target_pairs={{0,1},{1,0},{2,3},{3,2},{4,5},{5,4},{6,7},{7,6},{8,9},{9,8},{10,11... | collective-permute-start | bytes 786440 | tf_op jit(solution)/shard_map/ppermute | solution.py:58
  45.1 7.6 %collective-permute-start.19 = (bf16[32,4096]{1,0:T(8,128)(2,1)}, bf16[32,4096]{1,0:T(8,128)(2,1)}, u32[]{:S(2)}, u32[]{:S(2)}) collective-permute-start(bf16[32,4096]{1,0:T(8,128)(2,1)} %get-tuple-element.31), channel_id=1, source_target_pairs={{0,4},{4,0},{8,12},{12,8},{16,20},{20,16},{24,28},{28,24},{1,5},{5... | collective-permute-start | bytes 786440 | tf_op jit(solution)/shard_map/ppermute | solution.py:55
  46.0 5.0 %collective-permute-start.17 = (f32[128,256]{0,1:T(8,128)S(1)}, f32[128,256]{0,1:T(8,128)S(1)}, u32[]{:S(2)}, u32[]{:S(2)}) collective-permute-start(f32[128,256]{0,1:T(8,128)S(1)} %constant_dynamic-slice_fusion.1), channel_id=1, source_target_pairs={{0,2},{1,3},{2,0},{3,1},{4,6},{5,7},{6,4},{7,5},{8,10},{9,11},{10,... | collective-permute-start | bytes 393224 | tf_op jit(solution)/shard_map/ppermute | solution.py:58
  51.5 1.2 %collective-permute-start.18 = (f32[2,256]{1,0:T(2,128)S(1)}, f32[2,256]{1,0:T(2,128)S(1)}, u32[]{:S(2)}, u32[]{:S(2)}) collective-permute-start(f32[2,256]{1,0:T(2,128)S(1)} %pad_maximum_fusion.17), channel_id=1, source_target_pairs={{0,1},{1,0},{2,3},{3,2},{4,5},{5,4},{6,7},{7,6},{8,9},{9,8},{10,11... | collective-permute-start | bytes 6152 | tf_op jit(solution)/shard_map/ppermute | solution.py:58
  52.8 3.8 %collective-permute-start.20 = (f32[2,256]{1,0:T(2,128)S(1)}, f32[2,256]{1,0:T(2,128)S(1)}, u32[]{:S(2)}, u32[]{:S(2)}) collective-permute-start(f32[2,256]{1,0:T(2,128)S(1)} %fusion.34), channel_id=1, source_target_pairs={{0,8},{4,12},{8,0},{12,4},{16,24},{20,28},{24,16},{28,20},{1,9},{5... | collective-permute-start | bytes 6152 | tf_op jit(solution)/shard_map/ppermute | solution.py:55
  56.6 8.3 %copy-start.5 = (bf16[32,4096]{1,0:T(8,128)(2,1)S(1)}, bf16[32,4096]{1,0:T(8,128)(2,1)}, u32[]{:S(2)}) copy-start(bf16[32,4096]{1,0:T(8,128)(2,1)} %copy-done.4) | copy-start | bytes 786436
  57.0 2.0 %collective-permute-start.21 = (f32[64,256]{1,0:T(8,128)S(1)}, f32[64,256]{1,0:T(8,128)S(1)}, u32[]{:S(2)}, u32[]{:S(2)}) collective-permute-start(f32[64,256]{1,0:T(8,128)S(1)} %fusion.24), channel_id=1, source_target_pairs={{0,1},{1,0},{2,3},{3,2},{4,5},{5,4},{6,7},{7,6},{8,9},{9,8},{10,11... | collective-permute-start | bytes 196616 | tf_op jit(solution)/shard_map/ppermute | solution.py:58
  57.3 4.6 %collective-permute-start.24 = (f32[64,256]{1,0:T(8,128)S(1)}, f32[64,256]{1,0:T(8,128)S(1)}, u32[]{:S(2)}, u32[]{:S(2)}) collective-permute-start(f32[64,256]{1,0:T(8,128)S(1)} %slice.202), channel_id=1, source_target_pairs={{0,4},{4,0},{8,12},{12,8},{16,20},{20,16},{24,28},{28,24},{1,5},{5... | collective-permute-start | bytes 196616 | tf_op jit(solution)/shard_map/ppermute | solution.py:55
  59.1 9.5 %collective-permute-start.22 = (f32[64,256]{1,0:T(8,128)S(1)}, f32[64,256]{1,0:T(8,128)S(1)}, u32[]{:S(2)}, u32[]{:S(2)}) collective-permute-start(f32[64,256]{1,0:T(8,128)S(1)} %pad_maximum_fusion.13), channel_id=1, source_target_pairs={{0,8},{4,12},{8,0},{12,4},{16,24},{20,28},{24,16},{28,20},{1,9},{5... | collective-permute-start | bytes 196616 | tf_op jit(solution)/shard_map/ppermute | solution.py:55
  61.9 4.9 %collective-permute-start.25 = (f32[64,128]{1,0:T(8,128)S(1)}, f32[64,128]{1,0:T(8,128)S(1)}, u32[]{:S(2)}, u32[]{:S(2)}) collective-permute-start(f32[64,128]{1,0:T(8,128)S(1)} %slice.204), channel_id=1, source_target_pairs={{0,16},{4,20},{8,24},{12,28},{16,0},{20,4},{24,8},{28,12},{1,17},{... | collective-permute-start | bytes 98312 | tf_op jit(solution)/shard_map/ppermute | solution.py:55
  62.2 15.8 %collective-permute-start.30 = (bf16[64,4096]{1,0:T(8,128)(2,1)}, bf16[64,4096]{1,0:T(8,128)(2,1)S(1)}, u32[]{:S(2)}, u32[]{:S(2)}) collective-permute-start(bf16[64,4096]{1,0:T(8,128)(2,1)} %collective-permute-done.29), channel_id=1, source_target_pairs={{0,4},{4,0},{8,12},{12,8},{16,20},{20,16},{24,28},{28,24},{1,5},{5... | collective-permute-start | bytes 1572872 | tf_op jit(solution)/shard_map/ppermute | solution.py:55
  66.8 3.9 %collective-permute-start.26 = (f32[64,128]{1,0:T(8,128)S(1)}, f32[64,128]{1,0:T(8,128)S(1)}, u32[]{:S(2)}, u32[]{:S(2)}) collective-permute-start(f32[64,128]{1,0:T(8,128)S(1)} %slice_add_fusion.3), channel_id=1, source_target_pairs={{0,2},{1,3},{2,0},{3,1},{4,6},{5,7},{6,4},{7,5},{8,10},{9,11},{10,... | collective-permute-start | bytes 98312 | tf_op jit(solution)/shard_map/ppermute | solution.py:58
  70.7 3.9 %collective-permute-start.27 = (f32[64,128]{1,0:T(8,128)S(1)}, f32[64,128]{1,0:T(8,128)S(1)}, u32[]{:S(2)}, u32[]{:S(2)}) collective-permute-start(f32[64,128]{1,0:T(8,128)S(1)} %add.238), channel_id=1, source_target_pairs={{0,8},{4,12},{8,0},{12,4},{16,24},{20,28},{24,16},{28,20},{1,9},{5... | collective-permute-start | bytes 98312 | tf_op jit(solution)/shard_map/ppermute | solution.py:55
  72.2 4.3 %collective-permute-start.23 = (f32[128,128]{1,0:T(8,128)S(1)}, f32[128,128]{1,0:T(8,128)S(1)}, u32[]{:S(2)}, u32[]{:S(2)}) collective-permute-start(f32[128,128]{1,0:T(8,128)S(1)} %pad_maximum_fusion.14), channel_id=1, source_target_pairs={{0,2},{1,3},{2,0},{3,1},{4,6},{5,7},{6,4},{7,5},{8,10},{9,11},{10,... | collective-permute-start | bytes 196616 | tf_op jit(solution)/shard_map/ppermute | solution.py:58
  74.7 1.8 %collective-permute-start.28 = (f32[128,128]{1,0:T(8,128)S(1)}, f32[128,128]{1,0:T(8,128)S(1)}, u32[]{:S(2)}, u32[]{:S(2)}) collective-permute-start(f32[128,128]{1,0:T(8,128)S(1)} %pad_maximum_fusion.15), channel_id=1, source_target_pairs={{0,1},{1,0},{2,3},{3,2},{4,5},{5,4},{6,7},{7,6},{8,9},{9,8},{10,11... | collective-permute-start | bytes 196616 | tf_op jit(solution)/shard_map/ppermute | solution.py:58
  78.9 5.1 %collective-permute-start.31 = (bf16[256,256]{1,0:T(8,128)(2,1)S(1)}, bf16[256,256]{1,0:T(8,128)(2,1)S(1)}, u32[]{:S(2)}, u32[]{:S(2)}) collective-permute-start(bf16[256,256]{1,0:T(8,128)(2,1)S(1)} %convolution_convert_fusion), channel_id=1, source_target_pairs={{0,8},{4,12},{8,0},{12,4},{16,24},{20,28},{24,16},{28,20},{1,9},{5... | collective-permute-start | bytes 393224 | tf_op jit(solution)/shard_map/ppermute | solution.py:55

commit v4 on v3

--- a/solution.py
+++ b/solution.py
@@ -110,32 +110,36 @@
             bit //= 2
         return total
 
-    first = [halves, passage_y]
-    own_part = over_cores(first, query_out)
-    tests_y = over_train(after(test_grads[:32], passages[1]), 1)
-    small = lax.dynamic_slice_in_dim(after(factors, own_part)[3 * rank :], core * half, half, 1)
+    tests_cut = tests // 2
+    tests_y = over_train(test_grads[:tests_cut], 1)
+    tests_y1 = tests_y
+    small = lax.dynamic_slice_in_dim(after(factors, tests_y1)[3 * rank :], core * half, half, 1)
     small_y = over_train(small, 1)
+    pass_high = tuple(passages[m] for m in masks if m > 1 and not m & 1)
     for mask in masks:
         if mask & 1 and mask & ~1:
-            passages[mask] = over_train(after(passages[mask & ~1], own_part, tests_y), 1)
-
-    own_part = over_chips(own_part)
-    query_near = after(query_near, small_y)
+            passages[mask] = over_train(after(passages[mask & ~1], factors, tests_y1), 1)
+    pass_far = tuple(passages[m] for m in masks if m > 1 and m & 1)
+    early = [0, 1] + [m for m in masks if m > 1 and not m & 1]
+    first = [halves, passage_y] + [passages[m].reshape(2, half, feats) for m in early[2:]]
+    own_core = own_part = over_cores(first, after(query_out, factors, tests_y1))
+
+    own_part = over_chips(after(own_part, factors))
     queries = jnp.stack((query_out, query_near)).reshape(2, segs, seg, feats)
     queries = queries.transpose(1, 0, 2, 3).reshape(2 * rows, feats)
-    near_part = over_chips(over_cores(first, query_near))
+    near_core = over_cores(first, query_near)
+    near_part = over_chips(near_core)
     top_part = jnp.concatenate((own_part, near_part), axis=1)
-    logits = {0: top_part[:half], 1: top_part[half:]}
+    logits = {m: top_part[i * half : (i + 1) * half] for i, m in enumerate(early)}
     for mask in masks:
-        if mask & ~1:
-            last_part = over_cores([passages[mask].reshape(2, half, feats)], queries)
-            if not mask & 1:
-                mid_part = last_part
+        if mask not in early:
+            block = passages[mask]
+            last_part = over_cores([block.reshape(2, half, feats)], queries)
             logits[mask] = over_chips(last_part)
     logits = jnp.concatenate([logits[mask] for mask in masks], axis=0) * scale
 
     pass_small = jnp.concatenate((small, small_y), axis=1)
-    pass_small = gather({0: after(pass_small, mid_part)}, high_bits)
+    pass_small = gather({0: after(pass_small, near_core)}, high_bits)
     pass_small = jnp.concatenate(
         [pass_small[m & ~1][:, (m & 1) * half : (m & 1) * half + half] for m in masks], axis=1
     )
@@ -148,7 +152,7 @@
         ),
         axis=0,
     )
-    shared_near = over_train(after(shared, mid_part), near)
+    shared_near = over_train(after(shared, near_core), near)
     mine_of = jnp.concatenate(
         [
             lax.dynamic_slice_in_dim(a[2 * rank :], seg_at * seg, seg, 1)
@@ -161,9 +165,8 @@
     def swap(a):
         return jnp.concatenate((a[:, seg:], a[:, :seg]), axis=1)
 
-    tests_y2 = over_train(after(test_grads[32:], *(passages[m] for m in masks if m & 1 and m > 1)), 1)
+    tests_y2 = over_train(after(test_grads[tests_cut:], *pass_far), 1)
     tests_y = jnp.concatenate((tests_y, tests_y2), axis=0)
-    logits = after(logits, pass_small, shared_near)
     top = jnp.max(logits, axis=0, keepdims=True)
     total = jnp.sum(jnp.exp(logits - top), axis=0, keepdims=True)
 
@@ -173,7 +176,7 @@
 
     top, total = merge(top, total, over_test(jnp.concatenate((top, total), axis=0), 1))
     top, total = merge(
-        top, total, over_train(after(swap(jnp.concatenate((top, total), axis=0)), tests_y2), near)
+        top, total, over_train(after(swap(jnp.concatenate((top, total), axis=0)), tests_y2, pass_small), near)
     )
     columns = jnp.concatenate(
         [
@@ -186,6 +189,8 @@
     prob = jnp.exp(logits - top) / total
     dlogit = (prob - (columns == wanted.astype(jnp.int32)).astype(F32)).astype(BF16)
 
+    dlogit = after(dlogit, tests_y2)
+
     out_query = dot(split_two(pass_small), dlogit, 1, 0)
     out_query = (out_query[:rank] + out_query[rank:]) * scale
     out_pass = dot(split_two(query_small), dlogit, 1, 1)
@@ -196,6 +201,7 @@
         out_pass = out_pass[:, :width] + over_train(out_pass[:, width:], bit)
         if bit == 1:
             out_pass_y = out_pass
+    out_pass_z = out_pass
     bit = 2
     while bit < n_test:
         out_pass = out_pass + over_test(out_pass, bit)
@@ -221,8 +227,8 @@
         )
         bit *= 2
 
-    held = gather({0: after(test_grads, mid_part)}, high_bits)
-    held = {m: after(a, out_pass_y) if m else a for m, a in held.items()}
+    held = gather({0: after(test_grads, near_core)}, high_bits)
+    held = {m: after(a, tests_y2, out_pass_y) if m else a for m, a in held.items()}
     held.update({m | 1: over_train(a, 1) if m else tests_y for m, a in held.items()})
     test_block = jnp.zeros((n_far * tests, test_grads.shape[1]), BF16)
     for mask in masks:
@@ -230,7 +236,7 @@
         at = lax.div(owner, 2 * near) * near + lax.rem(owner, near)
         test_block = lax.dynamic_update_slice_in_dim(test_block, held[mask], at * tests, 0)
 
-    def scores_of(acts, which):
+    def scores_of(acts, which, out_query):
         oq = out_query[which * rank : (which + 1) * rank]
         op = out_pass[which * rank : (which + 1) * rank]
         outer = (
@@ -240,8 +246,9 @@
         grads = outer.reshape(rank * rank, rows).astype(BF16)
         return dot(grads, test_block, 0, 1)
 
-    given = over_train(scores_of(shared_near, 1).astype(BF16), near).astype(F32)
-    mine = scores_of(shared, 0)
+    scores_near = scores_of(shared_near, 1, out_query).astype(BF16)
+    given = over_train(scores_near, near).astype(F32)
+    mine = scores_of(shared, 0, out_query)
     unit = near * tests
     mine = [mine[:, i : i + unit] for i in range(0, mine.shape[1], unit)]
     given = [given[:, i : i + unit] for i in range(0, given.shape[1], unit)]

time: 85.2 us -> 83.9 us (0.985)
  waiting for transfers between devices: 28.9 us -> 32.4 us
  local copies, waits for them, and re-layouts: 4.62 us -> 2.26 us
  other arithmetic: 6.95 us -> 5.87 us
    ppermute x17, waiting for transfers between devices: 10 us -> 22.9 us  [over_train(): return lax.ppermute(a, 'train', [(i, i ^ bit) for i in range(n_train)])]
    ppermute x15 -> x13, waiting for transfers between devices: 18.8 us -> 9.5 us  [over_test(): return lax.ppermute(a, 'test', [(i, i ^ bit) for i in range(n_test)])]
    dynamic_update_slice x3, local copies, waits for them, and re-layouts: 2.23 us -> 0.12 us  [local(): lax.dynamic_update_slice_in_dim(test_block, held[mask], at * tests, 0)]
    add x2, other arithmetic: 1.07 us -> 0.01 us  [local(): lax.broadcasted_iota(jnp.int32, (half, 1), 0)]
    slice x2, local copies, waits for them, and re-layouts: 1.89 us -> 0.84 us  [the longest x1 0.84 us: local(): tests_y2 = over_train(after(test_grads[tests_cut:], *pass_far), 1)]
    ppermute x15 -> x13, starting transfers between devices: 10.8 us -> 9.82 us  [over_test(): return lax.ppermute(a, 'test', [(i, i ^ bit) for i in range(n_test)])]
    dot_general x16 -> x14, matrix products: 10.1 us -> 9.52 us  [dot(): lax.dot_general(a, b, (((ca,), (cb,)), ((), ())), preferred_element_type=...]
  transfers between devices with their start and end apart: 32 -> 30, of which waited for: 14 -> 16; matrix products, arithmetic and copies ran while one was open for 23% -> 19% of each run, Pallas kernels for 0% -> 0%
where the time goes in v4:
time: 83.9 us; the launch traced here: 83.7 us
  starting transfers between devices  32.9 us (39%)
  waiting for transfers between devices  32.4 us (39%)
  matrix products  9.52 us (11%)
  other arithmetic  5.87 us (7%)
  local copies, waits for them, and re-layouts  2.26 us (3%)
    ppermute x17, starting transfers between devices, over_train(): return lax.ppermute(a, 'train', [(i, i ^ bit) for i in range(n_train)])  23.1 us
    ppermute x17, waiting for transfers between devices, over_train(): return lax.ppermute(a, 'train', [(i, i ^ bit) for i in range(n_train)])  22.9 us
    ppermute x13, starting transfers between devices, over_test(): return lax.ppermute(a, 'test', [(i, i ^ bit) for i in range(n_test)])  9.82 us
    dot_general x14, matrix products, dot(): lax.dot_general(a, b, (((ca,), (cb,)), ((), ())), preferred_element_type=...  9.52 us
    ppermute x13, waiting for transfers between devices, over_test(): return lax.ppermute(a, 'test', [(i, i ^ bit) for i in range(n_test)])  9.5 us
  transfers between devices with their start and end apart: 30, of which 16 were waited for; matrix products, arithmetic and copies ran while one was open for 19% of the time, Pallas kernels for 0%

profile of v4, /device:TPU:0, one launch (start us, length us, event | category | flops | bytes accessed | tf_op | source)
XLA Modules:
  0.0 83.7 jit_solution(7938901123343289885)
XLA Ops:
  0.0 4.1 %collective-permute-start.3 = (bf16[256,896]{1,0:T(8,128)(2,1)}, bf16[256,896]{1,0:T(8,128)(2,1)S(1)}, u32[]{:S(2)}, u32[]{:S(2)}) collective-permute-start(bf16[256,896]{1,0:T(8,128)(2,1)} %param.11), channel_id=1, source_target_pairs={{0,16},{4,20},{8,24},{12,28},{16,0},{20,4},{24,8},{28,12},{1,17},{... | collective-permute-start | bytes 1376264 | tf_op jit(solution)/shard_map/ppermute | solution.py:55
  4.1 0.7 convert_element_type.49
  4.8 1.5 %collective-permute-start.2 = (bf16[256,896]{1,0:T(8,128)(2,1)}, bf16[256,896]{1,0:T(8,128)(2,1)S(1)}, u32[]{:S(2)}, u32[]{:S(2)}) collective-permute-start(bf16[256,896]{1,0:T(8,128)(2,1)} %param.11), channel_id=1, source_target_pairs={{0,4},{4,0},{8,12},{12,8},{16,20},{20,16},{24,28},{28,24},{1,5},{5... | collective-permute-start | bytes 1376264 | tf_op jit(solution)/shard_map/ppermute | solution.py:55
  6.3 1.6 %collective-permute-start.4 = (bf16[256,896]{1,0:T(8,128)(2,1)}, bf16[256,896]{1,0:T(8,128)(2,1)S(1)}, u32[]{:S(2)}, u32[]{:S(2)}) collective-permute-start(bf16[256,896]{1,0:T(8,128)(2,1)} %param.9), channel_id=1, source_target_pairs={{0,8},{4,12},{8,0},{12,4},{16,24},{20,28},{24,16},{28,20},{1,9},{5... | collective-permute-start | bytes 1376264 | tf_op jit(solution)/shard_map/ppermute | solution.py:55
  7.9 1.3 %convolution_bitcast_fusion = f32[64,256]{1,0:T(8,128)S(1)} fusion(bf16[256,896]{1,0:T(8,128)(2,1)} %param.11, bf16[896,64]{0,1:T(8,128)(2,1)} %param.16), kind=kOutput, calls=%fused_computation.6 | convolution fusion | flops 29360128 | bytes 638976 | tf_op jit(solution)/shard_map/dot_general | solution.py:14
  9.2 1.3 %convolution_bitcast_fusion.1 = f32[64,256]{1,0:T(8,128)S(1)} fusion(bf16[256,896]{1,0:T(8,128)(2,1)} %param.9, bf16[896,64]{0,1:T(8,128)(2,1)} %param.16), kind=kOutput, calls=%fused_computation.7 | convolution fusion | flops 29360128 | bytes 638976 | tf_op jit(solution)/shard_map/dot_general | solution.py:14
  10.6 1.2 %convolution_bitcast_fusion.2 = f32[64,256]{1,0:T(8,128)S(1)} fusion(bf16[256,896]{1,0:T(8,128)(2,1)S(1)} %copy-done, bf16[896,64]{0,1:T(8,128)(2,1)} %param.15), kind=kOutput, calls=%fused_computation.8 | convolution fusion | flops 29360128 | bytes 638976 | tf_op jit(solution)/shard_map/dot_general | solution.py:14
  11.7 1.3 %convolution_bitcast_fusion.3 = f32[64,256]{1,0:T(8,128)S(1)} fusion(bf16[256,896]{1,0:T(8,128)(2,1)} %param.10, bf16[896,64]{0,1:T(8,128)(2,1)} %param.15), kind=kOutput, calls=%fused_computation.9 | convolution fusion | flops 29360128 | bytes 638976 | tf_op jit(solution)/shard_map/dot_general | solution.py:14
  13.1 0.7 pad_maximum_fusion.8
  13.8 0.8 %fusion.41 = (bf16[32,4096]{1,0:T(8,128)(2,1)}, bf16[32,4096]{1,0:T(8,128)(2,1)}) fusion(bf16[64,4096]{1,0:T(8,128)(2,1)S(1)} %copy-done.1), kind=kLoop, calls=%fused_computation.120 | loop fusion | bytes 1048576 | tf_op jit(solution)/shard_map/slice | solution.py:168
  15.1 0.8 dynamic-slice_bitcast_fusion.5
  16.1 1.6 %collective-permute-start.1 = (f32[256,256]{1,0:T(8,128)S(1)}, f32[256,256]{1,0:T(8,128)S(1)}, u32[]{:S(2)}, u32[]{:S(2)}) collective-permute-start(f32[256,256]{1,0:T(8,128)S(1)} %fusion.38), channel_id=1, source_target_pairs={{0,2},{1,3},{2,0},{3,1},{4,6},{5,7},{6,4},{7,5},{8,10},{9,11},{10,... | collective-permute-start | bytes 786440 | tf_op jit(solution)/shard_map/ppermute | solution.py:58
  17.7 7.1 %collective-permute-done.3 = bf16[256,896]{1,0:T(8,128)(2,1)S(1)} collective-permute-done((bf16[256,896]{1,0:T(8,128)(2,1)}, bf16[256,896]{1,0:T(8,128)(2,1)S(1)}, u32[]{:S(2)}, u32[]{:S(2)}) %collective-permute-start.3) | collective-permute-done | bytes 458784 | tf_op jit(solution)/shard_map/ppermute | solution.py:55
  24.8 2.1 %collective-permute-done.4 = bf16[256,896]{1,0:T(8,128)(2,1)S(1)} collective-permute-done((bf16[256,896]{1,0:T(8,128)(2,1)}, bf16[256,896]{1,0:T(8,128)(2,1)S(1)}, u32[]{:S(2)}, u32[]{:S(2)}) %collective-permute-start.4) | collective-permute-done | bytes 458784 | tf_op jit(solution)/shard_map/ppermute | solution.py:55
  27.7 0.6 collective-permute-start.8
  29.0 1.5 %collective-permute-start.13 = (bf16[256,896]{1,0:T(8,128)(2,1)S(1)}, bf16[256,896]{1,0:T(8,128)(2,1)S(1)}, u32[]{:S(2)}, u32[]{:S(2)}) collective-permute-start(bf16[256,896]{1,0:T(8,128)(2,1)S(1)} %collective-permute-done.3), channel_id=1, source_target_pairs={{0,4},{4,0},{8,12},{12,8},{16,20},{20,16},{24,28},{28,24},{1,5},{5... | collective-permute-start | bytes 1376264 | tf_op jit(solution)/shard_map/ppermute | solution.py:55
  30.5 1.2 %collective-permute-done.8 = f32[64,128]{1,0:T(8,128)S(1)} collective-permute-done((f32[64,128]{1,0:T(8,128)S(1)}, f32[64,128]{1,0:T(8,128)S(1)}, u32[]{:S(2)}, u32[]{:S(2)}) %collective-permute-start.8) | collective-permute-done | bytes 32800 | tf_op jit(solution)/shard_map/ppermute | solution.py:55
  32.1 0.8 collective-permute-start.9
  32.9 2.3 %collective-permute-start.6 = (f32[200,256]{1,0:T(8,128)S(1)}, f32[200,256]{1,0:T(8,128)S(1)}, u32[]{:S(2)}, u32[]{:S(2)}) collective-permute-start(f32[200,256]{1,0:T(8,128)S(1)} %pad_maximum_fusion.9), channel_id=1, source_target_pairs={{0,8},{4,12},{8,0},{12,4},{16,24},{20,28},{24,16},{28,20},{1,9},{5... | collective-permute-start | bytes 614408 | tf_op jit(solution)/shard_map/ppermute | solution.py:55
  35.7 1.6 %collective-permute-start.12 = (f32[384,128]{0,1:T(8,128)S(1)}, f32[384,128]{0,1:T(8,128)S(1)}, u32[]{:S(2)}, u32[]{:S(2)}) collective-permute-start(f32[384,128]{0,1:T(8,128)S(1)} %constant_dynamic-slice_fusion.2), channel_id=1, source_target_pairs={{0,2},{1,3},{2,0},{3,1},{4,6},{5,7},{6,4},{7,5},{8,10},{9,11},{10,... | collective-permute-start | bytes 589832 | tf_op jit(solution)/shard_map/ppermute | solution.py:58
  38.1 1.6 %collective-permute-start.11 = (f32[384,128]{0,1:T(8,128)S(1)}, f32[384,128]{0,1:T(8,128)S(1)}, u32[]{:S(2)}, u32[]{:S(2)}) collective-permute-start(f32[384,128]{0,1:T(8,128)S(1)} %constant_dynamic-slice_fusion.3), channel_id=1, source_target_pairs={{0,2},{1,3},{2,0},{3,1},{4,6},{5,7},{6,4},{7,5},{8,10},{9,11},{10,... | collective-permute-start | bytes 589832 | tf_op jit(solution)/shard_map/ppermute | solution.py:58
  39.7 2.0 %collective-permute-done.13 = bf16[256,896]{1,0:T(8,128)(2,1)S(1)} collective-permute-done((bf16[256,896]{1,0:T(8,128)(2,1)S(1)}, bf16[256,896]{1,0:T(8,128)(2,1)S(1)}, u32[]{:S(2)}, u32[]{:S(2)}) %collective-permute-start.13) | collective-permute-done | bytes 458784 | tf_op jit(solution)/shard_map/ppermute | solution.py:55
  42.2 1.3 %collective-permute-done.12 = f32[384,128]{0,1:T(8,128)S(1)} collective-permute-done((f32[384,128]{0,1:T(8,128)S(1)}, f32[384,128]{0,1:T(8,128)S(1)}, u32[]{:S(2)}, u32[]{:S(2)}) %collective-permute-start.12) | collective-permute-done | bytes 196640 | tf_op jit(solution)/shard_map/ppermute | solution.py:58
  43.5 0.6 collective-permute-start.17
  45.0 1.6 %collective-permute-start.15 = (f32[128,256]{0,1:T(8,128)S(1)}, f32[128,256]{0,1:T(8,128)S(1)}, u32[]{:S(2)}, u32[]{:S(2)}) collective-permute-start(f32[128,256]{0,1:T(8,128)S(1)} %constant_dynamic-slice_fusion.1), channel_id=1, source_target_pairs={{0,2},{1,3},{2,0},{3,1},{4,6},{5,7},{6,4},{7,5},{8,10},{9,11},{10,... | collective-permute-start | bytes 393224 | tf_op jit(solution)/shard_map/ppermute | solution.py:58
  46.6 3.4 %collective-permute-done.15 = f32[128,256]{0,1:T(8,128)S(1)} collective-permute-done((f32[128,256]{0,1:T(8,128)S(1)}, f32[128,256]{0,1:T(8,128)S(1)}, u32[]{:S(2)}, u32[]{:S(2)}) %collective-permute-start.15) | collective-permute-done | bytes 131104 | tf_op jit(solution)/shard_map/ppermute | solution.py:58
  50.5 1.1 %collective-permute-done.16 = f32[2,256]{1,0:T(2,128)S(1)} collective-permute-done((f32[2,256]{1,0:T(2,128)S(1)}, f32[2,256]{1,0:T(2,128)S(1)}, u32[]{:S(2)}, u32[]{:S(2)}) %collective-permute-start.16) | collective-permute-done | bytes 2080 | tf_op jit(solution)/shard_map/ppermute | solution.py:58
  51.7 1.2 %collective-permute-start.18 = (f32[2,256]{1,0:T(2,128)S(1)}, f32[2,256]{1,0:T(2,128)S(1)}, u32[]{:S(2)}, u32[]{:S(2)}) collective-permute-start(f32[2,256]{1,0:T(2,128)S(1)} %fusion.28), channel_id=1, source_target_pairs={{0,8},{4,12},{8,0},{12,4},{16,24},{20,28},{24,16},{28,20},{1,9},{5... | collective-permute-start | bytes 6152 | tf_op jit(solution)/shard_map/ppermute | solution.py:55
  52.9 2.6 %collective-permute-done.18 = f32[2,256]{1,0:T(2,128)S(1)} collective-permute-done((f32[2,256]{1,0:T(2,128)S(1)}, f32[2,256]{1,0:T(2,128)S(1)}, u32[]{:S(2)}, u32[]{:S(2)}) %collective-permute-start.18) | collective-permute-done | bytes 2080 | tf_op jit(solution)/shard_map/ppermute | solution.py:55
  56.2 1.3 %collective-permute-start.22 = (f32[64,256]{1,0:T(8,128)S(1)}, f32[64,256]{1,0:T(8,128)S(1)}, u32[]{:S(2)}, u32[]{:S(2)}) collective-permute-start(f32[64,256]{1,0:T(8,128)S(1)} %slice.208), channel_id=1, source_target_pairs={{0,4},{4,0},{8,12},{12,8},{16,20},{20,16},{24,28},{28,24},{1,5},{5... | collective-permute-start | bytes 196616 | tf_op jit(solution)/shard_map/ppermute | solution.py:55
  57.6 1.3 %collective-permute-start.20 = (f32[64,256]{1,0:T(8,128)S(1)}, f32[64,256]{1,0:T(8,128)S(1)}, u32[]{:S(2)}, u32[]{:S(2)}) collective-permute-start(f32[64,256]{1,0:T(8,128)S(1)} %pad_maximum_fusion.13), channel_id=1, source_target_pairs={{0,8},{4,12},{8,0},{12,4},{16,24},{20,28},{24,16},{28,20},{1,9},{5... | collective-permute-start | bytes 196616 | tf_op jit(solution)/shard_map/ppermute | solution.py:55
  58.9 1.9 %collective-permute-done.22 = f32[64,256]{1,0:T(8,128)S(1)} collective-permute-done((f32[64,256]{1,0:T(8,128)S(1)}, f32[64,256]{1,0:T(8,128)S(1)}, u32[]{:S(2)}, u32[]{:S(2)}) %collective-permute-start.22) | collective-permute-done | bytes 65568 | tf_op jit(solution)/shard_map/ppermute | solution.py:55
  60.8 2.1 %collective-permute-start.23 = (f32[64,128]{1,0:T(8,128)S(1)}, f32[64,128]{1,0:T(8,128)S(1)}, u32[]{:S(2)}, u32[]{:S(2)}) collective-permute-start(f32[64,128]{1,0:T(8,128)S(1)} %slice.210), channel_id=1, source_target_pairs={{0,16},{4,20},{8,24},{12,28},{16,0},{20,4},{24,8},{28,12},{1,17},{... | collective-permute-start | bytes 98312 | tf_op jit(solution)/shard_map/ppermute | solution.py:55
  63.0 1.4 %collective-permute-start.28 = (bf16[64,4096]{1,0:T(8,128)(2,1)S(1)}, bf16[64,4096]{1,0:T(8,128)(2,1)S(1)}, u32[]{:S(2)}, u32[]{:S(2)}) collective-permute-start(bf16[64,4096]{1,0:T(8,128)(2,1)S(1)} %collective-permute-done.27), channel_id=1, source_target_pairs={{0,4},{4,0},{8,12},{12,8},{16,20},{20,16},{24,28},{28,24},{1,5},{5... | collective-permute-start | bytes 1572872 | tf_op jit(solution)/shard_map/ppermute | solution.py:55
  64.4 1.0 %maximum_dynamic-update-slice_fusion = bf16[256,4096]{1,0:T(8,128)(2,1)S(1)} fusion(bf16[256,4096]{1,0:T(8,128)(2,1)S(1)} %constant_dynamic-update-slice_fusion.1, s32[]{:T(128)S(6)} %select_n.101, bf16[32,4096]{1,0:T(8,128)(2,1)S(1)} %collective-permute-done.17, bf16[32,4096]{1,0:T(8,128)(2,1)} %collective-permute-done.7), kind=kLoop, calls=%fused_computation.19 | loop fusion | flops 1048576 | bytes 1048580 | tf_op jit(solution)/shard_map/dynamic_update_slice | solution.py:237
  65.7 1.5 %collective-permute-start.24 = (f32[64,128]{1,0:T(8,128)S(1)}, f32[64,128]{1,0:T(8,128)S(1)}, u32[]{:S(2)}, u32[]{:S(2)}) collective-permute-start(f32[64,128]{1,0:T(8,128)S(1)} %slice_add_fusion.3), channel_id=1, source_target_pairs={{0,2},{1,3},{2,0},{3,1},{4,6},{5,7},{6,4},{7,5},{8,10},{9,11},{10,... | collective-permute-start | bytes 98312 | tf_op jit(solution)/shard_map/ppermute | solution.py:58
  67.3 2.4 %collective-permute-done.24 = f32[64,128]{1,0:T(8,128)S(1)} collective-permute-done((f32[64,128]{1,0:T(8,128)S(1)}, f32[64,128]{1,0:T(8,128)S(1)}, u32[]{:S(2)}, u32[]{:S(2)}) %collective-permute-start.24) | collective-permute-done | bytes 32800 | tf_op jit(solution)/shard_map/ppermute | solution.py:58
  69.6 1.0 %collective-permute-start.25 = (f32[64,128]{1,0:T(8,128)S(1)}, f32[64,128]{1,0:T(8,128)S(1)}, u32[]{:S(2)}, u32[]{:S(2)}) collective-permute-start(f32[64,128]{1,0:T(8,128)S(1)} %add.230), channel_id=1, source_target_pairs={{0,8},{4,12},{8,0},{12,4},{16,24},{20,28},{24,16},{28,20},{1,9},{5... | collective-permute-start | bytes 98312 | tf_op jit(solution)/shard_map/ppermute | solution.py:55
  70.6 1.5 %collective-permute-start.21 = (f32[128,128]{1,0:T(8,128)S(1)}, f32[128,128]{1,0:T(8,128)S(1)}, u32[]{:S(2)}, u32[]{:S(2)}) collective-permute-start(f32[128,128]{1,0:T(8,128)S(1)} %pad_maximum_fusion.14), channel_id=1, source_target_pairs={{0,2},{1,3},{2,0},{3,1},{4,6},{5,7},{6,4},{7,5},{8,10},{9,11},{10,... | collective-permute-start | bytes 196616 | tf_op jit(solution)/shard_map/ppermute | solution.py:58
  72.1 1.4 %collective-permute-done.25 = f32[64,128]{1,0:T(8,128)S(1)} collective-permute-done((f32[64,128]{1,0:T(8,128)S(1)}, f32[64,128]{1,0:T(8,128)S(1)}, u32[]{:S(2)}, u32[]{:S(2)}) %collective-permute-start.25) | collective-permute-done | bytes 32800 | tf_op jit(solution)/shard_map/ppermute | solution.py:55
  73.6 1.3 %collective-permute-done.21 = f32[128,128]{1,0:T(8,128)S(1)} collective-permute-done((f32[128,128]{1,0:T(8,128)S(1)}, f32[128,128]{1,0:T(8,128)S(1)}, u32[]{:S(2)}, u32[]{:S(2)}) %collective-permute-start.21) | collective-permute-done | bytes 65568 | tf_op jit(solution)/shard_map/ppermute | solution.py:58
  75.0 0.7 add_convert_fusion
  75.7 0.7 add_convert_fusion.1
  76.5 0.8 convolution_convert_fusion
  77.3 1.1 %collective-permute-start.29 = (bf16[256,256]{1,0:T(8,128)(2,1)S(1)}, bf16[256,256]{1,0:T(8,128)(2,1)S(1)}, u32[]{:S(2)}, u32[]{:S(2)}) collective-permute-start(bf16[256,256]{1,0:T(8,128)(2,1)S(1)} %convolution_convert_fusion), channel_id=1, source_target_pairs={{0,8},{4,12},{8,0},{12,4},{16,24},{20,28},{24,16},{28,20},{1,9},{5... | collective-permute-start | bytes 393224 | tf_op jit(solution)/shard_map/ppermute | solution.py:55
  78.4 0.8 fusion.50
  79.2 3.6 %collective-permute-done.29 = bf16[256,256]{1,0:T(8,128)(2,1)S(1)} collective-permute-done((bf16[256,256]{1,0:T(8,128)(2,1)S(1)}, bf16[256,256]{1,0:T(8,128)(2,1)S(1)}, u32[]{:S(2)}, u32[]{:S(2)}) %collective-permute-start.29) | collective-permute-done | bytes 131104 | tf_op jit(solution)/shard_map/ppermute | solution.py:55
  82.9 0.8 pad_maximum_fusion.3
  (113 shorter events, 6.9 us)
Async XLA Ops:
  0.0 10.5 %copy-start = (bf16[256,896]{1,0:T(8,128)(2,1)S(1)}, bf16[256,896]{1,0:T(8,128)(2,1)}, u32[]{:S(2)}) copy-start(bf16[256,896]{1,0:T(8,128)(2,1)} %param.12) | copy-start | bytes 1376260
  0.0 15.1 %copy-start.3 = (bf16[256,896]{1,0:T(8,128)(2,1)S(1)}, bf16[256,896]{1,0:T(8,128)(2,1)}, u32[]{:S(2)}) copy-start(bf16[256,896]{1,0:T(8,128)(2,1)} %param.11) | copy-start | bytes 1376260
  0.0 13.8 %copy-start.1 = (bf16[64,4096]{1,0:T(8,128)(2,1)S(1)}, bf16[64,4096]{1,0:T(8,128)(2,1)}, u32[]{:S(2)}) copy-start(bf16[64,4096]{1,0:T(8,128)(2,1)} %param.17) | copy-start | bytes 1572868
  0.0 24.8 %collective-permute-start.3 = (bf16[256,896]{1,0:T(8,128)(2,1)}, bf16[256,896]{1,0:T(8,128)(2,1)S(1)}, u32[]{:S(2)}, u32[]{:S(2)}) collective-permute-start(bf16[256,896]{1,0:T(8,128)(2,1)} %param.11), channel_id=1, source_target_pairs={{0,16},{4,20},{8,24},{12,28},{16,0},{20,4},{24,8},{28,12},{1,17},{... | collective-permute-start | bytes 1376264 | tf_op jit(solution)/shard_map/ppermute | solution.py:55
  4.8 12.9 %collective-permute-start.2 = (bf16[256,896]{1,0:T(8,128)(2,1)}, bf16[256,896]{1,0:T(8,128)(2,1)S(1)}, u32[]{:S(2)}, u32[]{:S(2)}) collective-permute-start(bf16[256,896]{1,0:T(8,128)(2,1)} %param.11), channel_id=1, source_target_pairs={{0,4},{4,0},{8,12},{12,8},{16,20},{20,16},{24,28},{28,24},{1,5},{5... | collective-permute-start | bytes 1376264 | tf_op jit(solution)/shard_map/ppermute | solution.py:55
  6.3 20.6 %collective-permute-start.4 = (bf16[256,896]{1,0:T(8,128)(2,1)}, bf16[256,896]{1,0:T(8,128)(2,1)S(1)}, u32[]{:S(2)}, u32[]{:S(2)}) collective-permute-start(bf16[256,896]{1,0:T(8,128)(2,1)} %param.9), channel_id=1, source_target_pairs={{0,8},{4,12},{8,0},{12,4},{16,24},{20,28},{24,16},{28,20},{1,9},{5... | collective-permute-start | bytes 1376264 | tf_op jit(solution)/shard_map/ppermute | solution.py:55
  10.5 5.4 %copy-start.7 = (s32[256]{0:T(256)S(1)}, s32[256]{0:T(256)}, u32[]{:S(2)}) copy-start(s32[256]{0:T(256)} %param.14) | copy-start | bytes 3076
  13.8 2.3 %collective-permute-start = (f32[256,256]{1,0:T(8,128)}, f32[256,256]{1,0:T(8,128)S(1)}, u32[]{:S(2)}, u32[]{:S(2)}) collective-permute-start(f32[256,256]{1,0:T(8,128)} %pad_maximum_fusion.8), channel_id=1, source_target_pairs={{0,1},{1,0},{2,3},{3,2},{4,5},{5,4},{6,7},{7,6},{8,9},{9,8},{10,11... | collective-permute-start | bytes 786440 | tf_op jit(solution)/shard_map/ppermute | solution.py:58
  14.6 13.0 %collective-permute-start.7 = (bf16[32,4096]{1,0:T(8,128)(2,1)}, bf16[32,4096]{1,0:T(8,128)(2,1)}, u32[]{:S(2)}, u32[]{:S(2)}) collective-permute-start(bf16[32,4096]{1,0:T(8,128)(2,1)} %get-tuple-element.44), channel_id=1, source_target_pairs={{0,4},{4,0},{8,12},{12,8},{16,20},{20,16},{24,28},{28,24},{1,5},{5... | collective-permute-start | bytes 786440 | tf_op jit(solution)/shard_map/ppermute | solution.py:55
  16.0 10.9 %copy-start.6 = (bf16[128,896]{1,0:T(8,128)(2,1)S(1)}, bf16[128,896]{1,0:T(8,128)(2,1)}, u32[]{:S(2)}) copy-start(bf16[128,896]{1,0:T(8,128)(2,1)} %get-tuple-element.46) | copy-start | bytes 688132
  16.1 11.4 %collective-permute-start.1 = (f32[256,256]{1,0:T(8,128)S(1)}, f32[256,256]{1,0:T(8,128)S(1)}, u32[]{:S(2)}, u32[]{:S(2)}) collective-permute-start(f32[256,256]{1,0:T(8,128)S(1)} %fusion.38), channel_id=1, source_target_pairs={{0,2},{1,3},{2,0},{3,1},{4,6},{5,7},{6,4},{7,5},{8,10},{9,11},{10,... | collective-permute-start | bytes 786440 | tf_op jit(solution)/shard_map/ppermute | solution.py:58
  17.7 9.7 %copy-start.2 = (bf16[256,896]{1,0:T(8,128)(2,1)S(1)}, bf16[256,896]{1,0:T(8,128)(2,1)}, u32[]{:S(2)}) copy-start(bf16[256,896]{1,0:T(8,128)(2,1)} %param.9) | copy-start | bytes 1376260
  27.3 4.3 %collective-permute-start.5 = (f32[384,256]{0,1:T(8,128)S(1)}, f32[384,256]{0,1:T(8,128)S(1)}, u32[]{:S(2)}, u32[]{:S(2)}) collective-permute-start(f32[384,256]{0,1:T(8,128)S(1)} %fusion.5), channel_id=1, source_target_pairs={{0,1},{1,0},{2,3},{3,2},{4,5},{5,4},{6,7},{7,6},{8,9},{9,8},{10,11... | collective-permute-start | bytes 1179656 | tf_op jit(solution)/shard_map/ppermute | solution.py:58
  27.6 4.1 %copy-start.5 = (bf16[128,896]{1,0:T(8,128)(2,1)S(1)}, bf16[128,896]{1,0:T(8,128)(2,1)}, u32[]{:S(2)}) copy-start(bf16[128,896]{1,0:T(8,128)(2,1)} %get-tuple-element.45) | copy-start | bytes 688132
  27.7 4.0 %collective-permute-start.8 = (f32[64,128]{1,0:T(8,128)S(1)}, f32[64,128]{1,0:T(8,128)S(1)}, u32[]{:S(2)}, u32[]{:S(2)}) collective-permute-start(f32[64,128]{1,0:T(8,128)S(1)} %constant_dynamic-slice_fusion.4), channel_id=1, source_target_pairs={{0,4},{4,0},{8,12},{12,8},{16,20},{20,16},{24,28},{28,24},{1,5},{5... | collective-permute-start | bytes 98312 | tf_op jit(solution)/shard_map/ppermute | solution.py:55
  28.7 7.0 %collective-permute-start.10 = (f32[384,256]{0,1:T(8,128)S(1)}, f32[384,256]{0,1:T(8,128)S(1)}, u32[]{:S(2)}, u32[]{:S(2)}) collective-permute-start(f32[384,256]{0,1:T(8,128)S(1)} %fusion.4), channel_id=1, source_target_pairs={{0,1},{1,0},{2,3},{3,2},{4,5},{5,4},{6,7},{7,6},{8,9},{9,8},{10,11... | collective-permute-start | bytes 1179656 | tf_op jit(solution)/shard_map/ppermute | solution.py:58
  29.0 12.7 %collective-permute-start.13 = (bf16[256,896]{1,0:T(8,128)(2,1)S(1)}, bf16[256,896]{1,0:T(8,128)(2,1)S(1)}, u32[]{:S(2)}, u32[]{:S(2)}) collective-permute-start(bf16[256,896]{1,0:T(8,128)(2,1)S(1)} %collective-permute-done.3), channel_id=1, source_target_pairs={{0,4},{4,0},{8,12},{12,8},{16,20},{20,16},{24,28},{28,24},{1,5},{5... | collective-permute-start | bytes 1376264 | tf_op jit(solution)/shard_map/ppermute | solution.py:55
  32.1 6.0 %collective-permute-start.9 = (f32[64,256]{1,0:T(8,128)S(1)}, f32[64,256]{1,0:T(8,128)S(1)}, u32[]{:S(2)}, u32[]{:S(2)}) collective-permute-start(f32[64,256]{1,0:T(8,128)S(1)} %pad_maximum_fusion.12), channel_id=1, source_target_pairs={{0,16},{4,20},{8,24},{12,28},{16,0},{20,4},{24,8},{28,12},{1,17},{... | collective-permute-start | bytes 196616 | tf_op jit(solution)/shard_map/ppermute | solution.py:55
  32.9 11.6 %collective-permute-start.6 = (f32[200,256]{1,0:T(8,128)S(1)}, f32[200,256]{1,0:T(8,128)S(1)}, u32[]{:S(2)}, u32[]{:S(2)}) collective-permute-start(f32[200,256]{1,0:T(8,128)S(1)} %pad_maximum_fusion.9), channel_id=1, source_target_pairs={{0,8},{4,12},{8,0},{12,4},{16,24},{20,28},{24,16},{28,20},{1,9},{5... | collective-permute-start | bytes 614408 | tf_op jit(solution)/shard_map/ppermute | solution.py:55
  35.3 27.7 %collective-permute-start.27 = (bf16[64,4096]{1,0:T(8,128)(2,1)S(1)}, bf16[64,4096]{1,0:T(8,128)(2,1)S(1)}, u32[]{:S(2)}, u32[]{:S(2)}) collective-permute-start(bf16[64,4096]{1,0:T(8,128)(2,1)S(1)} %copy-done.1), channel_id=1, source_target_pairs={{0,16},{4,20},{8,24},{12,28},{16,0},{20,4},{24,8},{28,12},{1,17},{... | collective-permute-start | bytes 1572872 | tf_op jit(solution)/shard_map/ppermute | solution.py:55
  35.7 7.8 %copy-start.4 = (bf16[32,4096]{1,0:T(8,128)(2,1)S(1)}, bf16[32,4096]{1,0:T(8,128)(2,1)}, u32[]{:S(2)}) copy-start(bf16[32,4096]{1,0:T(8,128)(2,1)} %get-tuple-element.30) | copy-start | bytes 786436
  35.7 7.8 %collective-permute-start.12 = (f32[384,128]{0,1:T(8,128)S(1)}, f32[384,128]{0,1:T(8,128)S(1)}, u32[]{:S(2)}, u32[]{:S(2)}) collective-permute-start(f32[384,128]{0,1:T(8,128)S(1)} %constant_dynamic-slice_fusion.2), channel_id=1, source_target_pairs={{0,2},{1,3},{2,0},{3,1},{4,6},{5,7},{6,4},{7,5},{8,10},{9,11},{10,... | collective-permute-start | bytes 589832 | tf_op jit(solution)/shard_map/ppermute | solution.py:58
  38.1 8.5 %collective-permute-start.11 = (f32[384,128]{0,1:T(8,128)S(1)}, f32[384,128]{0,1:T(8,128)S(1)}, u32[]{:S(2)}, u32[]{:S(2)}) collective-permute-start(f32[384,128]{0,1:T(8,128)S(1)} %constant_dynamic-slice_fusion.3), channel_id=1, source_target_pairs={{0,2},{1,3},{2,0},{3,1},{4,6},{5,7},{6,4},{7,5},{8,10},{9,11},{10,... | collective-permute-start | bytes 589832 | tf_op jit(solution)/shard_map/ppermute | solution.py:58
  42.1 2.4 %collective-permute-start.14 = (f32[128,512]{0,1:T(8,128)S(1)}, f32[128,512]{0,1:T(8,128)S(1)}, u32[]{:S(2)}, u32[]{:S(2)}) collective-permute-start(f32[128,512]{0,1:T(8,128)S(1)} %fusion.6), channel_id=1, source_target_pairs={{0,1},{1,0},{2,3},{3,2},{4,5},{5,4},{6,7},{7,6},{8,9},{9,8},{10,11... | collective-permute-start | bytes 786440 | tf_op jit(solution)/shard_map/ppermute | solution.py:58
  43.5 8.2 %collective-permute-start.17 = (bf16[32,4096]{1,0:T(8,128)(2,1)S(1)}, bf16[32,4096]{1,0:T(8,128)(2,1)S(1)}, u32[]{:S(2)}, u32[]{:S(2)}) collective-permute-start(bf16[32,4096]{1,0:T(8,128)(2,1)S(1)} %copy-done.4), channel_id=1, source_target_pairs={{0,4},{4,0},{8,12},{12,8},{16,20},{20,16},{24,28},{28,24},{1,5},{5... | collective-permute-start | bytes 786440 | tf_op jit(solution)/shard_map/ppermute | solution.py:55
  45.0 5.0 %collective-permute-start.15 = (f32[128,256]{0,1:T(8,128)S(1)}, f32[128,256]{0,1:T(8,128)S(1)}, u32[]{:S(2)}, u32[]{:S(2)}) collective-permute-start(f32[128,256]{0,1:T(8,128)S(1)} %constant_dynamic-slice_fusion.1), channel_id=1, source_target_pairs={{0,2},{1,3},{2,0},{3,1},{4,6},{5,7},{6,4},{7,5},{8,10},{9,11},{10,... | collective-permute-start | bytes 393224 | tf_op jit(solution)/shard_map/ppermute | solution.py:58
  50.4 1.2 %collective-permute-start.16 = (f32[2,256]{1,0:T(2,128)S(1)}, f32[2,256]{1,0:T(2,128)S(1)}, u32[]{:S(2)}, u32[]{:S(2)}) collective-permute-start(f32[2,256]{1,0:T(2,128)S(1)} %pad_maximum_fusion.17), channel_id=1, source_target_pairs={{0,1},{1,0},{2,3},{3,2},{4,5},{5,4},{6,7},{7,6},{8,9},{9,8},{10,11... | collective-permute-start | bytes 6152 | tf_op jit(solution)/shard_map/ppermute | solution.py:58
  51.7 3.8 %collective-permute-start.18 = (f32[2,256]{1,0:T(2,128)S(1)}, f32[2,256]{1,0:T(2,128)S(1)}, u32[]{:S(2)}, u32[]{:S(2)}) collective-permute-start(f32[2,256]{1,0:T(2,128)S(1)} %fusion.28), channel_id=1, source_target_pairs={{0,8},{4,12},{8,0},{12,4},{16,24},{20,28},{24,16},{28,20},{1,9},{5... | collective-permute-start | bytes 6152 | tf_op jit(solution)/shard_map/ppermute | solution.py:55
  55.9 1.6 %collective-permute-start.19 = (f32[64,256]{1,0:T(8,128)S(1)}, f32[64,256]{1,0:T(8,128)S(1)}, u32[]{:S(2)}, u32[]{:S(2)}) collective-permute-start(f32[64,256]{1,0:T(8,128)S(1)} %fusion.20), channel_id=1, source_target_pairs={{0,1},{1,0},{2,3},{3,2},{4,5},{5,4},{6,7},{7,6},{8,9},{9,8},{10,11... | collective-permute-start | bytes 196616 | tf_op jit(solution)/shard_map/ppermute | solution.py:58
  56.2 4.6 %collective-permute-start.22 = (f32[64,256]{1,0:T(8,128)S(1)}, f32[64,256]{1,0:T(8,128)S(1)}, u32[]{:S(2)}, u32[]{:S(2)}) collective-permute-start(f32[64,256]{1,0:T(8,128)S(1)} %slice.208), channel_id=1, source_target_pairs={{0,4},{4,0},{8,12},{12,8},{16,20},{20,16},{24,28},{28,24},{1,5},{5... | collective-permute-start | bytes 196616 | tf_op jit(solution)/shard_map/ppermute | solution.py:55
  57.6 9.6 %collective-permute-start.20 = (f32[64,256]{1,0:T(8,128)S(1)}, f32[64,256]{1,0:T(8,128)S(1)}, u32[]{:S(2)}, u32[]{:S(2)}) collective-permute-start(f32[64,256]{1,0:T(8,128)S(1)} %pad_maximum_fusion.13), channel_id=1, source_target_pairs={{0,8},{4,12},{8,0},{12,4},{16,24},{20,28},{24,16},{28,20},{1,9},{5... | collective-permute-start | bytes 196616 | tf_op jit(solution)/shard_map/ppermute | solution.py:55
  60.8 4.9 %collective-permute-start.23 = (f32[64,128]{1,0:T(8,128)S(1)}, f32[64,128]{1,0:T(8,128)S(1)}, u32[]{:S(2)}, u32[]{:S(2)}) collective-permute-start(f32[64,128]{1,0:T(8,128)S(1)} %slice.210), channel_id=1, source_target_pairs={{0,16},{4,20},{8,24},{12,28},{16,0},{20,4},{24,8},{28,12},{1,17},{... | collective-permute-start | bytes 98312 | tf_op jit(solution)/shard_map/ppermute | solution.py:55
  63.0 13.5 %collective-permute-start.28 = (bf16[64,4096]{1,0:T(8,128)(2,1)S(1)}, bf16[64,4096]{1,0:T(8,128)(2,1)S(1)}, u32[]{:S(2)}, u32[]{:S(2)}) collective-permute-start(bf16[64,4096]{1,0:T(8,128)(2,1)S(1)} %collective-permute-done.27), channel_id=1, source_target_pairs={{0,4},{4,0},{8,12},{12,8},{16,20},{20,16},{24,28},{28,24},{1,5},{5... | collective-permute-start | bytes 1572872 | tf_op jit(solution)/shard_map/ppermute | solution.py:55
  65.7 3.9 %collective-permute-start.24 = (f32[64,128]{1,0:T(8,128)S(1)}, f32[64,128]{1,0:T(8,128)S(1)}, u32[]{:S(2)}, u32[]{:S(2)}) collective-permute-start(f32[64,128]{1,0:T(8,128)S(1)} %slice_add_fusion.3), channel_id=1, source_target_pairs={{0,2},{1,3},{2,0},{3,1},{4,6},{5,7},{6,4},{7,5},{8,10},{9,11},{10,... | collective-permute-start | bytes 98312 | tf_op jit(solution)/shard_map/ppermute | solution.py:58
  69.6 3.9 %collective-permute-start.25 = (f32[64,128]{1,0:T(8,128)S(1)}, f32[64,128]{1,0:T(8,128)S(1)}, u32[]{:S(2)}, u32[]{:S(2)}) collective-permute-start(f32[64,128]{1,0:T(8,128)S(1)} %add.230), channel_id=1, source_target_pairs={{0,8},{4,12},{8,0},{12,4},{16,24},{20,28},{24,16},{28,20},{1,9},{5... | collective-permute-start | bytes 98312 | tf_op jit(solution)/shard_map/ppermute | solution.py:55
  70.6 4.3 %collective-permute-start.21 = (f32[128,128]{1,0:T(8,128)S(1)}, f32[128,128]{1,0:T(8,128)S(1)}, u32[]{:S(2)}, u32[]{:S(2)}) collective-permute-start(f32[128,128]{1,0:T(8,128)S(1)} %pad_maximum_fusion.14), channel_id=1, source_target_pairs={{0,2},{1,3},{2,0},{3,1},{4,6},{5,7},{6,4},{7,5},{8,10},{9,11},{10,... | collective-permute-start | bytes 196616 | tf_op jit(solution)/shard_map/ppermute | solution.py:58
  73.6 1.4 %collective-permute-start.26 = (f32[128,128]{1,0:T(8,128)S(1)}, f32[128,128]{1,0:T(8,128)S(1)}, u32[]{:S(2)}, u32[]{:S(2)}) collective-permute-start(f32[128,128]{1,0:T(8,128)S(1)} %pad_maximum_fusion.15), channel_id=1, source_target_pairs={{0,1},{1,0},{2,3},{3,2},{4,5},{5,4},{6,7},{7,6},{8,9},{9,8},{10,11... | collective-permute-start | bytes 196616 | tf_op jit(solution)/shard_map/ppermute | solution.py:58
  77.3 5.5 %collective-permute-start.29 = (bf16[256,256]{1,0:T(8,128)(2,1)S(1)}, bf16[256,256]{1,0:T(8,128)(2,1)S(1)}, u32[]{:S(2)}, u32[]{:S(2)}) collective-permute-start(bf16[256,256]{1,0:T(8,128)(2,1)S(1)} %convolution_convert_fusion), channel_id=1, source_target_pairs={{0,8},{4,12},{8,0},{12,4},{16,24},{20,28},{24,16},{28,20},{1,9},{5... | collective-permute-start | bytes 393224 | tf_op jit(solution)/shard_map/ppermute | solution.py:55

commit v5 on v4

--- a/solution.py
+++ b/solution.py
@@ -206,7 +206,8 @@
     while bit < n_test:
         out_pass = out_pass + over_test(out_pass, bit)
         bit *= 2
-    out_pass = jnp.concatenate((out_pass, over_train(out_pass, near)), axis=0)
+    out_pass_near = over_train(out_pass.astype(BF16), near).astype(F32)
+    out_pass = jnp.concatenate((out_pass, out_pass_near), axis=0)
     out_pass_other = over_test(out_pass, 1)
     out_pass = jnp.where(
         core == 0,

time: 83.9 us -> 83.9 us (level)
  no operation moved by 1% of the time
where the time goes in v5:
time: 83.9 us; the launch traced here: 83.7 us
  starting transfers between devices  33.1 us (39%)
  waiting for transfers between devices  32.3 us (38%)
  matrix products  9.53 us (11%)
  other arithmetic  5.87 us (7%)
  local copies, waits for them, and re-layouts  2.25 us (3%)
    ppermute x17, starting transfers between devices, over_train(): return lax.ppermute(a, 'train', [(i, i ^ bit) for i in range(n_train)])  23.2 us
    ppermute x17, waiting for transfers between devices, over_train(): return lax.ppermute(a, 'train', [(i, i ^ bit) for i in range(n_train)])  22.7 us
    ppermute x13, starting transfers between devices, over_test(): return lax.ppermute(a, 'test', [(i, i ^ bit) for i in range(n_test)])  9.89 us
    ppermute x13, waiting for transfers between devices, over_test(): return lax.ppermute(a, 'test', [(i, i ^ bit) for i in range(n_test)])  9.6 us
    dot_general x14, matrix products, dot(): lax.dot_general(a, b, (((ca,), (cb,)), ((), ())), preferred_element_type=...  9.53 us
  transfers between devices with their start and end apart: 30, of which 16 were waited for; matrix products, arithmetic and copies ran while one was open for 19% of the time, Pallas kernels for 0%

profile of v5, /device:TPU:0, one launch (start us, length us, event | category | flops | bytes accessed | tf_op | source)
XLA Modules:
  0.0 83.7 jit_solution(1150612902516722679)
XLA Ops:
  0.0 4.1 %collective-permute-start.3 = (bf16[256,896]{1,0:T(8,128)(2,1)}, bf16[256,896]{1,0:T(8,128)(2,1)S(1)}, u32[]{:S(2)}, u32[]{:S(2)}) collective-permute-start(bf16[256,896]{1,0:T(8,128)(2,1)} %param.11), channel_id=1, source_target_pairs={{0,16},{4,20},{8,24},{12,28},{16,0},{20,4},{24,8},{28,12},{1,17},{... | collective-permute-start | bytes 1376264 | tf_op jit(solution)/shard_map/ppermute | solution.py:55
  4.1 0.7 convert_element_type.55
  4.8 1.5 %collective-permute-start.2 = (bf16[256,896]{1,0:T(8,128)(2,1)}, bf16[256,896]{1,0:T(8,128)(2,1)S(1)}, u32[]{:S(2)}, u32[]{:S(2)}) collective-permute-start(bf16[256,896]{1,0:T(8,128)(2,1)} %param.11), channel_id=1, source_target_pairs={{0,4},{4,0},{8,12},{12,8},{16,20},{20,16},{24,28},{28,24},{1,5},{5... | collective-permute-start | bytes 1376264 | tf_op jit(solution)/shard_map/ppermute | solution.py:55
  6.3 1.6 %collective-permute-start.4 = (bf16[256,896]{1,0:T(8,128)(2,1)}, bf16[256,896]{1,0:T(8,128)(2,1)S(1)}, u32[]{:S(2)}, u32[]{:S(2)}) collective-permute-start(bf16[256,896]{1,0:T(8,128)(2,1)} %param.9), channel_id=1, source_target_pairs={{0,8},{4,12},{8,0},{12,4},{16,24},{20,28},{24,16},{28,20},{1,9},{5... | collective-permute-start | bytes 1376264 | tf_op jit(solution)/shard_map/ppermute | solution.py:55
  7.9 1.3 %convolution_bitcast_fusion = f32[64,256]{1,0:T(8,128)S(1)} fusion(bf16[256,896]{1,0:T(8,128)(2,1)} %param.11, bf16[896,64]{0,1:T(8,128)(2,1)} %param.16), kind=kOutput, calls=%fused_computation.6 | convolution fusion | flops 29360128 | bytes 638976 | tf_op jit(solution)/shard_map/dot_general | solution.py:14
  9.2 1.3 %convolution_bitcast_fusion.1 = f32[64,256]{1,0:T(8,128)S(1)} fusion(bf16[256,896]{1,0:T(8,128)(2,1)} %param.9, bf16[896,64]{0,1:T(8,128)(2,1)} %param.16), kind=kOutput, calls=%fused_computation.7 | convolution fusion | flops 29360128 | bytes 638976 | tf_op jit(solution)/shard_map/dot_general | solution.py:14
  10.6 1.2 %convolution_bitcast_fusion.2 = f32[64,256]{1,0:T(8,128)S(1)} fusion(bf16[256,896]{1,0:T(8,128)(2,1)S(1)} %copy-done, bf16[896,64]{0,1:T(8,128)(2,1)} %param.15), kind=kOutput, calls=%fused_computation.8 | convolution fusion | flops 29360128 | bytes 638976 | tf_op jit(solution)/shard_map/dot_general | solution.py:14
  11.7 1.3 %convolution_bitcast_fusion.3 = f32[64,256]{1,0:T(8,128)S(1)} fusion(bf16[256,896]{1,0:T(8,128)(2,1)} %param.10, bf16[896,64]{0,1:T(8,128)(2,1)} %param.15), kind=kOutput, calls=%fused_computation.9 | convolution fusion | flops 29360128 | bytes 638976 | tf_op jit(solution)/shard_map/dot_general | solution.py:14
  13.1 0.7 pad_maximum_fusion.8
  13.8 0.8 fusion.42
  15.1 0.8 dynamic-slice_bitcast_fusion.5
  16.1 1.6 %collective-permute-start.1 = (f32[256,256]{1,0:T(8,128)S(1)}, f32[256,256]{1,0:T(8,128)S(1)}, u32[]{:S(2)}, u32[]{:S(2)}) collective-permute-start(f32[256,256]{1,0:T(8,128)S(1)} %fusion.38), channel_id=1, source_target_pairs={{0,2},{1,3},{2,0},{3,1},{4,6},{5,7},{6,4},{7,5},{8,10},{9,11},{10,... | collective-permute-start | bytes 786440 | tf_op jit(solution)/shard_map/ppermute | solution.py:58
  17.7 7.1 %collective-permute-done.3 = bf16[256,896]{1,0:T(8,128)(2,1)S(1)} collective-permute-done((bf16[256,896]{1,0:T(8,128)(2,1)}, bf16[256,896]{1,0:T(8,128)(2,1)S(1)}, u32[]{:S(2)}, u32[]{:S(2)}) %collective-permute-start.3) | collective-permute-done | bytes 458784 | tf_op jit(solution)/shard_map/ppermute | solution.py:55
  24.8 2.1 %collective-permute-done.4 = bf16[256,896]{1,0:T(8,128)(2,1)S(1)} collective-permute-done((bf16[256,896]{1,0:T(8,128)(2,1)}, bf16[256,896]{1,0:T(8,128)(2,1)S(1)}, u32[]{:S(2)}, u32[]{:S(2)}) %collective-permute-start.4) | collective-permute-done | bytes 458784 | tf_op jit(solution)/shard_map/ppermute | solution.py:55
  27.7 0.6 collective-permute-start.8
  29.0 1.5 %collective-permute-start.13 = (bf16[256,896]{1,0:T(8,128)(2,1)S(1)}, bf16[256,896]{1,0:T(8,128)(2,1)S(1)}, u32[]{:S(2)}, u32[]{:S(2)}) collective-permute-start(bf16[256,896]{1,0:T(8,128)(2,1)S(1)} %collective-permute-done.3), channel_id=1, source_target_pairs={{0,4},{4,0},{8,12},{12,8},{16,20},{20,16},{24,28},{28,24},{1,5},{5... | collective-permute-start | bytes 1376264 | tf_op jit(solution)/shard_map/ppermute | solution.py:55
  30.5 1.2 %collective-permute-done.8 = f32[64,128]{1,0:T(8,128)S(1)} collective-permute-done((f32[64,128]{1,0:T(8,128)S(1)}, f32[64,128]{1,0:T(8,128)S(1)}, u32[]{:S(2)}, u32[]{:S(2)}) %collective-permute-start.8) | collective-permute-done | bytes 32800 | tf_op jit(solution)/shard_map/ppermute | solution.py:55
  32.1 0.8 collective-permute-start.9
  32.9 2.3 %collective-permute-start.6 = (f32[200,256]{1,0:T(8,128)S(1)}, f32[200,256]{1,0:T(8,128)S(1)}, u32[]{:S(2)}, u32[]{:S(2)}) collective-permute-start(f32[200,256]{1,0:T(8,128)S(1)} %pad_maximum_fusion.9), channel_id=1, source_target_pairs={{0,8},{4,12},{8,0},{12,4},{16,24},{20,28},{24,16},{28,20},{1,9},{5... | collective-permute-start | bytes 614408 | tf_op jit(solution)/shard_map/ppermute | solution.py:55
  35.7 1.6 %collective-permute-start.12 = (f32[384,128]{0,1:T(8,128)S(1)}, f32[384,128]{0,1:T(8,128)S(1)}, u32[]{:S(2)}, u32[]{:S(2)}) collective-permute-start(f32[384,128]{0,1:T(8,128)S(1)} %constant_dynamic-slice_fusion.2), channel_id=1, source_target_pairs={{0,2},{1,3},{2,0},{3,1},{4,6},{5,7},{6,4},{7,5},{8,10},{9,11},{10,... | collective-permute-start | bytes 589832 | tf_op jit(solution)/shard_map/ppermute | solution.py:58
  38.1 1.6 %collective-permute-start.11 = (f32[384,128]{0,1:T(8,128)S(1)}, f32[384,128]{0,1:T(8,128)S(1)}, u32[]{:S(2)}, u32[]{:S(2)}) collective-permute-start(f32[384,128]{0,1:T(8,128)S(1)} %constant_dynamic-slice_fusion.3), channel_id=1, source_target_pairs={{0,2},{1,3},{2,0},{3,1},{4,6},{5,7},{6,4},{7,5},{8,10},{9,11},{10,... | collective-permute-start | bytes 589832 | tf_op jit(solution)/shard_map/ppermute | solution.py:58
  39.7 2.0 %collective-permute-done.13 = bf16[256,896]{1,0:T(8,128)(2,1)S(1)} collective-permute-done((bf16[256,896]{1,0:T(8,128)(2,1)S(1)}, bf16[256,896]{1,0:T(8,128)(2,1)S(1)}, u32[]{:S(2)}, u32[]{:S(2)}) %collective-permute-start.13) | collective-permute-done | bytes 458784 | tf_op jit(solution)/shard_map/ppermute | solution.py:55
  42.2 1.3 %collective-permute-done.12 = f32[384,128]{0,1:T(8,128)S(1)} collective-permute-done((f32[384,128]{0,1:T(8,128)S(1)}, f32[384,128]{0,1:T(8,128)S(1)}, u32[]{:S(2)}, u32[]{:S(2)}) %collective-permute-start.12) | collective-permute-done | bytes 196640 | tf_op jit(solution)/shard_map/ppermute | solution.py:58
  43.5 0.6 collective-permute-start.17
  45.0 1.6 %collective-permute-start.15 = (f32[128,256]{0,1:T(8,128)S(1)}, f32[128,256]{0,1:T(8,128)S(1)}, u32[]{:S(2)}, u32[]{:S(2)}) collective-permute-start(f32[128,256]{0,1:T(8,128)S(1)} %constant_dynamic-slice_fusion.1), channel_id=1, source_target_pairs={{0,2},{1,3},{2,0},{3,1},{4,6},{5,7},{6,4},{7,5},{8,10},{9,11},{10,... | collective-permute-start | bytes 393224 | tf_op jit(solution)/shard_map/ppermute | solution.py:58
  46.6 3.4 %collective-permute-done.15 = f32[128,256]{0,1:T(8,128)S(1)} collective-permute-done((f32[128,256]{0,1:T(8,128)S(1)}, f32[128,256]{0,1:T(8,128)S(1)}, u32[]{:S(2)}, u32[]{:S(2)}) %collective-permute-start.15) | collective-permute-done | bytes 131104 | tf_op jit(solution)/shard_map/ppermute | solution.py:58
  50.5 1.1 %collective-permute-done.16 = f32[2,256]{1,0:T(2,128)S(1)} collective-permute-done((f32[2,256]{1,0:T(2,128)S(1)}, f32[2,256]{1,0:T(2,128)S(1)}, u32[]{:S(2)}, u32[]{:S(2)}) %collective-permute-start.16) | collective-permute-done | bytes 2080 | tf_op jit(solution)/shard_map/ppermute | solution.py:58
  51.7 1.2 %collective-permute-start.18 = (f32[2,256]{1,0:T(2,128)S(1)}, f32[2,256]{1,0:T(2,128)S(1)}, u32[]{:S(2)}, u32[]{:S(2)}) collective-permute-start(f32[2,256]{1,0:T(2,128)S(1)} %fusion.28), channel_id=1, source_target_pairs={{0,8},{4,12},{8,0},{12,4},{16,24},{20,28},{24,16},{28,20},{1,9},{5... | collective-permute-start | bytes 6152 | tf_op jit(solution)/shard_map/ppermute | solution.py:55
  52.9 2.6 %collective-permute-done.18 = f32[2,256]{1,0:T(2,128)S(1)} collective-permute-done((f32[2,256]{1,0:T(2,128)S(1)}, f32[2,256]{1,0:T(2,128)S(1)}, u32[]{:S(2)}, u32[]{:S(2)}) %collective-permute-start.18) | collective-permute-done | bytes 2080 | tf_op jit(solution)/shard_map/ppermute | solution.py:55
  56.2 1.3 %collective-permute-start.22 = (f32[64,256]{1,0:T(8,128)S(1)}, f32[64,256]{1,0:T(8,128)S(1)}, u32[]{:S(2)}, u32[]{:S(2)}) collective-permute-start(f32[64,256]{1,0:T(8,128)S(1)} %slice.208), channel_id=1, source_target_pairs={{0,4},{4,0},{8,12},{12,8},{16,20},{20,16},{24,28},{28,24},{1,5},{5... | collective-permute-start | bytes 196616 | tf_op jit(solution)/shard_map/ppermute | solution.py:55
  57.6 1.3 %collective-permute-start.20 = (f32[64,256]{1,0:T(8,128)S(1)}, f32[64,256]{1,0:T(8,128)S(1)}, u32[]{:S(2)}, u32[]{:S(2)}) collective-permute-start(f32[64,256]{1,0:T(8,128)S(1)} %pad_maximum_fusion.13), channel_id=1, source_target_pairs={{0,8},{4,12},{8,0},{12,4},{16,24},{20,28},{24,16},{28,20},{1,9},{5... | collective-permute-start | bytes 196616 | tf_op jit(solution)/shard_map/ppermute | solution.py:55
  58.9 1.9 %collective-permute-done.22 = f32[64,256]{1,0:T(8,128)S(1)} collective-permute-done((f32[64,256]{1,0:T(8,128)S(1)}, f32[64,256]{1,0:T(8,128)S(1)}, u32[]{:S(2)}, u32[]{:S(2)}) %collective-permute-start.22) | collective-permute-done | bytes 65568 | tf_op jit(solution)/shard_map/ppermute | solution.py:55
  60.8 2.1 %collective-permute-start.23 = (f32[64,128]{1,0:T(8,128)S(1)}, f32[64,128]{1,0:T(8,128)S(1)}, u32[]{:S(2)}, u32[]{:S(2)}) collective-permute-start(f32[64,128]{1,0:T(8,128)S(1)} %slice.210), channel_id=1, source_target_pairs={{0,16},{4,20},{8,24},{12,28},{16,0},{20,4},{24,8},{28,12},{1,17},{... | collective-permute-start | bytes 98312 | tf_op jit(solution)/shard_map/ppermute | solution.py:55
  63.0 1.4 %collective-permute-start.28 = (bf16[64,4096]{1,0:T(8,128)(2,1)S(1)}, bf16[64,4096]{1,0:T(8,128)(2,1)S(1)}, u32[]{:S(2)}, u32[]{:S(2)}) collective-permute-start(bf16[64,4096]{1,0:T(8,128)(2,1)S(1)} %collective-permute-done.27), channel_id=1, source_target_pairs={{0,4},{4,0},{8,12},{12,8},{16,20},{20,16},{24,28},{28,24},{1,5},{5... | collective-permute-start | bytes 1572872 | tf_op jit(solution)/shard_map/ppermute | solution.py:55
  64.4 1.0 %maximum_dynamic-update-slice_fusion = bf16[256,4096]{1,0:T(8,128)(2,1)S(1)} fusion(bf16[256,4096]{1,0:T(8,128)(2,1)S(1)} %constant_dynamic-update-slice_fusion.1, s32[]{:T(128)S(6)} %select_n.101, bf16[32,4096]{1,0:T(8,128)(2,1)S(1)} %collective-permute-done.17, bf16[32,4096]{1,0:T(8,128)(2,1)} %collective-permute-done.7), kind=kLoop, calls=%fused_computation.19 | loop fusion | flops 1048576 | bytes 1048580 | tf_op jit(solution)/shard_map/dynamic_update_slice | solution.py:238
  65.7 1.5 %collective-permute-start.24 = (f32[64,128]{1,0:T(8,128)S(1)}, f32[64,128]{1,0:T(8,128)S(1)}, u32[]{:S(2)}, u32[]{:S(2)}) collective-permute-start(f32[64,128]{1,0:T(8,128)S(1)} %slice_add_fusion.3), channel_id=1, source_target_pairs={{0,2},{1,3},{2,0},{3,1},{4,6},{5,7},{6,4},{7,5},{8,10},{9,11},{10,... | collective-permute-start | bytes 98312 | tf_op jit(solution)/shard_map/ppermute | solution.py:58
  67.3 2.4 %collective-permute-done.24 = f32[64,128]{1,0:T(8,128)S(1)} collective-permute-done((f32[64,128]{1,0:T(8,128)S(1)}, f32[64,128]{1,0:T(8,128)S(1)}, u32[]{:S(2)}, u32[]{:S(2)}) %collective-permute-start.24) | collective-permute-done | bytes 32800 | tf_op jit(solution)/shard_map/ppermute | solution.py:58
  69.6 1.0 %collective-permute-start.25 = (bf16[64,128]{1,0:T(8,128)(2,1)S(1)}, bf16[64,128]{1,0:T(8,128)(2,1)S(1)}, u32[]{:S(2)}, u32[]{:S(2)}) collective-permute-start(bf16[64,128]{1,0:T(8,128)(2,1)S(1)} %get-tuple-element.35), channel_id=1, source_target_pairs={{0,8},{4,12},{8,0},{12,4},{16,24},{20,28},{24,16},{28,20},{1,9},{5... | collective-permute-start | bytes 49160 | tf_op jit(solution)/shard_map/ppermute | solution.py:55
  70.7 1.5 %collective-permute-start.21 = (f32[128,128]{1,0:T(8,128)S(1)}, f32[128,128]{1,0:T(8,128)S(1)}, u32[]{:S(2)}, u32[]{:S(2)}) collective-permute-start(f32[128,128]{1,0:T(8,128)S(1)} %pad_maximum_fusion.14), channel_id=1, source_target_pairs={{0,2},{1,3},{2,0},{3,1},{4,6},{5,7},{6,4},{7,5},{8,10},{9,11},{10,... | collective-permute-start | bytes 196616 | tf_op jit(solution)/shard_map/ppermute | solution.py:58
  72.2 1.3 %collective-permute-done.25 = bf16[64,128]{1,0:T(8,128)(2,1)S(1)} collective-permute-done((bf16[64,128]{1,0:T(8,128)(2,1)S(1)}, bf16[64,128]{1,0:T(8,128)(2,1)S(1)}, u32[]{:S(2)}, u32[]{:S(2)}) %collective-permute-start.25) | collective-permute-done | bytes 16416 | tf_op jit(solution)/shard_map/ppermute | solution.py:55
  73.5 1.4 %collective-permute-done.21 = f32[128,128]{1,0:T(8,128)S(1)} collective-permute-done((f32[128,128]{1,0:T(8,128)S(1)}, f32[128,128]{1,0:T(8,128)S(1)}, u32[]{:S(2)}, u32[]{:S(2)}) %collective-permute-start.21) | collective-permute-done | bytes 65568 | tf_op jit(solution)/shard_map/ppermute | solution.py:58
  75.0 0.7 add_convert_fusion
  75.8 0.7 add_convert_fusion.1
  76.6 0.8 convolution_convert_fusion
  77.4 1.1 %collective-permute-start.29 = (bf16[256,256]{1,0:T(8,128)(2,1)S(1)}, bf16[256,256]{1,0:T(8,128)(2,1)S(1)}, u32[]{:S(2)}, u32[]{:S(2)}) collective-permute-start(bf16[256,256]{1,0:T(8,128)(2,1)S(1)} %convolution_convert_fusion), channel_id=1, source_target_pairs={{0,8},{4,12},{8,0},{12,4},{16,24},{20,28},{24,16},{28,20},{1,9},{5... | collective-permute-start | bytes 393224 | tf_op jit(solution)/shard_map/ppermute | solution.py:55
  78.5 0.8 fusion.51
  79.3 3.5 %collective-permute-done.29 = bf16[256,256]{1,0:T(8,128)(2,1)S(1)} collective-permute-done((bf16[256,256]{1,0:T(8,128)(2,1)S(1)}, bf16[256,256]{1,0:T(8,128)(2,1)S(1)}, u32[]{:S(2)}, u32[]{:S(2)}) %collective-permute-start.29) | collective-permute-done | bytes 131104 | tf_op jit(solution)/shard_map/ppermute | solution.py:55
  82.8 0.8 pad_maximum_fusion.3
  (114 shorter events, 7.0 us)
Async XLA Ops:
  0.0 10.5 %copy-start = (bf16[256,896]{1,0:T(8,128)(2,1)S(1)}, bf16[256,896]{1,0:T(8,128)(2,1)}, u32[]{:S(2)}) copy-start(bf16[256,896]{1,0:T(8,128)(2,1)} %param.12) | copy-start | bytes 1376260
  0.0 15.1 %copy-start.3 = (bf16[256,896]{1,0:T(8,128)(2,1)S(1)}, bf16[256,896]{1,0:T(8,128)(2,1)}, u32[]{:S(2)}) copy-start(bf16[256,896]{1,0:T(8,128)(2,1)} %param.11) | copy-start | bytes 1376260
  0.0 13.8 %copy-start.1 = (bf16[64,4096]{1,0:T(8,128)(2,1)S(1)}, bf16[64,4096]{1,0:T(8,128)(2,1)}, u32[]{:S(2)}) copy-start(bf16[64,4096]{1,0:T(8,128)(2,1)} %param.17) | copy-start | bytes 1572868
  0.0 24.8 %collective-permute-start.3 = (bf16[256,896]{1,0:T(8,128)(2,1)}, bf16[256,896]{1,0:T(8,128)(2,1)S(1)}, u32[]{:S(2)}, u32[]{:S(2)}) collective-permute-start(bf16[256,896]{1,0:T(8,128)(2,1)} %param.11), channel_id=1, source_target_pairs={{0,16},{4,20},{8,24},{12,28},{16,0},{20,4},{24,8},{28,12},{1,17},{... | collective-permute-start | bytes 1376264 | tf_op jit(solution)/shard_map/ppermute | solution.py:55
  4.8 12.9 %collective-permute-start.2 = (bf16[256,896]{1,0:T(8,128)(2,1)}, bf16[256,896]{1,0:T(8,128)(2,1)S(1)}, u32[]{:S(2)}, u32[]{:S(2)}) collective-permute-start(bf16[256,896]{1,0:T(8,128)(2,1)} %param.11), channel_id=1, source_target_pairs={{0,4},{4,0},{8,12},{12,8},{16,20},{20,16},{24,28},{28,24},{1,5},{5... | collective-permute-start | bytes 1376264 | tf_op jit(solution)/shard_map/ppermute | solution.py:55
  6.3 20.6 %collective-permute-start.4 = (bf16[256,896]{1,0:T(8,128)(2,1)}, bf16[256,896]{1,0:T(8,128)(2,1)S(1)}, u32[]{:S(2)}, u32[]{:S(2)}) collective-permute-start(bf16[256,896]{1,0:T(8,128)(2,1)} %param.9), channel_id=1, source_target_pairs={{0,8},{4,12},{8,0},{12,4},{16,24},{20,28},{24,16},{28,20},{1,9},{5... | collective-permute-start | bytes 1376264 | tf_op jit(solution)/shard_map/ppermute | solution.py:55
  10.5 5.4 %copy-start.7 = (s32[256]{0:T(256)S(1)}, s32[256]{0:T(256)}, u32[]{:S(2)}) copy-start(s32[256]{0:T(256)} %param.14) | copy-start | bytes 3076
  13.8 2.3 %collective-permute-start = (f32[256,256]{1,0:T(8,128)}, f32[256,256]{1,0:T(8,128)S(1)}, u32[]{:S(2)}, u32[]{:S(2)}) collective-permute-start(f32[256,256]{1,0:T(8,128)} %pad_maximum_fusion.8), channel_id=1, source_target_pairs={{0,1},{1,0},{2,3},{3,2},{4,5},{5,4},{6,7},{7,6},{8,9},{9,8},{10,11... | collective-permute-start | bytes 786440 | tf_op jit(solution)/shard_map/ppermute | solution.py:58
  14.6 13.0 %collective-permute-start.7 = (bf16[32,4096]{1,0:T(8,128)(2,1)}, bf16[32,4096]{1,0:T(8,128)(2,1)}, u32[]{:S(2)}, u32[]{:S(2)}) collective-permute-start(bf16[32,4096]{1,0:T(8,128)(2,1)} %get-tuple-element.46), channel_id=1, source_target_pairs={{0,4},{4,0},{8,12},{12,8},{16,20},{20,16},{24,28},{28,24},{1,5},{5... | collective-permute-start | bytes 786440 | tf_op jit(solution)/shard_map/ppermute | solution.py:55
  16.0 10.9 %copy-start.6 = (bf16[128,896]{1,0:T(8,128)(2,1)S(1)}, bf16[128,896]{1,0:T(8,128)(2,1)}, u32[]{:S(2)}) copy-start(bf16[128,896]{1,0:T(8,128)(2,1)} %get-tuple-element.48) | copy-start | bytes 688132
  16.1 11.4 %collective-permute-start.1 = (f32[256,256]{1,0:T(8,128)S(1)}, f32[256,256]{1,0:T(8,128)S(1)}, u32[]{:S(2)}, u32[]{:S(2)}) collective-permute-start(f32[256,256]{1,0:T(8,128)S(1)} %fusion.38), channel_id=1, source_target_pairs={{0,2},{1,3},{2,0},{3,1},{4,6},{5,7},{6,4},{7,5},{8,10},{9,11},{10,... | collective-permute-start | bytes 786440 | tf_op jit(solution)/shard_map/ppermute | solution.py:58
  17.7 9.7 %copy-start.2 = (bf16[256,896]{1,0:T(8,128)(2,1)S(1)}, bf16[256,896]{1,0:T(8,128)(2,1)}, u32[]{:S(2)}) copy-start(bf16[256,896]{1,0:T(8,128)(2,1)} %param.9) | copy-start | bytes 1376260
  27.3 4.3 %collective-permute-start.5 = (f32[384,256]{0,1:T(8,128)S(1)}, f32[384,256]{0,1:T(8,128)S(1)}, u32[]{:S(2)}, u32[]{:S(2)}) collective-permute-start(f32[384,256]{0,1:T(8,128)S(1)} %fusion.5), channel_id=1, source_target_pairs={{0,1},{1,0},{2,3},{3,2},{4,5},{5,4},{6,7},{7,6},{8,9},{9,8},{10,11... | collective-permute-start | bytes 1179656 | tf_op jit(solution)/shard_map/ppermute | solution.py:58
  27.6 4.1 %copy-start.5 = (bf16[128,896]{1,0:T(8,128)(2,1)S(1)}, bf16[128,896]{1,0:T(8,128)(2,1)}, u32[]{:S(2)}) copy-start(bf16[128,896]{1,0:T(8,128)(2,1)} %get-tuple-element.47) | copy-start | bytes 688132
  27.7 4.0 %collective-permute-start.8 = (f32[64,128]{1,0:T(8,128)S(1)}, f32[64,128]{1,0:T(8,128)S(1)}, u32[]{:S(2)}, u32[]{:S(2)}) collective-permute-start(f32[64,128]{1,0:T(8,128)S(1)} %constant_dynamic-slice_fusion.4), channel_id=1, source_target_pairs={{0,4},{4,0},{8,12},{12,8},{16,20},{20,16},{24,28},{28,24},{1,5},{5... | collective-permute-start | bytes 98312 | tf_op jit(solution)/shard_map/ppermute | solution.py:55
  28.7 7.0 %collective-permute-start.10 = (f32[384,256]{0,1:T(8,128)S(1)}, f32[384,256]{0,1:T(8,128)S(1)}, u32[]{:S(2)}, u32[]{:S(2)}) collective-permute-start(f32[384,256]{0,1:T(8,128)S(1)} %fusion.4), channel_id=1, source_target_pairs={{0,1},{1,0},{2,3},{3,2},{4,5},{5,4},{6,7},{7,6},{8,9},{9,8},{10,11... | collective-permute-start | bytes 1179656 | tf_op jit(solution)/shard_map/ppermute | solution.py:58
  29.0 12.7 %collective-permute-start.13 = (bf16[256,896]{1,0:T(8,128)(2,1)S(1)}, bf16[256,896]{1,0:T(8,128)(2,1)S(1)}, u32[]{:S(2)}, u32[]{:S(2)}) collective-permute-start(bf16[256,896]{1,0:T(8,128)(2,1)S(1)} %collective-permute-done.3), channel_id=1, source_target_pairs={{0,4},{4,0},{8,12},{12,8},{16,20},{20,16},{24,28},{28,24},{1,5},{5... | collective-permute-start | bytes 1376264 | tf_op jit(solution)/shard_map/ppermute | solution.py:55
  32.1 6.0 %collective-permute-start.9 = (f32[64,256]{1,0:T(8,128)S(1)}, f32[64,256]{1,0:T(8,128)S(1)}, u32[]{:S(2)}, u32[]{:S(2)}) collective-permute-start(f32[64,256]{1,0:T(8,128)S(1)} %pad_maximum_fusion.12), channel_id=1, source_target_pairs={{0,16},{4,20},{8,24},{12,28},{16,0},{20,4},{24,8},{28,12},{1,17},{... | collective-permute-start | bytes 196616 | tf_op jit(solution)/shard_map/ppermute | solution.py:55
  32.9 11.6 %collective-permute-start.6 = (f32[200,256]{1,0:T(8,128)S(1)}, f32[200,256]{1,0:T(8,128)S(1)}, u32[]{:S(2)}, u32[]{:S(2)}) collective-permute-start(f32[200,256]{1,0:T(8,128)S(1)} %pad_maximum_fusion.9), channel_id=1, source_target_pairs={{0,8},{4,12},{8,0},{12,4},{16,24},{20,28},{24,16},{28,20},{1,9},{5... | collective-permute-start | bytes 614408 | tf_op jit(solution)/shard_map/ppermute | solution.py:55
  35.3 27.7 %collective-permute-start.27 = (bf16[64,4096]{1,0:T(8,128)(2,1)S(1)}, bf16[64,4096]{1,0:T(8,128)(2,1)S(1)}, u32[]{:S(2)}, u32[]{:S(2)}) collective-permute-start(bf16[64,4096]{1,0:T(8,128)(2,1)S(1)} %copy-done.1), channel_id=1, source_target_pairs={{0,16},{4,20},{8,24},{12,28},{16,0},{20,4},{24,8},{28,12},{1,17},{... | collective-permute-start | bytes 1572872 | tf_op jit(solution)/shard_map/ppermute | solution.py:55
  35.7 7.8 %copy-start.4 = (bf16[32,4096]{1,0:T(8,128)(2,1)S(1)}, bf16[32,4096]{1,0:T(8,128)(2,1)}, u32[]{:S(2)}) copy-start(bf16[32,4096]{1,0:T(8,128)(2,1)} %get-tuple-element.30) | copy-start | bytes 786436
  35.7 7.8 %collective-permute-start.12 = (f32[384,128]{0,1:T(8,128)S(1)}, f32[384,128]{0,1:T(8,128)S(1)}, u32[]{:S(2)}, u32[]{:S(2)}) collective-permute-start(f32[384,128]{0,1:T(8,128)S(1)} %constant_dynamic-slice_fusion.2), channel_id=1, source_target_pairs={{0,2},{1,3},{2,0},{3,1},{4,6},{5,7},{6,4},{7,5},{8,10},{9,11},{10,... | collective-permute-start | bytes 589832 | tf_op jit(solution)/shard_map/ppermute | solution.py:58
  38.1 8.5 %collective-permute-start.11 = (f32[384,128]{0,1:T(8,128)S(1)}, f32[384,128]{0,1:T(8,128)S(1)}, u32[]{:S(2)}, u32[]{:S(2)}) collective-permute-start(f32[384,128]{0,1:T(8,128)S(1)} %constant_dynamic-slice_fusion.3), channel_id=1, source_target_pairs={{0,2},{1,3},{2,0},{3,1},{4,6},{5,7},{6,4},{7,5},{8,10},{9,11},{10,... | collective-permute-start | bytes 589832 | tf_op jit(solution)/shard_map/ppermute | solution.py:58
  42.1 2.4 %collective-permute-start.14 = (f32[128,512]{0,1:T(8,128)S(1)}, f32[128,512]{0,1:T(8,128)S(1)}, u32[]{:S(2)}, u32[]{:S(2)}) collective-permute-start(f32[128,512]{0,1:T(8,128)S(1)} %fusion.6), channel_id=1, source_target_pairs={{0,1},{1,0},{2,3},{3,2},{4,5},{5,4},{6,7},{7,6},{8,9},{9,8},{10,11... | collective-permute-start | bytes 786440 | tf_op jit(solution)/shard_map/ppermute | solution.py:58
  43.5 8.2 %collective-permute-start.17 = (bf16[32,4096]{1,0:T(8,128)(2,1)S(1)}, bf16[32,4096]{1,0:T(8,128)(2,1)S(1)}, u32[]{:S(2)}, u32[]{:S(2)}) collective-permute-start(bf16[32,4096]{1,0:T(8,128)(2,1)S(1)} %copy-done.4), channel_id=1, source_target_pairs={{0,4},{4,0},{8,12},{12,8},{16,20},{20,16},{24,28},{28,24},{1,5},{5... | collective-permute-start | bytes 786440 | tf_op jit(solution)/shard_map/ppermute | solution.py:55
  45.0 5.0 %collective-permute-start.15 = (f32[128,256]{0,1:T(8,128)S(1)}, f32[128,256]{0,1:T(8,128)S(1)}, u32[]{:S(2)}, u32[]{:S(2)}) collective-permute-start(f32[128,256]{0,1:T(8,128)S(1)} %constant_dynamic-slice_fusion.1), channel_id=1, source_target_pairs={{0,2},{1,3},{2,0},{3,1},{4,6},{5,7},{6,4},{7,5},{8,10},{9,11},{10,... | collective-permute-start | bytes 393224 | tf_op jit(solution)/shard_map/ppermute | solution.py:58
  50.4 1.2 %collective-permute-start.16 = (f32[2,256]{1,0:T(2,128)S(1)}, f32[2,256]{1,0:T(2,128)S(1)}, u32[]{:S(2)}, u32[]{:S(2)}) collective-permute-start(f32[2,256]{1,0:T(2,128)S(1)} %pad_maximum_fusion.17), channel_id=1, source_target_pairs={{0,1},{1,0},{2,3},{3,2},{4,5},{5,4},{6,7},{7,6},{8,9},{9,8},{10,11... | collective-permute-start | bytes 6152 | tf_op jit(solution)/shard_map/ppermute | solution.py:58
  51.7 3.8 %collective-permute-start.18 = (f32[2,256]{1,0:T(2,128)S(1)}, f32[2,256]{1,0:T(2,128)S(1)}, u32[]{:S(2)}, u32[]{:S(2)}) collective-permute-start(f32[2,256]{1,0:T(2,128)S(1)} %fusion.28), channel_id=1, source_target_pairs={{0,8},{4,12},{8,0},{12,4},{16,24},{20,28},{24,16},{28,20},{1,9},{5... | collective-permute-start | bytes 6152 | tf_op jit(solution)/shard_map/ppermute | solution.py:55
  55.9 1.6 %collective-permute-start.19 = (f32[64,256]{1,0:T(8,128)S(1)}, f32[64,256]{1,0:T(8,128)S(1)}, u32[]{:S(2)}, u32[]{:S(2)}) collective-permute-start(f32[64,256]{1,0:T(8,128)S(1)} %fusion.20), channel_id=1, source_target_pairs={{0,1},{1,0},{2,3},{3,2},{4,5},{5,4},{6,7},{7,6},{8,9},{9,8},{10,11... | collective-permute-start | bytes 196616 | tf_op jit(solution)/shard_map/ppermute | solution.py:58
  56.2 4.6 %collective-permute-start.22 = (f32[64,256]{1,0:T(8,128)S(1)}, f32[64,256]{1,0:T(8,128)S(1)}, u32[]{:S(2)}, u32[]{:S(2)}) collective-permute-start(f32[64,256]{1,0:T(8,128)S(1)} %slice.208), channel_id=1, source_target_pairs={{0,4},{4,0},{8,12},{12,8},{16,20},{20,16},{24,28},{28,24},{1,5},{5... | collective-permute-start | bytes 196616 | tf_op jit(solution)/shard_map/ppermute | solution.py:55
  57.6 9.6 %collective-permute-start.20 = (f32[64,256]{1,0:T(8,128)S(1)}, f32[64,256]{1,0:T(8,128)S(1)}, u32[]{:S(2)}, u32[]{:S(2)}) collective-permute-start(f32[64,256]{1,0:T(8,128)S(1)} %pad_maximum_fusion.13), channel_id=1, source_target_pairs={{0,8},{4,12},{8,0},{12,4},{16,24},{20,28},{24,16},{28,20},{1,9},{5... | collective-permute-start | bytes 196616 | tf_op jit(solution)/shard_map/ppermute | solution.py:55
  60.8 4.9 %collective-permute-start.23 = (f32[64,128]{1,0:T(8,128)S(1)}, f32[64,128]{1,0:T(8,128)S(1)}, u32[]{:S(2)}, u32[]{:S(2)}) collective-permute-start(f32[64,128]{1,0:T(8,128)S(1)} %slice.210), channel_id=1, source_target_pairs={{0,16},{4,20},{8,24},{12,28},{16,0},{20,4},{24,8},{28,12},{1,17},{... | collective-permute-start | bytes 98312 | tf_op jit(solution)/shard_map/ppermute | solution.py:55
  63.0 13.6 %collective-permute-start.28 = (bf16[64,4096]{1,0:T(8,128)(2,1)S(1)}, bf16[64,4096]{1,0:T(8,128)(2,1)S(1)}, u32[]{:S(2)}, u32[]{:S(2)}) collective-permute-start(bf16[64,4096]{1,0:T(8,128)(2,1)S(1)} %collective-permute-done.27), channel_id=1, source_target_pairs={{0,4},{4,0},{8,12},{12,8},{16,20},{20,16},{24,28},{28,24},{1,5},{5... | collective-permute-start | bytes 1572872 | tf_op jit(solution)/shard_map/ppermute | solution.py:55
  65.7 3.9 %collective-permute-start.24 = (f32[64,128]{1,0:T(8,128)S(1)}, f32[64,128]{1,0:T(8,128)S(1)}, u32[]{:S(2)}, u32[]{:S(2)}) collective-permute-start(f32[64,128]{1,0:T(8,128)S(1)} %slice_add_fusion.3), channel_id=1, source_target_pairs={{0,2},{1,3},{2,0},{3,1},{4,6},{5,7},{6,4},{7,5},{8,10},{9,11},{10,... | collective-permute-start | bytes 98312 | tf_op jit(solution)/shard_map/ppermute | solution.py:58
  69.6 3.8 %collective-permute-start.25 = (bf16[64,128]{1,0:T(8,128)(2,1)S(1)}, bf16[64,128]{1,0:T(8,128)(2,1)S(1)}, u32[]{:S(2)}, u32[]{:S(2)}) collective-permute-start(bf16[64,128]{1,0:T(8,128)(2,1)S(1)} %get-tuple-element.35), channel_id=1, source_target_pairs={{0,8},{4,12},{8,0},{12,4},{16,24},{20,28},{24,16},{28,20},{1,9},{5... | collective-permute-start | bytes 49160 | tf_op jit(solution)/shard_map/ppermute | solution.py:55
  70.7 4.3 %collective-permute-start.21 = (f32[128,128]{1,0:T(8,128)S(1)}, f32[128,128]{1,0:T(8,128)S(1)}, u32[]{:S(2)}, u32[]{:S(2)}) collective-permute-start(f32[128,128]{1,0:T(8,128)S(1)} %pad_maximum_fusion.14), channel_id=1, source_target_pairs={{0,2},{1,3},{2,0},{3,1},{4,6},{5,7},{6,4},{7,5},{8,10},{9,11},{10,... | collective-permute-start | bytes 196616 | tf_op jit(solution)/shard_map/ppermute | solution.py:58
  73.5 1.5 %collective-permute-start.26 = (f32[128,128]{1,0:T(8,128)S(1)}, f32[128,128]{1,0:T(8,128)S(1)}, u32[]{:S(2)}, u32[]{:S(2)}) collective-permute-start(f32[128,128]{1,0:T(8,128)S(1)} %pad_maximum_fusion.15), channel_id=1, source_target_pairs={{0,1},{1,0},{2,3},{3,2},{4,5},{5,4},{6,7},{7,6},{8,9},{9,8},{10,11... | collective-permute-start | bytes 196616 | tf_op jit(solution)/shard_map/ppermute | solution.py:58
  77.4 5.4 %collective-permute-start.29 = (bf16[256,256]{1,0:T(8,128)(2,1)S(1)}, bf16[256,256]{1,0:T(8,128)(2,1)S(1)}, u32[]{:S(2)}, u32[]{:S(2)}) collective-permute-start(bf16[256,256]{1,0:T(8,128)(2,1)S(1)} %convolution_convert_fusion), channel_id=1, source_target_pairs={{0,8},{4,12},{8,0},{12,4},{16,24},{20,28},{24,16},{28,20},{1,9},{5... | collective-permute-start | bytes 393224 | tf_op jit(solution)/shard_map/ppermute | solution.py:55
